TPU v7x, 32 devices: a whole 2x2x4 slice. The times are simulated.
32 devices in a mesh: fsdp: 4 (over z), ctx: 4 (over y, x), tp: 2 (over core).
Axes of the slice: x: 2, y: 2, z: 4, core: 2. Of those that a mesh axis runs over, the one named last changes fastest.
Arguments:
- tokens: bfloat16 [8192, 2048], P(('fsdp', 'ctx')), may hold values from -6 to 6
- cotangent: bfloat16 [8192, 2048], P(('fsdp', 'ctx')), may hold values from -6 to 6
- lengths: int32 [4], P('fsdp'), may hold values from 1024 to 2048, as said below
- deal: int32 [4, 16], P('fsdp'), may hold values from 0 to 15, as said below
- attn_gain: bfloat16 [2048], P(('fsdp', 'ctx')), may hold values from 0.25 to 1.75
- w_query: bfloat16 [2048, 2048], P(('fsdp', 'ctx'), 'tp'), may hold values from -0.125 to 0.125
- w_key: bfloat16 [2048, 1024], P(('fsdp', 'ctx'), 'tp'), may hold values from -0.125 to 0.125
- w_value: bfloat16 [2048, 1024], P(('fsdp', 'ctx'), 'tp'), may hold values from -0.125 to 0.125
- w_out: bfloat16 [2048, 2048], P('tp', ('fsdp', 'ctx')), may hold values from -2 to 2
- query_gain: bfloat16 [128], replicated, may hold values from 0.25 to 1.75
- key_gain: bfloat16 [128], replicated, may hold values from 0.25 to 1.75
- ffn_gain: bfloat16 [2048], P(('fsdp', 'ctx')), may hold values from 0.25 to 1.75
- w_gate: bfloat16 [2048, 6144], P(('fsdp', 'ctx'), 'tp'), may hold values from -0.125 to 0.125
- w_up: bfloat16 [2048, 6144], P(('fsdp', 'ctx'), 'tp'), may hold values from -0.125 to 0.125
- w_down: bfloat16 [6144, 2048], P('tp', ('fsdp', 'ctx')), may hold values from -0.078125 to 0.078125
Outputs:
- output: bfloat16 [8192, 2048], P(('fsdp', 'ctx'))
- grad_tokens: float32 [8192, 2048], P(('fsdp', 'ctx'))
- grad_attn_gain: float32 [2048], P(('fsdp', 'ctx'))
- grad_w_query: float32 [2048, 2048], P(('fsdp', 'ctx'), 'tp')
- grad_w_key: float32 [2048, 1024], P(('fsdp', 'ctx'), 'tp')
- grad_w_value: float32 [2048, 1024], P(('fsdp', 'ctx'), 'tp')
- grad_w_out: float32 [2048, 2048], P('tp', ('fsdp', 'ctx'))
- grad_query_gain: float32 [128], replicated
- grad_key_gain: float32 [128], replicated
- grad_ffn_gain: float32 [2048], P(('fsdp', 'ctx'))
- grad_w_gate: float32 [2048, 6144], P(('fsdp', 'ctx'), 'tp')
- grad_w_up: float32 [2048, 6144], P(('fsdp', 'ctx'), 'tp')
- grad_w_down: float32 [6144, 2048], P('tp', ('fsdp', 'ctx'))
Inputs may be any that keep to these rules, and one draw needn't show every extreme that they name: `lengths`: length of each sequence, counted in slots; in every draw one sequence has 2048 and another half of 2048. `deal`: each row is a permutation of the 16 blocks; the first slot block of each index of ctx (every 4-th, from 0) holds one of the blocks 0 to 3.
All inputs are finite; a program needn't handle non-finite values.
Results may differ from a plain program's by a relative error of at most 0.017.
Values may be sent and summed in bfloat16 or wider, within the bound.
No kernel may reach another device: no remote copies, remote signals or barrier semaphores. Data moves between devices by JAX's collectives and lax.ppermute only.
A program may use at most 256 MiB of HBM per device.

v0:
```python
import math

import jax
import jax.numpy as jnp
from jax import lax
from jax.sharding import PartitionSpec as P

BLK = 128


EPS = 1e-06
THETA = 1000000.0
SPAN = 512


def product(left, right):
    return jnp.dot(left, right, preferred_element_type=jnp.float32)


def left_transposed(left, right):
    return lax.dot_general(
        left, right, (((0,), (0,)), ((), ())), preferred_element_type=jnp.float32
    )


def right_transposed(left, right):
    return lax.dot_general(
        left, right, (((1,), (1,)), ((), ())), preferred_element_type=jnp.float32
    )


def rms_norm(values, gain):
    return values * lax.rsqrt(jnp.mean(values * values, axis=-1, keepdims=True) + EPS) * gain


def rotary_tables(positions, head_size):
    frequency = THETA ** (-(jnp.arange(head_size // 2, dtype=jnp.float32) * 2.0 / head_size))
    angles = positions.astype(jnp.float32)[:, None] * frequency[None, :]
    angles = jnp.concatenate([angles, angles], axis=-1)
    return (jnp.cos(angles), jnp.sin(angles))


def rotate_half(values, cosine, sine):
    half_size = values.shape[-1] // 2
    turned = jnp.concatenate([-values[..., half_size:], values[..., :half_size]], axis=-1)
    return values * cosine + turned * sine


def head_path(projected, gain, cosine, sine, head_count):
    row_count = projected.shape[0]
    shaped = projected.reshape(row_count, head_count, -1)
    normed = rms_norm(shaped, gain)
    return rotate_half(normed, cosine[:, None, :], sine[:, None, :]).reshape(row_count, -1)


def score_weights(queries, key_block, query_pos, key_pos, key_valid, scale):
    raw_scores = jnp.einsum(
        "tkgd,skd->kgts", queries, key_block, preferred_element_type=jnp.float32
    )
    allowed = key_valid[None, :] & (key_pos[None, :] <= query_pos[:, None])
    return jnp.where(allowed[None, None], jnp.exp(raw_scores * scale), 0.0)


def on_device(
    tokens,
    cotangent,
    lengths,
    deal,
    attn_gain,
    w_query,
    w_key,
    w_value,
    w_out,
    query_gain,
    key_gain,
    ffn_gain,
    w_gate,
    w_up,
    w_down,
):
    local_rows = tokens.shape[0]
    head_size = query_gain.shape[0]
    scale = head_size ** (-0.5)
    slot_pos = (deal[0][:, None] * BLK + jnp.arange(BLK, dtype=jnp.int32)[None, :]).reshape(-1)
    slot_valid = slot_pos < lengths[0]
    slot_count = slot_pos.shape[0]
    offset = lax.axis_index("ctx") * local_rows
    query_pos = lax.dynamic_slice_in_dim(slot_pos, offset, local_rows)
    query_valid = lax.dynamic_slice_in_dim(slot_valid, offset, local_rows)
    cosine, sine = rotary_tables(query_pos, head_size)
    query_scale = query_gain.astype(jnp.float32)
    key_scale = key_gain.astype(jnp.float32)
    attn_gain_full, query_weight, key_weight, value_weight, out_weight = (
        lax.all_gather(attn_gain, ("fsdp", "ctx"), axis=0, tiled=True),
        lax.all_gather(w_query, ("fsdp", "ctx"), axis=0, tiled=True),
        lax.all_gather(w_key, ("fsdp", "ctx"), axis=0, tiled=True),
        lax.all_gather(w_value, ("fsdp", "ctx"), axis=0, tiled=True),
        lax.all_gather(w_out, ("fsdp", "ctx"), axis=1, tiled=True),
    )
    attn_scale = attn_gain_full.astype(jnp.float32)
    query_heads = query_weight.shape[1] // head_size
    key_heads = key_weight.shape[1] // head_size
    group_size = query_heads // key_heads
    inputs = tokens.astype(jnp.float32)
    normed = rms_norm(inputs, attn_scale).astype(jnp.bfloat16)
    query_proj = product(normed, query_weight)
    key_proj = product(normed, key_weight)
    values_local = product(normed, value_weight).astype(jnp.bfloat16)
    queries = head_path(query_proj, query_scale, cosine, sine, query_heads).astype(jnp.bfloat16)
    keys_local = head_path(key_proj, key_scale, cosine, sine, key_heads).astype(jnp.bfloat16)
    query_blocks = queries.reshape(local_rows, key_heads, group_size, head_size)
    start_accum = jnp.zeros((local_rows, key_heads, group_size, head_size), jnp.float32)
    start_totals = jnp.zeros((key_heads, group_size, local_rows), jnp.float32)
    key_piece = lax.all_gather(keys_local, "ctx", axis=0, tiled=True)
    value_piece = lax.all_gather(values_local, "ctx", axis=0, tiled=True)
    piece_rows = key_piece.shape[0]
    stride = math.gcd(piece_rows, SPAN)
    part_count = piece_rows // stride
    key_pos = slot_pos.reshape(part_count, stride)
    key_valid = slot_valid.reshape(part_count, stride)
    key_steps = key_piece.reshape(part_count, stride, key_heads, head_size)
    value_steps = value_piece.reshape(part_count, stride, key_heads, head_size)

    def one_block(inner_carry, operands):
        accum, totals = inner_carry
        key_block, value_block, block_pos, block_valid = operands
        exp_scores = score_weights(
            query_blocks, key_block, query_pos, block_pos, block_valid, scale
        )
        totals = totals + jnp.sum(exp_scores, axis=-1)
        accum = accum + jnp.einsum(
            "kgts,skd->tkgd",
            exp_scores.astype(jnp.bfloat16),
            value_block,
            preferred_element_type=jnp.float32,
        )
        return ((accum, totals), None)

    outcome, unused = lax.scan(
        one_block, (start_accum, start_totals), (key_steps, value_steps, key_pos, key_valid)
    )
    accum, totals = outcome
    row_totals = jnp.transpose(totals, (2, 0, 1))
    mixed = accum / row_totals[..., None]
    mixed_low = mixed.reshape(local_rows, query_heads * head_size).astype(jnp.bfloat16)
    attn_branch = lax.psum(product(mixed_low, out_weight), "tp")
    hidden = inputs + attn_branch
    feed_gain_full, gate_weight, up_weight, down_weight = (
        lax.all_gather(ffn_gain, ("fsdp", "ctx"), axis=0, tiled=True),
        lax.all_gather(w_gate, ("fsdp", "ctx"), axis=0, tiled=True),
        lax.all_gather(w_up, ("fsdp", "ctx"), axis=0, tiled=True),
        lax.all_gather(w_down, ("fsdp", "ctx"), axis=1, tiled=True),
    )
    feed_scale = feed_gain_full.astype(jnp.float32)
    normed_two = rms_norm(hidden, feed_scale).astype(jnp.bfloat16)
    gate_proj = product(normed_two, gate_weight)
    up_proj = product(normed_two, up_weight)
    inner_low = (jax.nn.silu(gate_proj) * up_proj).astype(jnp.bfloat16)
    feed_branch = lax.psum(product(inner_low, down_weight).astype(jnp.bfloat16), "tp").astype(
        jnp.float32
    )
    output = (hidden + feed_branch).astype(jnp.bfloat16)
    grad_seed = cotangent.astype(jnp.float32) * query_valid[:, None].astype(jnp.float32)
    seed_low = grad_seed.astype(jnp.bfloat16)
    grad_down = left_transposed(inner_low, seed_low)
    grad_inner = right_transposed(seed_low, down_weight)
    unused, swiglu_back = jax.vjp(
        lambda gate_in, up_in: jax.nn.silu(gate_in) * up_in, gate_proj, up_proj
    )
    grad_gate_proj, grad_up_proj = swiglu_back(grad_inner)
    gate_low = grad_gate_proj.astype(jnp.bfloat16)
    up_low = grad_up_proj.astype(jnp.bfloat16)
    grad_gate = left_transposed(normed_two, gate_low)
    grad_up = left_transposed(normed_two, up_low)
    grad_normed_two = lax.psum(
        right_transposed(gate_low, gate_weight) + right_transposed(up_low, up_weight), "tp"
    )
    unused, norm_back_two = jax.vjp(rms_norm, hidden, feed_scale)
    grad_hidden_norm, grad_feed_gain = norm_back_two(grad_normed_two)
    grad_hidden = grad_seed + grad_hidden_norm
    feed_grads = (
        lax.psum_scatter(grad_feed_gain, ("fsdp", "ctx"), scatter_dimension=0, tiled=True),
        lax.psum_scatter(grad_gate, ("fsdp", "ctx"), scatter_dimension=0, tiled=True),
        lax.psum_scatter(grad_up, ("fsdp", "ctx"), scatter_dimension=0, tiled=True),
        lax.psum_scatter(grad_down, ("fsdp", "ctx"), scatter_dimension=1, tiled=True),
    )
    grad_attn_low = grad_hidden.astype(jnp.bfloat16)
    grad_out = left_transposed(mixed_low, grad_attn_low)
    grad_mixed = right_transposed(grad_attn_low, out_weight).reshape(
        local_rows, key_heads, group_size, head_size
    )
    row_shift = jnp.transpose(jnp.sum(grad_mixed * mixed, axis=-1) / row_totals, (1, 2, 0))
    grad_accum = (grad_mixed / row_totals[..., None]).astype(jnp.bfloat16)
    keys_all, values_all = (
        lax.all_gather(keys_local, "ctx", axis=0, tiled=True),
        lax.all_gather(values_local, "ctx", axis=0, tiled=True),
    )
    stride = math.gcd(slot_count, SPAN)
    part_count = slot_count // stride

    def back_block(grad_queries, operands):
        key_block, value_block, block_pos, block_valid = operands
        exp_scores = score_weights(
            query_blocks, key_block, query_pos, block_pos, block_valid, scale
        )
        grad_probs = jnp.einsum(
            "tkgd,skd->kgts", grad_accum, value_block, preferred_element_type=jnp.float32
        )
        grad_scores = (exp_scores * (grad_probs - row_shift[..., None])).astype(jnp.bfloat16)
        grad_queries = grad_queries + scale * jnp.einsum(
            "kgts,skd->tkgd", grad_scores, key_block, preferred_element_type=jnp.float32
        )
        grad_keys = scale * jnp.einsum(
            "kgts,tkgd->skd", grad_scores, query_blocks, preferred_element_type=jnp.float32
        )
        grad_values = jnp.einsum(
            "kgts,tkgd->skd",
            exp_scores.astype(jnp.bfloat16),
            grad_accum,
            preferred_element_type=jnp.float32,
        )
        return (grad_queries, (grad_keys, grad_values))

    grad_queries, (key_terms, value_terms) = lax.scan(
        back_block,
        jnp.zeros((local_rows, key_heads, group_size, head_size), jnp.float32),
        (
            keys_all.reshape(part_count, stride, key_heads, head_size),
            values_all.reshape(part_count, stride, key_heads, head_size),
            slot_pos.reshape(part_count, stride),
            slot_valid.reshape(part_count, stride),
        ),
    )
    key_terms = key_terms.reshape(slot_count, key_heads * head_size)
    value_terms = value_terms.reshape(slot_count, key_heads * head_size)
    grad_keys_local, grad_values_local = (
        lax.psum_scatter(
            key_terms.astype(jnp.bfloat16), "ctx", scatter_dimension=0, tiled=True
        ).astype(jnp.float32),
        lax.psum_scatter(
            value_terms.astype(jnp.bfloat16), "ctx", scatter_dimension=0, tiled=True
        ).astype(jnp.float32),
    )
    grad_values_low = grad_values_local.astype(jnp.bfloat16)
    unused, query_back = jax.vjp(
        lambda proj_in, gain_in: head_path(proj_in, gain_in, cosine, sine, query_heads),
        query_proj,
        query_scale,
    )
    grad_query_proj, grad_query_gain = query_back(
        grad_queries.reshape(local_rows, query_heads * head_size)
    )
    unused, key_back = jax.vjp(
        lambda proj_in, gain_in: head_path(proj_in, gain_in, cosine, sine, key_heads),
        key_proj,
        key_scale,
    )
    grad_key_proj, grad_key_gain = key_back(grad_keys_local)
    query_low = grad_query_proj.astype(jnp.bfloat16)
    key_low = grad_key_proj.astype(jnp.bfloat16)
    grad_query_weight = left_transposed(normed, query_low)
    grad_key_weight = left_transposed(normed, key_low)
    grad_value_weight = left_transposed(normed, grad_values_low)
    grad_normed = lax.psum(
        (
            right_transposed(query_low, query_weight)
            + right_transposed(key_low, key_weight)
            + right_transposed(grad_values_low, value_weight)
        ).astype(jnp.bfloat16),
        "tp",
    ).astype(jnp.float32)
    unused, norm_back_one = jax.vjp(rms_norm, inputs, attn_scale)
    grad_inputs_norm, grad_attn_gain = norm_back_one(grad_normed)
    grad_tokens = grad_hidden + grad_inputs_norm
    attention_grads = (
        lax.psum_scatter(grad_attn_gain, ("fsdp", "ctx"), scatter_dimension=0, tiled=True),
        lax.psum_scatter(grad_query_weight, ("fsdp", "ctx"), scatter_dimension=0, tiled=True),
        lax.psum_scatter(grad_key_weight, ("fsdp", "ctx"), scatter_dimension=0, tiled=True),
        lax.psum_scatter(grad_value_weight, ("fsdp", "ctx"), scatter_dimension=0, tiled=True),
        lax.psum_scatter(grad_out, ("fsdp", "ctx"), scatter_dimension=1, tiled=True),
    )
    gain_grads = lax.psum((grad_query_gain, grad_key_gain), ("fsdp", "ctx", "tp"))
    return (
        output,
        grad_tokens,
        attention_grads[0],
        attention_grads[1],
        attention_grads[2],
        attention_grads[3],
        attention_grads[4],
        gain_grads[0],
        gain_grads[1],
        feed_grads[0],
        feed_grads[1],
        feed_grads[2],
        feed_grads[3],
    )


def solution(mesh):
    return jax.shard_map(
        on_device,
        mesh=mesh,
        in_specs=(
            P(("fsdp", "ctx"), None),
            P(("fsdp", "ctx"), None),
            P("fsdp"),
            P("fsdp", None),
            P(("fsdp", "ctx")),
            P(("fsdp", "ctx"), "tp"),
            P(("fsdp", "ctx"), "tp"),
            P(("fsdp", "ctx"), "tp"),
            P("tp", ("fsdp", "ctx")),
            P(),
            P(),
            P(("fsdp", "ctx")),
            P(("fsdp", "ctx"), "tp"),
            P(("fsdp", "ctx"), "tp"),
            P("tp", ("fsdp", "ctx")),
        ),
        out_specs=(
            P(("fsdp", "ctx"), None),
            P(("fsdp", "ctx"), None),
            P(("fsdp", "ctx")),
            P(("fsdp", "ctx"), "tp"),
            P(("fsdp", "ctx"), "tp"),
            P(("fsdp", "ctx"), "tp"),
            P("tp", ("fsdp", "ctx")),
            P(),
            P(),
            P(("fsdp", "ctx")),
            P(("fsdp", "ctx"), "tp"),
            P(("fsdp", "ctx"), "tp"),
            P("tp", ("fsdp", "ctx")),
        ),
        check_vma=False,
    )
```

profile of v0, /device:TPU:0, one launch (start us, length us, event | category | flops | bytes accessed | tf_op | source)
XLA Modules:
  0.0 2875.6 jit_solution(13433355775586683882)
XLA Ops:
  8.7 42.4 %all-gather = bf16[16,1,128]{2,1,0:T(2,128)(2,1)S(1)} all-gather(bf16[1,1,128]{2,1,0:T(2,128)(2,1)} %bitcast.300), channel_id=1, replica_groups=mesh['fsdp'=4,'ctx'=4,'tp'=2] {'fsdp','ctx'}, dimensions={0}, use_global_device_ids=true | all-gather | bytes 4352 | tf_op jit(solution)/shard_map/all_gather | solution.py:94
  56.8 17.5 all-gather.16.cloned.1.call-done
  79.9 56.6 %all-gather.12.cloned.1.call-done = bf16[2048,512]{1,0:T(8,128)(2,1)} async-done(((bf16[128,512]{1,0:T(8,128)(2,1)}), bf16[2048,512]{1,0:T(8,128)(2,1)}) %all-gather.12.cloned.1.call-update) | async-done | bytes 2097168 | tf_op jit(solution)/shard_map/all_gather | solution.py:97
  141.9 30.8 %all-gather.18.cloned.1.call-done = bf16[2048,512]{0,1:T(8,128)(2,1)} async-done(((bf16[512,512]{0,1:T(8,128)(2,1)}), bf16[2048,512]{0,1:T(8,128)(2,1)}) %all-gather.18.cloned.1.call-update) | async-done | bytes 2097168 | tf_op jit(solution)/shard_map/all_gather | solution.py:114
  172.7 4.5 reshape.339
  177.2 4.5 copy.114
  181.7 28.6 all-gather.14.cloned.1.call-done
  214.3 74.8 %all-gather.20.cloned.1.call-done = bf16[2048,1024]{1,0:T(8,128)(2,1)} async-done(((bf16[128,1024]{1,0:T(8,128)(2,1)}), bf16[2048,1024]{1,0:T(8,128)(2,1)}) %all-gather.20.cloned.1.call-update) | async-done | bytes 4194320 | tf_op jit(solution)/shard_map/all_gather | solution.py:95
  289.1 5.2 fusion.87
  308.3 66.8 %while.28 = (s32[]{:T(128)}, f32[512,4,2,128]{0,3,2,1:T(8,128)S(1)}, f32[4,2,512]{2,1,0:T(2,128)S(1)}, bf16[4,512,4,128]{3,2,1,0:T(4,128)(2,1)}, pred[4,512]{1,0...) while((s32[]{:T(128)}, ...), condition=%wide.region_5.6_spmd.clone, body=%wide.region_3.5_spmd.clone.sunk | while | flops 1087901696 | bytes 26028164 | solution.py:139
  309.1 6.3 fusion.158
  319.6 5.8 bitcast_add_fusion.8
  325.7 6.3 fusion.158
  336.2 5.8 bitcast_add_fusion.8
  342.3 6.3 fusion.158
  352.7 5.8 bitcast_add_fusion.8
  358.9 6.3 fusion.158
  369.3 5.8 bitcast_add_fusion.8
  379.5 6.9 fusion.94
  388.5 37.6 %all-gather.1 = bf16[16,1,128]{2,1,0:T(2,128)(2,1)S(1)} all-gather(bf16[1,1,128]{2,1,0:T(2,128)(2,1)S(1)} %bitcast.301), channel_id=1, replica_groups=mesh['fsdp'=4,'ctx'=4,'tp'=2] {'fsdp','ctx'}, dimensions={0}, use_global_device_ids=true | all-gather | bytes 4352 | tf_op jit(solution)/shard_map/all_gather | solution.py:149
  433.7 135.9 %all-gather.24.cloned.1.call-done = bf16[2048,3072]{1,0:T(8,128)(2,1)} async-done(((bf16[128,3072]{1,0:T(8,128)(2,1)}), bf16[2048,3072]{1,0:T(8,128)(2,1)}) %all-gather.24.cloned.1.call-update) | async-done | bytes 12582928 | tf_op jit(solution)/shard_map/all_gather | solution.py:150
  569.6 12.2 fusion.95
  581.8 141.2 %all-gather.26.cloned.1.call-done = bf16[2048,3072]{1,0:T(8,128)(2,1)} async-done(((bf16[128,3072]{1,0:T(8,128)(2,1)}), bf16[2048,3072]{1,0:T(8,128)(2,1)}) %all-gather.26.cloned.1.call-update) | async-done | bytes 12582928 | tf_op jit(solution)/shard_map/all_gather | solution.py:151
  723.0 11.9 fusion.96
  734.9 185.2 %all-gather.28.cloned.1.call-done = bf16[3072,2048]{1,0:T(8,128)(2,1)} async-done(((bf16[3072,128]{1,0:T(8,128)(2,1)}), bf16[3072,2048]{1,0:T(8,128)(2,1)}) %all-gather.28.cloned.1.call-update) | async-done | bytes 12582928 | tf_op jit(solution)/shard_map/all_gather | solution.py:152
  920.1 17.5 multiply_convert_fusion
  937.6 12.2 fusion.97
  949.8 12.0 convolution_add_fusion
  961.8 26.7 all-reduce.15.cloned.1.call-done
  988.5 5.2 multiply_reduce_fusion
  1004.1 78.3 %while.29 = (s32[]{:T(128)}, f32[512,4,2,128]{0,3,2,1:T(8,128)}, bf16[4,512,4,128]{3,1,2,0:T(8,128)(2,1)}, bf16[4,512,4,128]{3,1,2,0:T(8,128)(2,1)}, bf16[4,512,...) while((s32[]{:T(128)}, f32[512,4,2,128]{0,3,2,1:T(8,128)}, ...), condition=%wide.region_13.14_spmd.clone, body=%wide.region_12.13_spmd.clone.sunk | while | flops 2703491072 | bytes 160722784 | solution.py:224
  1087.4 11.7 convolution_convert_fusion
  1130.3 32.1 %reduce-scatter.12.cloned.1.call-done = bf16[512,512]{1,0:T(8,128)(2,1)} async-done(((bf16[2048,512]{1,0:T(8,128)(2,1)}), bf16[512,512]{1,0:T(8,128)(2,1)}) %reduce-scatter.12.cloned.1.call-update) | async-done | bytes 524304 | tf_op jit(solution)/shard_map/reduce_scatter | solution.py:240
  1162.4 6.3 add_convert_fusion
  1179.9 8.0 fusion.65
  1189.1 6.2 fusion.59
  1195.4 14.3 fusion.99
  1209.8 14.1 fusion.100
  1224.5 14.1 fusion.71
  1240.4 42.1 %all-reduce.6 = (f32[128]{0:T(128)}, f32[128]{0:T(128)}) all-reduce(f32[128]{0:T(128)S(1)} %get-tuple-element.308, f32[128]{0:T(128)S(1)} %get-tuple-element.310), channel_id=1, replica_groups=mesh['fsdp'=4,'ctx'=4,'tp'=2] {'fsdp','ctx','tp'}, use_global_device_ids=true, to_apply=%region_27.28 | all-reduce | flops 256 | bytes 2048 | tf_op jit(solution)/shard_map/psum | solution.py:282
  1285.9 78.3 %all-reduce.7 = (f32[2048]{0:T(1024)S(1)}, f32[2048]{0:T(1024)S(1)}) all-reduce(f32[2048]{0:T(1024)S(1)} %get-tuple-element.306, f32[2048]{0:T(1024)S(1)} %copy-done.50), channel_id=4, replica_groups=mesh['fsdp'=4,'ctx'=4,'tp'=2] {'fsdp','ctx'}, use_global_device_ids=true, to_apply=%region_21.22.clone | all-reduce | flops 4096 | bytes 32768
  1365.4 7.4 fusion.51
  1372.8 24.8 reduce-scatter.18.cloned.1.call-done
  1397.6 180.3 %reduce-scatter.20.cloned.1.call-done = f32[1024,128]{1,0:T(8,128)} async-done(((f32[1024,2048]{1,0:T(8,128)}), f32[1024,128]{1,0:T(8,128)}) %reduce-scatter.20.cloned.1.call-update) | async-done | bytes 524304 | tf_op jit(solution)/shard_map/reduce_scatter | solution.py:280
  1577.8 183.1 %reduce-scatter.14.cloned.1.call-done = f32[128,1024]{1,0:T(8,128)} async-done(((f32[2048,1024]{1,0:T(8,128)}), f32[128,1024]{1,0:T(8,128)}) %reduce-scatter.14.cloned.1.call-update) | async-done | bytes 524304 | tf_op jit(solution)/shard_map/reduce_scatter | solution.py:277
  1760.9 371.4 %reduce-scatter.22.cloned.1.call-done = f32[128,3072]{1,0:T(8,128)} async-done(((f32[2048,3072]{1,0:T(8,128)}), f32[128,3072]{1,0:T(8,128)}) %reduce-scatter.22.cloned.1.call-update) | async-done | bytes 1572880 | tf_op jit(solution)/shard_map/reduce_scatter | solution.py:183
  2132.4 367.8 %reduce-scatter.24.cloned.1.call-done = f32[128,3072]{1,0:T(8,128)} async-done(((f32[2048,3072]{1,0:T(8,128)}), f32[128,3072]{1,0:T(8,128)}) %reduce-scatter.24.cloned.1.call-update) | async-done | bytes 1572880 | tf_op jit(solution)/shard_map/reduce_scatter | solution.py:184
  2500.2 368.3 %reduce-scatter.26.cloned.1.call-done = f32[3072,128]{1,0:T(8,128)} async-done(((f32[3072,2048]{1,0:T(8,128)}), f32[3072,128]{1,0:T(8,128)}) %reduce-scatter.26.cloned.1.call-update) | async-done | bytes 1572880 | tf_op jit(solution)/shard_map/reduce_scatter | solution.py:185
  (361 shorter events, 210.1 us)
Async XLA Ops:
  7.2 49.1 %copy-start.10 = (bf16[512,2048]{1,0:T(8,128)(2,1)S(1)}, bf16[512,2048]{1,0:T(8,128)(2,1)}, u32[]{:S(2)}) copy-start(bf16[512,2048]{1,0:T(8,128)(2,1)} %param.19) | copy-start | bytes 6291460
  7.2 67.1 %all-gather.16.cloned.1.call-start = ((), (), s32[]{:S(2)}) async-start(), calls=%async_computation.11 | async-start | bytes 2228224 | tf_op jit(solution)/shard_map/all_gather | solution.py:96
  7.9 128.5 %all-gather.12.cloned.1.call-start = ((), (), s32[]{:S(2)}) async-start(), calls=%async_computation.9 | async-start | bytes 2228224 | tf_op jit(solution)/shard_map/all_gather | solution.py:97
  8.7 164.0 %all-gather.18.cloned.1.call-start = ((), (), s32[]{:S(2)}) async-start(), calls=%async_computation.12 | async-start | bytes 2621440 | tf_op jit(solution)/shard_map/all_gather | solution.py:114
  51.1 237.9 %copy-start.40 = (f32[16,1,128]{2,1,0:T(1,128)}, f32[16,1,128]{2,1,0:T(1,128)S(1)}, u32[]{:S(2)}) copy-start(f32[16,1,128]{2,1,0:T(1,128)S(1)} %convert_element_type.149) | copy-start | bytes 24580
  52.6 941.2 %copy-start.55 = (f32[512]{0:T(512)}, f32[512]{0:T(512)S(1)}, u32[]{:S(2)}) copy-start(f32[512]{0:T(512)S(1)} %get-tuple-element.362) | copy-start | bytes 6148
  53.3 24.1 copy-start.57
  54.6 22.7 copy-start.26
  54.6 248.0 %copy-start.24 = (f32[512,128]{1,0:T(8,128)}, f32[512,128]{1,0:T(8,128)S(1)}, u32[]{:S(2)}) copy-start(f32[512,128]{1,0:T(8,128)S(1)} %get-tuple-element.381) | copy-start | bytes 786436
  56.8 20.5 copy-start.51
  56.8 232.3 %copy-start.46 = (f32[512]{0:T(512)}, f32[512]{0:T(512)S(1)}, u32[]{:S(2)}) copy-start(f32[512]{0:T(512)S(1)} %fusion.80) | copy-start | bytes 6148
  79.8 61.9 %copy-start.61 = (bf16[128]{0:T(256)(128)(2,1)S(1)}, bf16[128]{0:T(256)(128)(2,1)}, u32[]{:S(2)}) copy-start(bf16[128]{0:T(256)(128)(2,1)} %param.28) | copy-start | bytes 772
  79.8 130.5 %all-gather.14.cloned.1.call-start = ((), (), s32[]{:S(2)}) async-start(), calls=%async_computation.10 | async-start | bytes 2621440 | tf_op jit(solution)/shard_map/all_gather | solution.py:115
  140.2 148.9 %all-gather.20.cloned.1.call-start = ((), (), s32[]{:S(2)}) async-start(), calls=%async_computation.13 | async-start | bytes 4456448 | tf_op jit(solution)/shard_map/all_gather | solution.py:95
  140.7 238.7 %all-gather.22.cloned.1.call-start = ((), (), s32[]{:S(2)}) async-start(), calls=%async_computation.14 | async-start | bytes 4456448 | tf_op jit(solution)/shard_map/all_gather | solution.py:98
  141.3 284.8 %all-reduce.13.cloned.1.call-start = ((), (), s32[]{:S(2)}) async-start(), calls=%async_computation.15 | async-start | bytes 8388608 | tf_op jit(solution)/shard_map/psum | solution.py:146
  141.7 156.6 %copy-start.53 = (f32[128]{0:T(128)}, f32[128]{0:T(128)S(1)}, u32[]{:S(2)}) copy-start(f32[128]{0:T(128)S(1)} %convert_element_type.122) | copy-start | bytes 1540
  386.4 183.2 %all-gather.24.cloned.1.call-start = ((), (), s32[]{:S(2)}) async-start(), calls=%async_computation.16 | async-start | bytes 13369344 | tf_op jit(solution)/shard_map/all_gather | solution.py:150
  387.1 335.9 %all-gather.26.cloned.1.call-start = ((), (), s32[]{:S(2)}) async-start(), calls=%async_computation.17 | async-start | bytes 13369344 | tf_op jit(solution)/shard_map/all_gather | solution.py:151
  387.9 532.2 %all-gather.28.cloned.1.call-start = ((), (), s32[]{:S(2)}) async-start(), calls=%async_computation.18 | async-start | bytes 13369344 | tf_op jit(solution)/shard_map/all_gather | solution.py:152
  388.5 600.1 %all-reduce.15.cloned.1.call-start = ((), (), s32[]{:S(2)}) async-start(), calls=%async_computation.19 | async-start | bytes 8388608 | tf_op jit(solution)/shard_map/psum | solution.py:175
  937.6 12.2 copy-start.63
  961.8 162.1 %reduce-scatter.10.cloned.1.call-start = ((), (), s32[]{:S(2)}) async-start(), calls=%async_computation.20 | async-start | bytes 2621440 | tf_op jit(solution)/shard_map/reduce_scatter | solution.py:237
  988.5 5.2 copy-start.4
  988.5 5.9 copy-start.17
  1004.4 5.6 copy-start.35
  1014.1 7.0 copy-start.2
  1023.9 5.6 copy-start.35
  1033.7 7.0 copy-start.2
  1043.5 5.6 copy-start.35
  1053.3 7.0 copy-start.2
  1063.1 5.6 copy-start.35
  1072.9 7.0 copy-start.2
  1087.3 75.0 %reduce-scatter.12.cloned.1.call-start = ((), (), s32[]{:S(2)}) async-start(), calls=%async_computation.21 | async-start | bytes 2621440 | tf_op jit(solution)/shard_map/reduce_scatter | solution.py:240
  1087.4 11.7 copy-start.7
  1106.0 176.6 %all-reduce.17.cloned.1.call-start = ((), (), s32[]{:S(2)}) async-start(), calls=%async_computation.29 | async-start | bytes 8388608 | tf_op jit(solution)/shard_map/psum | solution.py:159
  1112.8 4.7 copy-start.60
  1117.5 7.6 copy-start.32
  1127.0 35.4 %copy-start.33 = (bf16[2048,512]{1,0:T(8,128)(2,1)S(1)}, bf16[2048,512]{1,0:T(8,128)(2,1)}, u32[]{:S(2)}) copy-start(bf16[2048,512]{1,0:T(8,128)(2,1)} %all-gather.12.cloned.1.call-done) | copy-start | bytes 6291460
  1168.6 204.1 %reduce-scatter.16.cloned.1.call-start = ((), (), s32[]{:S(2)}) async-start(), calls=%async_computation.23 | async-start | bytes 4456448 | tf_op jit(solution)/shard_map/reduce_scatter | solution.py:278
  1173.7 223.9 %reduce-scatter.18.cloned.1.call-start = ((), (), s32[]{:S(2)}) async-start(), calls=%async_computation.24 | async-start | bytes 4456448 | tf_op jit(solution)/shard_map/reduce_scatter | solution.py:279
  1178.6 399.2 %reduce-scatter.20.cloned.1.call-start = ((), (), s32[]{:S(2)}) async-start(), calls=%async_computation.25 | async-start | bytes 8912896 | tf_op jit(solution)/shard_map/reduce_scatter | solution.py:280
  1187.9 573.1 %reduce-scatter.14.cloned.1.call-start = ((), (), s32[]{:S(2)}) async-start(), calls=%async_computation.22 | async-start | bytes 8912896 | tf_op jit(solution)/shard_map/reduce_scatter | solution.py:277
  1195.3 937.0 %reduce-scatter.22.cloned.1.call-start = ((), (), s32[]{:S(2)}) async-start(), calls=%async_computation.26 | async-start | bytes 26738688 | tf_op jit(solution)/shard_map/reduce_scatter | solution.py:183
  1209.7 1290.5 %reduce-scatter.24.cloned.1.call-start = ((), (), s32[]{:S(2)}) async-start(), calls=%async_computation.27 | async-start | bytes 26738688 | tf_op jit(solution)/shard_map/reduce_scatter | solution.py:184
  1223.9 1644.6 %reduce-scatter.26.cloned.1.call-start = ((), (), s32[]{:S(2)}) async-start(), calls=%async_computation.28 | async-start | bytes 26738688 | tf_op jit(solution)/shard_map/reduce_scatter | solution.py:185
  1238.6 47.3 %copy-start.50 = (f32[2048]{0:T(1024)S(1)}, f32[2048]{0:T(1024)}, u32[]{:S(2)}) copy-start(f32[2048]{0:T(1024)} %get-tuple-element.304) | copy-start | bytes 24580
  1238.6 126.8 %copy-start.52 = (f32[512]{0:T(512)S(1)}, f32[512]{0:T(512)}, u32[]{:S(2)}) copy-start(f32[512]{0:T(512)} %copy-done.51) | copy-start | bytes 6148
  (58 other events, 140.8 us)
Sparse Core Ops, SparseCore 0:
  10.8 63.4 all-gather.15
  77.1 59.3 all-gather.11
  138.8 33.8 all-gather.17
  175.0 35.3 all-gather.13
  212.9 76.0 all-gather.19
  291.6 87.7 all-gather.21
  386.5 26.6 all-reduce.12
  416.4 153.1 all-gather.23
  572.8 150.1 all-gather.25
  725.9 194.1 all-gather.27
  961.9 26.6 all-reduce.14
  1087.5 36.3 reduce-scatter.9
  1127.1 35.2 reduce-scatter.11
  1168.8 28.4 all-reduce.16
  1200.1 97.6 reduce-scatter.15
  1300.7 96.8 reduce-scatter.17
  1400.4 177.4 reduce-scatter.19
  1580.7 180.2 reduce-scatter.13
  1768.2 364.1 reduce-scatter.21
  2139.5 360.6 reduce-scatter.23
  2507.5 360.9 reduce-scatter.25
where the time goes:
time: 2880 us
  waiting for transfers between devices  2230 us (77%)
  matrix products  283 us (10%)
  blocking collectives  200 us (7%)
  local copies, waits for them, and re-layouts  89.1 us (3%)
  other arithmetic  48.9 us (2%)
    reduce_scatter x1, waiting for transfers between devices, on_device(): lax.psum_scatter(grad_gate, ('fsdp', 'ctx'), scatter_dimension=0, tiled=T...  371 us
    reduce_scatter x1, waiting for transfers between devices, on_device(): lax.psum_scatter(grad_down, ('fsdp', 'ctx'), scatter_dimension=1, tiled=T...  368 us
    reduce_scatter x1, waiting for transfers between devices, on_device(): lax.psum_scatter(grad_up, ('fsdp', 'ctx'), scatter_dimension=0, tiled=True)  368 us
    all_gather x1, waiting for transfers between devices, on_device(): lax.all_gather(w_down, ('fsdp', 'ctx'), axis=1, tiled=True)  185 us
    reduce_scatter x1, waiting for transfers between devices, on_device(): lax.psum_scatter(grad_query_weight, ('fsdp', 'ctx'), scatter_dimension=0,...  183 us
    reduce_scatter x1, waiting for transfers between devices, on_device(): lax.psum_scatter(grad_out, ('fsdp', 'ctx'), scatter_dimension=1, tiled=True)  180 us
    all_gather x1, waiting for transfers between devices, on_device(): lax.all_gather(w_up, ('fsdp', 'ctx'), axis=0, tiled=True)  141 us
    all_gather x1, waiting for transfers between devices, on_device(): lax.all_gather(w_gate, ('fsdp', 'ctx'), axis=0, tiled=True)  136 us
  transfers between devices with their start and end apart: 21, of which 18 were waited for; matrix products, arithmetic and copies ran while one was open for 9% of the time, Pallas kernels for 0%

commit v1 on v0

v1 whole, which is shorter than its diff:
```python
import functools
import math

import jax
import jax.numpy as jnp
from jax import lax
from jax.experimental import pallas as pl
from jax.experimental.pallas import tpu as pltpu
from jax.sharding import PartitionSpec as P

BLK = 128
EPS = 1e-06
THETA = 1000000.0
CTX = 4
TILE = 256


def _dot(a, b, dims):
    return lax.dot_general(a, b, (dims, ((), ())), preferred_element_type=jnp.float32)


def _forward_kernel(heads, scale, info, *refs):
    waves = refs[:-11]
    cos_ref, sin_ref, qg_ref, kg_ref, low_ref, mixed_ref, mlow_ref, rtot_ref, q_s, k_s, v_s = refs[-11:]
    hd = cos_ref.shape[1]
    rows = cos_ref.shape[0]
    wave_rows = rows // len(waves)
    factor = scale * math.log2(math.e)

    def prepare(block, wave_ref, base):
        local = pl.multiple_of(block * BLK, BLK)
        at = pl.multiple_of(base + block * BLK, BLK)
        here = pl.ds(at, BLK)
        cosine = cos_ref[here, :]
        sine = sin_ref[here, :]
        for h in range(heads + 1):
            u = wave_ref[pl.ds(local, BLK), h * hd : (h + 1) * hd]
            gain = qg_ref[...] if h < heads else kg_ref[...]
            n = u * lax.rsqrt(jnp.mean(u * u, axis=1, keepdims=True) + EPS) * gain
            o = (n * cosine + pltpu.roll(n, hd // 2, 1) * sine).astype(jnp.bfloat16)
            low_ref[here, h * hd : (h + 1) * hd] = o
            if h < heads:
                q_s[h, here, :] = o
            else:
                k_s[here, :] = o
        val = wave_ref[pl.ds(local, BLK), (heads + 1) * hd :].astype(jnp.bfloat16)
        low_ref[here, (heads + 1) * hd :] = val
        v_s[here, :] = val

    for w, wave_ref in enumerate(waves):

        @pl.loop(0, wave_rows // BLK)
        def _(block, wave_ref=wave_ref, base=w * wave_rows):
            prepare(block, wave_ref, base)

    length = info[rows // BLK]
    per = TILE // BLK

    def gather(ref, tile, *lead):
        parts = [
            ref[lead + (pl.ds(pl.multiple_of(info[tile * per + b] * BLK, BLK), BLK), slice(None))]
            for b in range(per)
        ]
        return jnp.concatenate(parts, axis=0)

    @pl.loop(0, rows // TILE)
    def _(i):
        query = jnp.concatenate([gather(q_s, i, h) for h in range(heads)], axis=0)
        full = jnp.minimum(i, length // TILE)

        def scores(j):
            return jnp.exp2(_dot(query, gather(k_s, j), ((1,), (1,))) * factor)

        def take(expo, j, acc, tot):
            part = expo[:, :hd]
            for b in range(1, TILE // hd):
                part = part + expo[:, b * hd : (b + 1) * hd]
            acc = acc + _dot(expo.astype(jnp.bfloat16), gather(v_s, j), ((1,), (0,)))
            return acc, tot + part

        def step(j, carry):
            return take(scores(j), j, *carry)

        zero = jnp.zeros((heads * TILE, hd), jnp.float32)
        acc, tot = lax.fori_loop(0, full, step, (zero, zero))
        expo = scores(full)
        qpos = i * TILE + lax.rem(lax.broadcasted_iota(jnp.int32, expo.shape, 0), TILE)
        kpos = full * TILE + lax.broadcasted_iota(jnp.int32, expo.shape, 1)
        expo = jnp.where((kpos <= qpos) & (kpos < length), expo, 0.0)
        acc, tot = take(expo, full, acc, tot)
        recip = 1.0 / jnp.sum(tot, axis=1, keepdims=True)
        mixed = acc * recip
        recip = jnp.broadcast_to(recip, mixed.shape)
        for h in range(heads):
            for b in range(per):
                at = pl.ds(pl.multiple_of(info[i * per + b] * BLK, BLK), BLK)
                cut = slice(h * TILE + b * BLK, h * TILE + (b + 1) * BLK)
                lanes = slice(h * hd, (h + 1) * hd)
                mixed_ref[at, lanes] = mixed[cut]
                mlow_ref[at, lanes] = mixed[cut].astype(jnp.bfloat16)
                rtot_ref[at, lanes] = recip[cut]


def attend_forward(info, waves, cosine, sine, query_gain, key_gain, heads):
    rows, hd = cosine.shape
    assert waves[0].shape[1] == (heads + 2) * hd
    width = heads * hd
    pairs = rows * rows // 2 * heads
    return pl.pallas_call(
        functools.partial(_forward_kernel, heads, hd**-0.5),
        out_shape=(
            jax.ShapeDtypeStruct((rows, (heads + 2) * hd), jnp.bfloat16),
            jax.ShapeDtypeStruct((rows, width), jnp.float32),
            jax.ShapeDtypeStruct((rows, width), jnp.bfloat16),
            jax.ShapeDtypeStruct((rows, width), jnp.float32),
        ),
        in_specs=[pl.BlockSpec(memory_space=pltpu.SMEM)]
        + [pl.BlockSpec(memory_space=pltpu.VMEM)] * (len(waves) + 4),
        out_specs=[pl.BlockSpec(memory_space=pltpu.VMEM)] * 4,
        scratch_shapes=[
            pltpu.VMEM((heads, rows, hd), jnp.bfloat16),
            pltpu.VMEM((rows, hd), jnp.bfloat16),
            pltpu.VMEM((rows, hd), jnp.bfloat16),
        ],
        compiler_params=pltpu.CompilerParams(vmem_limit_bytes=48 * 2**20),
        cost_estimate=pl.CostEstimate(
            flops=pairs * hd * 4, bytes_accessed=rows * hd * 60, transcendentals=pairs
        ),
        name="attend_forward",
    )(info, *waves, cosine, sine, query_gain, key_gain)


def _backward_kernel(heads, scale, info, *refs):
    count = (len(refs) - 13) // 2
    waves, gmixed = refs[:count], refs[count : 2 * count]
    (low_ref, mixed_ref, rtot_ref, cos_ref, sin_ref, qg_ref, kg_ref, out_ref, gain_ref, gacc_s, dq_s, dk_s, dv_s) = refs[
        2 * count :
    ]
    hd = cos_ref.shape[1]
    rows = cos_ref.shape[0]
    wave_rows = rows // count
    factor = scale * math.log2(math.e)
    length = info[rows // BLK]
    per = TILE // BLK

    dk_s[...] = jnp.zeros_like(dk_s)
    dv_s[...] = jnp.zeros_like(dv_s)
    gain_ref[...] = jnp.zeros_like(gain_ref)

    for w, g_ref in enumerate(gmixed):

        @pl.loop(0, wave_rows // BLK)
        def _(block, g_ref=g_ref, base=w * wave_rows):
            local = pl.ds(pl.multiple_of(block * BLK, BLK), BLK)
            at = pl.ds(pl.multiple_of(base + block * BLK, BLK), BLK)
            for h in range(heads):
                lanes = slice(h * hd, (h + 1) * hd)
                g = g_ref[local, lanes] * rtot_ref[at, lanes]
                gacc_s[h, at, :] = g.astype(jnp.bfloat16)
                dq_s[h, at, :] = g * mixed_ref[at, lanes]

    def spots(tile):
        return [pl.ds(pl.multiple_of(info[tile * per + b] * BLK, BLK), BLK) for b in range(per)]

    @pl.loop(0, pl.cdiv(length, TILE))
    def _(i):
        at = spots(i)
        query = jnp.concatenate(
            [low_ref[s, h * hd : (h + 1) * hd] for h in range(heads) for s in at], axis=0
        )
        gacc = jnp.concatenate([gacc_s[h, s, :] for h in range(heads) for s in at], axis=0)
        terms = jnp.concatenate([dq_s[h, s, :] for h in range(heads) for s in at], axis=0)
        shift = jnp.sum(terms.T, axis=0, keepdims=True)

        def tile(j, dq, masked):
            spot = spots(j)
            key = jnp.concatenate([low_ref[s, heads * hd : (heads + 1) * hd] for s in spot], axis=0)
            val = jnp.concatenate([low_ref[s, (heads + 1) * hd :] for s in spot], axis=0)
            expo = jnp.exp2(_dot(key, query, ((1,), (1,))) * factor)
            if masked:
                kpos = j * TILE + lax.broadcasted_iota(jnp.int32, expo.shape, 0)
                qpos = i * TILE + lax.rem(lax.broadcasted_iota(jnp.int32, expo.shape, 1), TILE)
                expo = jnp.where((kpos <= qpos) & (kpos < length), expo, 0.0)
            probs = _dot(val, gacc, ((1,), (1,)))
            ds = (expo * (probs - shift)).astype(jnp.bfloat16)
            dv = _dot(expo.astype(jnp.bfloat16), gacc, ((1,), (0,)))
            dk = _dot(ds, query, ((1,), (0,)))
            for b, s in enumerate(spot):
                dv_s[s, :] += dv[b * BLK : (b + 1) * BLK]
                dk_s[s, :] += dk[b * BLK : (b + 1) * BLK]
            return dq + _dot(ds, key, ((0,), (0,)))

        zero = jnp.zeros((heads * TILE, hd), jnp.float32)
        dq = lax.fori_loop(0, i, lambda j, dq: tile(j, dq, False), zero)
        dq = tile(i, dq, True) * scale
        for h in range(heads):
            for b, s in enumerate(at):
                dq_s[h, s, :] = dq[h * TILE + b * BLK : h * TILE + (b + 1) * BLK]

    def finish(wave_ref, block, base):
        local = pl.ds(pl.multiple_of(block * BLK, BLK), BLK)
        at = pl.ds(pl.multiple_of(base + block * BLK, BLK), BLK)
        cosine = cos_ref[at, :]
        sine = sin_ref[at, :]
        for h in range(heads + 1):
            lanes = slice(h * hd, (h + 1) * hd)
            u = wave_ref[local, lanes]
            r = lax.rsqrt(jnp.mean(u * u, axis=1, keepdims=True) + EPS)
            d = dq_s[h, at, :] if h < heads else dk_s[at, :] * scale
            dn = d * cosine - pltpu.roll(d, hd // 2, 1) * sine
            gain = qg_ref[...] if h < heads else kg_ref[...]
            hat = u * r
            row = 0 if h < heads else 1
            gain_ref[row : row + 1, :] += jnp.sum(dn * hat, axis=0, keepdims=True)
            dg = dn * gain
            du = r * (dg - hat * jnp.mean(dg * hat, axis=1, keepdims=True))
            out_ref[at, lanes] = du.astype(jnp.bfloat16)
        out_ref[at, (heads + 1) * hd :] = dv_s[at, :].astype(jnp.bfloat16)

    for b in range(rows // BLK):

        @pl.when(b * BLK >= pl.cdiv(length, TILE) * TILE)
        def _(b=b):
            at = pl.ds(pl.multiple_of(info[b] * BLK, BLK), BLK)
            for h in range(heads):
                dq_s[h, at, :] = jnp.zeros((BLK, hd), jnp.float32)

    for w, wave_ref in enumerate(waves):

        @pl.loop(0, wave_rows // BLK)
        def _(block, wave_ref=wave_ref, base=w * wave_rows):
            finish(wave_ref, block, base)


def attend_backward(info, waves, gmixed, low, mixed, rtot, cosine, sine, query_gain, key_gain, heads):
    rows, hd = cosine.shape
    pairs = rows * rows // 2 * heads
    return pl.pallas_call(
        functools.partial(_backward_kernel, heads, hd**-0.5),
        out_shape=(
            jax.ShapeDtypeStruct((rows, (heads + 2) * hd), jnp.bfloat16),
            jax.ShapeDtypeStruct((8, hd), jnp.float32),
        ),
        in_specs=[pl.BlockSpec(memory_space=pltpu.SMEM)]
        + [pl.BlockSpec(memory_space=pltpu.VMEM)] * (2 * len(waves) + 7),
        out_specs=[pl.BlockSpec(memory_space=pltpu.VMEM)] * 2,
        scratch_shapes=[
            pltpu.VMEM((heads, rows, hd), jnp.bfloat16),
            pltpu.VMEM((heads, rows, hd), jnp.float32),
            pltpu.VMEM((rows, hd), jnp.float32),
            pltpu.VMEM((rows, hd), jnp.float32),
        ],
        compiler_params=pltpu.CompilerParams(vmem_limit_bytes=48 * 2**20),
        cost_estimate=pl.CostEstimate(
            flops=pairs * hd * 10, bytes_accessed=rows * hd * 100, transcendentals=pairs
        ),
        name="attend_backward",
    )(info, *waves, *gmixed, low, mixed, rtot, cosine, sine, query_gain, key_gain)


def product(left, right):
    return jnp.dot(left, right, preferred_element_type=jnp.float32)


def left_transposed(left, right):
    return lax.dot_general(
        left, right, (((0,), (0,)), ((), ())), preferred_element_type=jnp.float32
    )


def right_transposed(left, right):
    return lax.dot_general(
        left, right, (((1,), (1,)), ((), ())), preferred_element_type=jnp.float32
    )


def low(values):
    return values.astype(jnp.bfloat16)


def wide(values):
    return values.astype(jnp.float32)


def across(values, bits):
    return lax.ppermute(values, "ctx", [(i, i ^ bits) for i in range(CTX)])


def other_core(values):
    return lax.ppermute(values, "tp", [(0, 1), (1, 0)])


def next_stage(values):
    count = lax.axis_size("fsdp")
    return lax.ppermute(values, "fsdp", [(i, (i - 1) % count) for i in range(count)])


def in_order(pieces, spot, axis):
    for bit in (1, 2):
        odd = (spot & bit) != 0
        pieces = [jnp.where(odd, pieces[j ^ bit], pieces[j]) for j in range(CTX)]
    return jnp.concatenate(pieces, axis=axis)


def gather_rows(own):
    half = own.shape[0] // 2
    own_other = other_core(own)
    by_x = across(own, 1)
    by_y = across(own, 2)
    x_other = other_core(by_x)
    y_other = other_core(by_y)
    far_top = across(by_x[:half], 2)
    far_bottom = across(by_y[half:], 1)
    far = jnp.concatenate([far_top, far_bottom], axis=0)
    far_other = other_core(far)
    return [
        jnp.concatenate(pair, axis=0)
        for pair in ((own, own_other), (by_x, x_other), (by_y, y_other), (far, far_other))
    ]


def scatter_rows(part):
    def over_cores(chip):
        mine, others = part(chip)
        return mine + wide(other_core(low(others)))

    far = low(over_cores(3))
    half = far.shape[0] // 2
    to_y = across(far[:half], 1)
    to_x = across(far[half:], 2)
    by_x = over_cores(1)
    by_x = low(jnp.concatenate([by_x[:half], by_x[half:] + wide(to_x)], axis=0))
    from_x = across(by_x, 1)
    by_y = over_cores(2)
    by_y = low(jnp.concatenate([by_y[:half] + wide(to_y), by_y[half:]], axis=0))
    from_y = across(by_y, 2)
    return over_cores(0) + wide(from_x) + wide(from_y)


def halves(left, right_of):
    half = left.shape[0] // 2
    return right_of(left[:half]), right_of(left[half:])


def deal_out(values, spot, size, axis):
    got = []
    for j in range(CTX):
        piece = [
            lax.dynamic_slice_in_dim(v, (spot ^ j) * n, n, axis) for v, n in zip(values, size)
        ]
        piece = jnp.concatenate(piece, axis=axis) if len(piece) > 1 else piece[0]
        got.append(across(piece, j) if j else piece)
    return got


def ring_gather(shard):
    pieces = [shard]
    for _ in range(lax.axis_size("fsdp") - 1):
        pieces.append(next_stage(pieces[-1]))
    return pieces


def ring_sum(chunk):
    count = lax.axis_size("fsdp")
    total = chunk(1 % count)
    for step in range(2, count + 1):
        total = chunk(step % count) + wide(next_stage(low(total)))
    return total


def turned(values, shift, count):
    width = values.shape[1]
    return lax.dynamic_slice_in_dim(
        jnp.concatenate([values, values], axis=1), shift * (width // count), width, 1
    )


def on_device(
    tokens,
    cotangent,
    lengths,
    deal,
    attn_gain,
    w_query,
    w_key,
    w_value,
    w_out,
    query_gain,
    key_gain,
    ffn_gain,
    w_gate,
    w_up,
    w_down,
):
    stage = lax.axis_index("fsdp")
    stages = lax.axis_size("fsdp")
    spot = lax.axis_index("ctx")
    core = lax.axis_index("tp")
    local_rows, width = tokens.shape
    head_size = query_gain.shape[0]
    rows = local_rows * CTX
    half_rows = local_rows // 2
    heads = w_query.shape[1] // head_size // CTX
    query_cols = heads * head_size
    units = w_gate.shape[1] // CTX
    chunk = width // stages
    shard = chunk // CTX

    attn_scale = wide(attn_gain)[:, None]
    feed_scale = wide(ffn_gain)[:, None]
    scaled = [low(wide(w) * attn_scale) for w in (w_query, w_key, w_value)]
    proj_shard = in_order(
        deal_out(scaled, spot, (query_cols, head_size, head_size), 1), spot, 0
    )
    proj_weight = jnp.concatenate(ring_gather(proj_shard), axis=0)
    out_shard = in_order(deal_out([w_out], spot, (query_cols,), 0), spot, 1)
    out_weight = jnp.concatenate(ring_gather(out_shard), axis=1)
    scaled = [low(wide(w) * feed_scale) for w in (w_gate, w_up)]
    feed_shard = in_order(deal_out(scaled, spot, (units, units), 1), spot, 0)
    feed_weight = jnp.concatenate(ring_gather(feed_shard), axis=0)
    down_shard = in_order(deal_out([w_down], spot, (units,), 0), spot, 1)
    down_weight = jnp.concatenate(ring_gather(down_shard), axis=1)

    per_half = half_rows // BLK
    order = jnp.arange(deal.shape[1], dtype=jnp.int32).reshape(CTX, 2, per_half)
    chips = jnp.arange(CTX, dtype=jnp.int32) ^ spot
    cores = jnp.arange(2, dtype=jnp.int32) ^ core
    order = ((chips[:, None] * 2 + cores[None, :])[:, :, None] * per_half + order[0, 0]).reshape(-1)
    blocks = jnp.sum(
        jnp.where(order[:, None] == jnp.arange(order.shape[0])[None, :], deal[0][None, :], 0), axis=1
    )
    spots = jnp.arange(order.shape[0], dtype=jnp.int32)
    where_is = jnp.sum(
        jnp.where(blocks[None, :] == spots[:, None], spots[None, :], 0), axis=1
    ).astype(jnp.int32)
    info = jnp.concatenate([where_is, lengths])
    positions = (blocks[:, None] * BLK + jnp.arange(BLK, dtype=jnp.int32)[None, :]).reshape(-1)
    frequency = THETA ** (-(jnp.arange(head_size // 2, dtype=jnp.float32) * 2.0 / head_size))
    angles = wide(positions)[:, None] * frequency[None, :]
    cosine, sine = jnp.cos(angles), jnp.sin(angles)
    cosine = jnp.concatenate([cosine, cosine], axis=1)
    sine = jnp.concatenate([-sine, sine], axis=1)
    query_scale = wide(query_gain)[None, :]
    key_scale = wide(key_gain)[None, :]

    own = lax.dynamic_slice_in_dim(tokens, core * half_rows, half_rows, 0)
    inputs = wide(turned(own, stage, stages))
    rstd = lax.rsqrt(jnp.mean(inputs * inputs, axis=1, keepdims=True) + EPS)
    hat = inputs * rstd
    normed = gather_rows(low(hat))
    projected = [product(n, proj_weight) for n in normed]
    qkv, mixed, mixed_low, recip = attend_forward(
        info, projected, cosine, sine, query_scale, key_scale, heads
    )

    def rows_of(values, chip):
        return values[chip * local_rows : (chip + 1) * local_rows]

    attn = scatter_rows(
        lambda chip: halves(rows_of(mixed_low, chip), lambda m: product(m, out_weight))
    )
    hidden = inputs + attn

    valid = positions[:half_rows] < lengths[0]
    seed = lax.dynamic_slice_in_dim(cotangent, core * half_rows, half_rows, 0)
    seed = jnp.where(valid[:, None], turned(seed, stage, stages), 0).astype(jnp.bfloat16)
    seeds = gather_rows(seed)
    rstd_two = lax.rsqrt(jnp.mean(hidden * hidden, axis=1, keepdims=True) + EPS)
    hat_two = hidden * rstd_two
    normed_two = gather_rows(low(hat_two))
    inner, grads = [], []
    for chip in range(CTX):
        gate_up = product(normed_two[chip], feed_weight)
        gate, upper = gate_up[:, :units], gate_up[:, units:]
        grad_inner = right_transposed(seeds[chip], down_weight)
        sigma = jax.nn.sigmoid(gate)
        silu = gate * sigma
        inner.append(low(silu * upper))
        grad_gate = grad_inner * upper * sigma * (1.0 + gate * (1.0 - sigma))
        grads.append(low(jnp.concatenate([grad_gate, grad_inner * silu], axis=1)))
    grad_normed_two = scatter_rows(
        lambda chip: halves(grads[chip], lambda g: right_transposed(g, feed_weight))
    )
    feed = scatter_rows(lambda chip: halves(inner[chip], lambda m: product(m, down_weight)))
    output_half = low(hidden + feed)
    grad_hat = grad_normed_two - hat_two * jnp.mean(
        grad_normed_two * hat_two, axis=1, keepdims=True
    )
    grad_hidden = wide(seed) + rstd_two * grad_hat
    grad_attn = gather_rows(low(grad_hidden))

    inner_all = jnp.concatenate(inner, axis=0)
    seed_all = jnp.concatenate(seeds, axis=0)
    grads_all = jnp.concatenate(grads, axis=0)
    normed_two_all = jnp.concatenate(normed_two, axis=0)
    grad_down = ring_sum(
        lambda k: left_transposed(inner_all, seed_all[:, k * chunk : (k + 1) * chunk])
    )
    grad_feed = ring_sum(
        lambda k: left_transposed(normed_two_all[:, k * chunk : (k + 1) * chunk], grads_all)
    )

    grad_mixed = [right_transposed(g, out_weight) for g in grad_attn]
    grad_proj, gain_sums = attend_backward(
        info, projected, grad_mixed, qkv, mixed, recip, cosine, sine, query_scale, key_scale, heads
    )
    grad_normed = scatter_rows(
        lambda chip: halves(
            rows_of(grad_proj, chip), lambda g: right_transposed(g, proj_weight)
        )
    )
    grad_attn_all = jnp.concatenate(grad_attn, axis=0)
    normed_all = jnp.concatenate(normed, axis=0)
    grad_out = ring_sum(
        lambda k: left_transposed(mixed_low, grad_attn_all[:, k * chunk : (k + 1) * chunk])
    )
    grad_project = ring_sum(
        lambda k: left_transposed(normed_all[:, k * chunk : (k + 1) * chunk], grad_proj)
    )
    grad_hat = grad_normed - hat * jnp.mean(grad_normed * hat, axis=1, keepdims=True)
    grad_tokens_half = grad_hidden + rstd * grad_hat

    def whole_rows(values):
        values = turned(values, (stages - stage) % stages, stages)
        other = other_core(values)
        first = core == 0
        return jnp.concatenate(
            [jnp.where(first, values, other), jnp.where(first, other, values)], axis=0
        )

    def dealt_rows(values):
        values = low(values)
        got = [
            lax.dynamic_slice_in_dim(values, (spot ^ j) * shard, shard, 0) for j in range(CTX)
        ]
        return [across(v, j) if j else v for j, v in enumerate(got)]

    def dealt_cols(values):
        values = low(values)
        got = [
            lax.dynamic_slice_in_dim(values, (spot ^ j) * shard, shard, 1) for j in range(CTX)
        ]
        return wide(in_order([across(v, j) if j else v for j, v in enumerate(got)], spot, 0))

    def cut(pieces, start, size):
        return wide(in_order([p[:, start : start + size] for p in pieces], spot, 1))

    feed_pieces = dealt_rows(grad_feed)
    grad_gate_w = cut(feed_pieces, 0, units)
    grad_up_w = cut(feed_pieces, units, units)
    proj_pieces = dealt_rows(grad_project)
    grad_query_w = cut(proj_pieces, 0, query_cols)
    grad_key_w = cut(proj_pieces, query_cols, head_size)
    grad_value_w = cut(proj_pieces, query_cols + head_size, head_size)

    def gain_part(pairs):
        return sum(jnp.sum(wide(w) * g, axis=1) for w, g in pairs)

    feed_gain = gain_part(((w_gate, grad_gate_w), (w_up, grad_up_w)))
    norm_gain = gain_part(((w_query, grad_query_w), (w_key, grad_key_w), (w_value, grad_value_w)))
    feed_gain = feed_gain + other_core(feed_gain)
    norm_gain = norm_gain + other_core(norm_gain)
    gain_sums = gain_sums + other_core(gain_sums)
    for bit in (1, 2):
        gain_sums = gain_sums + across(gain_sums, bit)
    term = gain_sums
    for _ in range(stages - 1):
        term = next_stage(term)
        gain_sums = gain_sums + term
    return (
        whole_rows(output_half),
        whole_rows(grad_tokens_half),
        norm_gain,
        grad_query_w * attn_scale,
        grad_key_w * attn_scale,
        grad_value_w * attn_scale,
        dealt_cols(grad_out),
        gain_sums[0],
        gain_sums[1],
        feed_gain,
        grad_gate_w * feed_scale,
        grad_up_w * feed_scale,
        dealt_cols(grad_down),
    )


def solution(mesh):
    return jax.shard_map(
        on_device,
        mesh=mesh,
        in_specs=(
            P(("fsdp", "ctx"), None),
            P(("fsdp", "ctx"), None),
            P("fsdp"),
            P("fsdp", None),
            P(("fsdp", "ctx")),
            P(("fsdp", "ctx"), "tp"),
            P(("fsdp", "ctx"), "tp"),
            P(("fsdp", "ctx"), "tp"),
            P("tp", ("fsdp", "ctx")),
            P(),
            P(),
            P(("fsdp", "ctx")),
            P(("fsdp", "ctx"), "tp"),
            P(("fsdp", "ctx"), "tp"),
            P("tp", ("fsdp", "ctx")),
        ),
        out_specs=(
            P(("fsdp", "ctx"), None),
            P(("fsdp", "ctx"), None),
            P(("fsdp", "ctx")),
            P(("fsdp", "ctx"), "tp"),
            P(("fsdp", "ctx"), "tp"),
            P(("fsdp", "ctx"), "tp"),
            P("tp", ("fsdp", "ctx")),
            P(),
            P(),
            P(("fsdp", "ctx")),
            P(("fsdp", "ctx"), "tp"),
            P(("fsdp", "ctx"), "tp"),
            P("tp", ("fsdp", "ctx")),
        ),
        check_vma=False,
    )
```

time: 2880 us -> 768 us (0.27)
  waiting for transfers between devices: 2230 us -> 312 us
  blocking collectives: 200 us -> 0 us
  matrix products: 283 us -> 146 us
  starting transfers between devices: 1.61 us -> 134 us
  Pallas kernels: 0 us -> 59.1 us
  local copies, waits for them, and re-layouts: 89.1 us -> 54.1 us
    reduce_scatter x9 -> x0, waiting for transfers between devices: 1530 us -> none  [the longest x1 371 us: on_device(): lax.psum_scatter(grad_gate, ('fsdp', 'ctx'), scatter_dimension=0, tiled=T...]
    all_gather x9 -> x0, waiting for transfers between devices: 674 us -> none  [the longest x1 185 us: on_device(): lax.all_gather(w_down, ('fsdp', 'ctx'), axis=1, tiled=True)]
    ppermute x0 -> x122, waiting for transfers between devices: none -> 312 us  [the longest x58 161 us: across(): return lax.ppermute(values, 'ctx', [(i, i ^ bits) for i in range(CTX)])]
    ppermute x0 -> x122, starting transfers between devices: none -> 134 us  [the longest x58 64.2 us: across(): return lax.ppermute(values, 'ctx', [(i, i ^ bits) for i in range(CTX)])]
    dot_general x28 -> x0, matrix products: 107 us -> none  [the longest x8 34.8 us: score_weights(): jnp.einsum('tkgd,skd->kgts', queries, key_block, preferred_element_type=j...]
    all_gather x2 -> x0, blocking collectives: 80 us -> none  [the longest x1 42.4 us: on_device(): lax.all_gather(attn_gain, ('fsdp', 'ctx'), axis=0, tiled=True)]
    unnamed x1 -> x0, blocking collectives: 78.3 us -> none
    pallas_call x0 -> x2, Pallas kernels: none -> 59.1 us  [the longest x1 34.8 us: attend_backward(): pl.pallas_call(functools.partial(_backward_kernel, heads, hd ** (-0.5)),...]
  transfers between devices with their start and end apart: 21 -> 122, of which waited for: 18 -> 52; matrix products, arithmetic and copies ran while one was open for 9% -> 32% of each run, Pallas kernels for 0% -> 3%
where the time goes in v1:
time: 768 us; the launch traced here: 764 us
  waiting for transfers between devices  312 us (41%)
  matrix products  146 us (19%)
  starting transfers between devices  134 us (17%)
  Pallas kernels  59.1 us (8%)
  other arithmetic  54.7 us (7%)
  local copies, waits for them, and re-layouts  54.1 us (7%)
    ppermute x58, waiting for transfers between devices, across(): return lax.ppermute(values, 'ctx', [(i, i ^ bits) for i in range(CTX)])  161 us
    ppermute x27, waiting for transfers between devices, next_stage(): lax.ppermute(values, 'fsdp', [(i, (i - 1) % count) for i in range(count)])  148 us
    ppermute x58, starting transfers between devices, across(): return lax.ppermute(values, 'ctx', [(i, i ^ bits) for i in range(CTX)])  64.2 us
    ppermute x27, starting transfers between devices, next_stage(): lax.ppermute(values, 'fsdp', [(i, (i - 1) % count) for i in range(count)])  63.1 us
    dot_general x24, matrix products, right_transposed(): lax.dot_general(left, right, (((1,), (1,)), ((), ())), preferred_element_...  51.5 us
    dot_general x16, matrix products, left_transposed(): lax.dot_general(left, right, (((0,), (0,)), ((), ())), preferred_element_...  50.1 us
    dot_general x24, matrix products, product(): return jnp.dot(left, right, preferred_element_type=jnp.float32)  44.3 us
    unnamed x246, local copies, waits for them, and re-layouts  39.1 us
  transfers between devices with their start and end apart: 122, of which 52 were waited for; matrix products, arithmetic and copies ran while one was open for 32% of the time, Pallas kernels for 3%

profile of v1, /device:TPU:0, one launch (start us, length us, event | category | flops | bytes accessed | tf_op | source)
XLA Modules:
  0.0 763.6 jit_solution(6783688204644814227)
XLA Ops:
  48.7 7.0 collective-permute-done.36
  62.1 6.1 collective-permute-done.17
  70.6 4.3 collective-permute-start.4
  75.8 19.7 %collective-permute-done.18 = bf16[256,512]{1,0:T(8,128)(2,1)S(1)} collective-permute-done((bf16[256,512]{1,0:T(8,128)(2,1)S(1)}, bf16[256,512]{1,0:T(8,128)(2,1)S(1)}, u32[]{:S(2)}, u32[]{:S(2)}) %collective-permute-start.18) | collective-permute-done | bytes 262176 | tf_op jit(solution)/shard_map/ppermute | solution.py:295
  95.5 14.0 %collective-permute-start.19 = (bf16[256,512]{1,0:T(8,128)(2,1)S(1)}, bf16[256,512]{1,0:T(8,128)(2,1)S(1)}, u32[]{:S(2)}, u32[]{:S(2)}) collective-permute-start(bf16[256,512]{1,0:T(8,128)(2,1)S(1)} %collective-permute-done.18), channel_id=1, source_target_pairs={{0,24},{8,0},{16,8},{24,16},{1,25},{9,1},{17,9},{25,17},{2,26},{10... | collective-permute-start | bytes 786440 | tf_op jit(solution)/shard_map/ppermute | solution.py:295
  109.7 6.0 collective-permute-done.19
  117.7 4.3 collective-permute-start.5
  125.5 15.1 %collective-permute-done.9 = bf16[256,2048]{1,0:T(8,128)(2,1)S(1)} collective-permute-done((bf16[256,2048]{1,0:T(8,128)(2,1)S(1)}, bf16[256,2048]{1,0:T(8,128)(2,1)S(1)}, u32[]{:S(2)}, u32[]{:S(2)}) %collective-permute-start.9) | collective-permute-done | bytes 1048608 | tf_op jit(solution)/shard_map/ppermute | solution.py:286
  140.5 4.3 collective-permute-start.32
  148.2 5.5 collective-permute-done.64
  153.7 4.3 collective-permute-start.6
  168.6 22.3 %collective-permute-done.6 = bf16[512,512]{0,1:T(8,128)(2,1)S(1)} collective-permute-done((bf16[512,512]{0,1:T(8,128)(2,1)S(1)}, bf16[512,512]{0,1:T(8,128)(2,1)S(1)}, u32[]{:S(2)}, u32[]{:S(2)}) %collective-permute-start.6) | collective-permute-done | bytes 524320 | tf_op jit(solution)/shard_map/ppermute | solution.py:295
  192.3 13.3 %collective-permute-done.39 = bf16[768,512]{1,0:T(8,128)(2,1)} collective-permute-done((bf16[768,512]{1,0:T(8,128)(2,1)S(1)}, bf16[768,512]{1,0:T(8,128)(2,1)}, u32[]{:S(2)}, u32[]{:S(2)}) %collective-permute-start.39) | collective-permute-done | bytes 786464 | tf_op jit(solution)/shard_map/ppermute | solution.py:295
  208.9 4.4 collective-permute-start.40
  223.2 24.2 %attend_forward.1 = (bf16[2048,512]{1,0:T(8,128)(2,1)}, f32[2048,256]{1,0:T(8,128)}, bf16[2048,256]{1,0:T(8,128)(2,1)S(1)}, f32[2048,256]{1,0:T(8,128)}) custom-call(s32[17]{0:T(128)S(1)} %pad_add_fusion.info, f32[512,512]{1,0:T(8,128)S(1)} %fusion.54.refs_0_, f32[512,512]{1,0:T(8,128)S(1)} %fusion.58.refs_1_, f32[512,512]{1,0:T(8,128)S(1)} %fusion.62.refs_2_, ...), custom_call_target="tpu_custom_call" | custom-call | flops 2147483648 | bytes 15728640 | tf_op jit(solution)/shard_map/attend_forward/pallas_call | solution.py:109
  256.6 11.2 %collective-permute-done.23 = bf16[128,2048]{1,0:T(8,128)(2,1)S(1)} collective-permute-done((bf16[128,2048]{1,0:T(8,128)(2,1)S(1)}, bf16[128,2048]{1,0:T(8,128)(2,1)S(1)}, u32[]{:S(2)}, u32[]{:S(2)}) %collective-permute-start.23) | collective-permute-done | bytes 524320 | tf_op jit(solution)/shard_map/ppermute | solution.py:286
  275.9 16.8 %collective-permute-done.24 = bf16[256,2048]{1,0:T(8,128)(2,1)S(1)} collective-permute-done((bf16[256,2048]{1,0:T(8,128)(2,1)S(1)}, bf16[256,2048]{1,0:T(8,128)(2,1)S(1)}, u32[]{:S(2)}, u32[]{:S(2)}) %collective-permute-start.24) | collective-permute-done | bytes 1048608 | tf_op jit(solution)/shard_map/ppermute | solution.py:286
  301.7 11.1 %collective-permute-done.34 = bf16[512,1536]{1,0:T(8,128)(2,1)S(1)} collective-permute-done((bf16[512,1536]{1,0:T(8,128)(2,1)}, bf16[512,1536]{1,0:T(8,128)(2,1)S(1)}, u32[]{:S(2)}, u32[]{:S(2)}) %collective-permute-start.34) | collective-permute-done | bytes 1572896 | tf_op jit(solution)/shard_map/ppermute | solution.py:295
  313.0 7.3 collective-permute-done.46
  337.3 5.1 fusion.86
  342.4 4.4 multiply_convert_fusion.2
  349.7 5.1 fusion.76
  354.8 4.2 multiply_convert_fusion.6
  376.2 4.9 multiply_convert_fusion.4
  381.1 9.8 %maximum_maximum_fusion = bf16[2048,1536]{1,0:T(8,128)(2,1)S(1)} fusion(bf16[512,768]{1,0:T(8,128)(2,1)} %get-tuple-element.111, bf16[512,768]{1,0:T(8,128)(2,1)} %get-tuple-element.110, bf16[512,768]{1,0:T(8,128)(2,1)S(1)} %copy-done.61, bf16[512,768]{1,0:T(8,128)(2,1)S(1)} %copy-done.59, bf16[512,768]{1,0:T(8,128)(2,1)} %copy-done.64, ...), kind=kLoop, calls=%fused_computation | loop fusion | flops 50331648 | bytes 12582912 | tf_op jit(solution)/shard_map/concatenate | solution.py:494
  392.1 6.4 convolution_convert_fusion
  398.5 4.4 fusion.140
  416.9 4.6 convolution_add_fusion.15
  422.8 6.0 collective-permute-done.116
  428.8 5.2 add_convert_fusion.2
  442.7 8.8 %collective-permute-done.71 = bf16[128,2048]{1,0:T(8,128)(2,1)S(1)} collective-permute-done((bf16[128,2048]{1,0:T(8,128)(2,1)S(1)}, bf16[128,2048]{1,0:T(8,128)(2,1)S(1)}, u32[]{:S(2)}, u32[]{:S(2)}) %collective-permute-start.71) | collective-permute-done | bytes 524320 | tf_op jit(solution)/shard_map/ppermute | solution.py:286
  451.9 5.5 collective-permute-done.50
  458.6 7.6 collective-permute-done.67
  467.9 10.6 %collective-permute-done.117 = bf16[768,512]{1,0:T(8,128)(2,1)} collective-permute-done((bf16[768,512]{1,0:T(8,128)(2,1)}, bf16[768,512]{1,0:T(8,128)(2,1)}, u32[]{:S(2)}, u32[]{:S(2)}) %collective-permute-start.117) | collective-permute-done | bytes 786464 | tf_op jit(solution)/shard_map/ppermute | solution.py:295
  484.3 6.5 fusion.2
  490.8 10.0 %collective-permute-done.118 = bf16[768,512]{1,0:T(8,128)(2,1)S(1)} collective-permute-done((bf16[768,512]{1,0:T(8,128)(2,1)S(1)}, bf16[768,512]{1,0:T(8,128)(2,1)S(1)}, u32[]{:S(2)}, u32[]{:S(2)}) %collective-permute-start.118) | collective-permute-done | bytes 786464 | tf_op jit(solution)/shard_map/ppermute | solution.py:295
  531.5 12.0 %collective-permute-done.55 = bf16[256,2048]{1,0:T(8,128)(2,1)} collective-permute-done((bf16[256,2048]{1,0:T(8,128)(2,1)}, bf16[256,2048]{1,0:T(8,128)(2,1)}, u32[]{:S(2)}, u32[]{:S(2)}) %collective-permute-start.55) | collective-permute-done | bytes 1048608 | tf_op jit(solution)/shard_map/ppermute | solution.py:286
  549.2 5.0 collective-permute-done.110
  554.2 4.8 fusion.1
  559.0 4.6 collective-permute-start.111
  578.8 15.2 %collective-permute-done.111 = bf16[512,1536]{1,0:T(8,128)(2,1)S(1)} collective-permute-done((bf16[512,1536]{1,0:T(8,128)(2,1)S(1)}, bf16[512,1536]{1,0:T(8,128)(2,1)S(1)}, u32[]{:S(2)}, u32[]{:S(2)}) %collective-permute-start.111) | collective-permute-done | bytes 1572896 | tf_op jit(solution)/shard_map/ppermute | solution.py:295
  603.0 5.9 collective-permute-done.114
  619.4 34.8 %attend_backward.1 = (bf16[2048,512]{1,0:T(8,128)(2,1)}, f32[8,128]{1,0:T(8,128)S(1)}) custom-call(s32[17]{0:T(128)S(1)} %pad_add_fusion.info, f32[512,512]{1,0:T(8,128)S(1)} %fusion.54.refs_0_, f32[512,512]{1,0:T(8,128)S(1)} %fusion.58.refs_1_, f32[512,512]{1,0:T(8,128)S(1)} %fusion.62.refs_2_, f32[512,512]{1,0:T(8,128)} %copy-done.6, ...), custom_call_target="tpu_custom_call" | custom-call | flops 5368709120 | bytes 26214400 | tf_op jit(solution)/shard_map/attend_backward/pallas_call | solution.py:238
  681.4 6.0 collective-permute-done.98
  688.2 7.7 %collective-permute-done.90 = bf16[512,512]{0,1:T(8,128)(2,1)S(1)} collective-permute-done((bf16[512,512]{0,1:T(8,128)(2,1)S(1)}, bf16[512,512]{0,1:T(8,128)(2,1)S(1)}, u32[]{:S(2)}, u32[]{:S(2)}) %collective-permute-start.90) | collective-permute-done | bytes 524320 | tf_op jit(solution)/shard_map/ppermute | solution.py:295
  703.7 6.7 collective-permute-done.84
  722.3 13.7 %collective-permute-done.85 = bf16[256,2048]{1,0:T(8,128)(2,1)S(1)} collective-permute-done((bf16[256,2048]{1,0:T(8,128)(2,1)S(1)}, bf16[256,2048]{1,0:T(8,128)(2,1)S(1)}, u32[]{:S(2)}, u32[]{:S(2)}) %collective-permute-start.85) | collective-permute-done | bytes 1048608 | tf_op jit(solution)/shard_map/ppermute | solution.py:286
  741.1 4.5 collective-permute-done.92
  (654 shorter events, 328.6 us)
Async XLA Ops:
  2.3 33.5 %collective-permute-start.15 = (bf16[256,128]{1,0:T(8,128)(2,1)}, bf16[256,128]{1,0:T(8,128)(2,1)S(1)}, u32[]{:S(2)}, u32[]{:S(2)}) collective-permute-start(bf16[256,128]{1,0:T(8,128)(2,1)} %get-tuple-element.191), channel_id=1, source_target_pairs={{0,4},{2,6},{4,0},{6,2},{1,5},{3,7},{5,1},{7,3},{8,12},{10,14},{12... | collective-permute-start | bytes 196616 | tf_op jit(solution)/shard_map/ppermute | solution.py:286
  5.3 30.5 %collective-permute-start.14 = (bf16[256,128]{1,0:T(8,128)(2,1)}, bf16[256,128]{1,0:T(8,128)(2,1)}, u32[]{:S(2)}, u32[]{:S(2)}) collective-permute-start(bf16[256,128]{1,0:T(8,128)(2,1)} %get-tuple-element.192), channel_id=1, source_target_pairs={{0,6},{2,4},{4,2},{6,0},{1,7},{3,5},{5,3},{7,1},{8,14},{10,12},{12... | collective-permute-start | bytes 196616 | tf_op jit(solution)/shard_map/ppermute | solution.py:286
  6.7 31.1 %collective-permute-start.16 = (bf16[256,128]{1,0:T(8,128)(2,1)}, bf16[256,128]{1,0:T(8,128)(2,1)}, u32[]{:S(2)}, u32[]{:S(2)}) collective-permute-start(bf16[256,128]{1,0:T(8,128)(2,1)} %get-tuple-element.193), channel_id=1, source_target_pairs={{0,2},{2,0},{4,6},{6,4},{1,3},{3,1},{5,7},{7,5},{8,10},{10,8},{12,... | collective-permute-start | bytes 196616 | tf_op jit(solution)/shard_map/ppermute | solution.py:286
  12.9 28.4 %collective-permute-start.1 = (bf16[128,512]{0,1:T(8,128)(2,1)}, bf16[128,512]{0,1:T(8,128)(2,1)S(1)}, u32[]{:S(2)}, u32[]{:S(2)}) collective-permute-start(bf16[128,512]{0,1:T(8,128)(2,1)} %pad_maximum_fusion.36), channel_id=1, source_target_pairs={{0,6},{2,4},{4,2},{6,0},{1,7},{3,5},{5,3},{7,1},{8,14},{10,12},{12... | collective-permute-start | bytes 393224 | tf_op jit(solution)/shard_map/ppermute | solution.py:286
  16.4 25.0 %collective-permute-start.3 = (bf16[128,512]{0,1:T(8,128)(2,1)}, bf16[128,512]{0,1:T(8,128)(2,1)S(1)}, u32[]{:S(2)}, u32[]{:S(2)}) collective-permute-start(bf16[128,512]{0,1:T(8,128)(2,1)} %pad_maximum_fusion.38), channel_id=1, source_target_pairs={{0,2},{2,0},{4,6},{6,4},{1,3},{3,1},{5,7},{7,5},{8,10},{10,8},{12,... | collective-permute-start | bytes 393224 | tf_op jit(solution)/shard_map/ppermute | solution.py:286
  41.5 29.1 %collective-permute-start.29 = (bf16[128,1536]{1,0:T(8,128)(2,1)S(1)}, bf16[128,1536]{1,0:T(8,128)(2,1)S(1)}, u32[]{:S(2)}, u32[]{:S(2)}) collective-permute-start(bf16[128,1536]{1,0:T(8,128)(2,1)S(1)} %pad_maximum_fusion.30), channel_id=1, source_target_pairs={{0,6},{2,4},{4,2},{6,0},{1,7},{3,5},{5,3},{7,1},{8,14},{10,12},{12... | collective-permute-start | bytes 1179656 | tf_op jit(solution)/shard_map/ppermute | solution.py:286
  45.6 29.4 %collective-permute-start.31 = (bf16[128,1536]{1,0:T(8,128)(2,1)S(1)}, bf16[128,1536]{1,0:T(8,128)(2,1)S(1)}, u32[]{:S(2)}, u32[]{:S(2)}) collective-permute-start(bf16[128,1536]{1,0:T(8,128)(2,1)S(1)} %pad_maximum_fusion.32), channel_id=1, source_target_pairs={{0,2},{2,0},{4,6},{6,4},{1,3},{3,1},{5,7},{7,5},{8,10},{10,8},{12,... | collective-permute-start | bytes 1179656 | tf_op jit(solution)/shard_map/ppermute | solution.py:286
  55.8 60.7 %collective-permute-start.63 = (bf16[256,2048]{1,0:T(8,128)(2,1)S(1)}, bf16[256,2048]{1,0:T(8,128)(2,1)S(1)}, u32[]{:S(2)}, u32[]{:S(2)}) collective-permute-start(bf16[256,2048]{1,0:T(8,128)(2,1)S(1)} %get-tuple-element.65), channel_id=1, source_target_pairs={{0,4},{2,6},{4,0},{6,2},{1,5},{3,7},{5,1},{7,3},{8,12},{10,14},{12... | collective-permute-start | bytes 3145736 | tf_op jit(solution)/shard_map/ppermute | solution.py:286
  68.2 55.0 %collective-permute-start.59 = (bf16[256,2048]{1,0:T(8,128)(2,1)S(1)}, bf16[256,2048]{1,0:T(8,128)(2,1)S(1)}, u32[]{:S(2)}, u32[]{:S(2)}) collective-permute-start(bf16[256,2048]{1,0:T(8,128)(2,1)S(1)} %get-tuple-element.65), channel_id=1, source_target_pairs={{0,2},{2,0},{4,6},{6,4},{1,3},{3,1},{5,7},{7,5},{8,10},{10,8},{12,... | collective-permute-start | bytes 3145736 | tf_op jit(solution)/shard_map/ppermute | solution.py:286
  75.0 41.3 %collective-permute-start.38 = (bf16[768,512]{1,0:T(8,128)(2,1)S(1)}, bf16[768,512]{1,0:T(8,128)(2,1)S(1)}, u32[]{:S(2)}, u32[]{:S(2)}) collective-permute-start(bf16[768,512]{1,0:T(8,128)(2,1)S(1)} %pad_maximum_fusion.26), channel_id=1, source_target_pairs={{0,24},{8,0},{16,8},{24,16},{1,25},{9,1},{17,9},{25,17},{2,26},{10... | collective-permute-start | bytes 2359304 | tf_op jit(solution)/shard_map/ppermute | solution.py:295
  116.3 28.5 %collective-permute-start = (bf16[256,2048]{1,0:T(8,128)(2,1)S(1)}, bf16[256,2048]{1,0:T(8,128)(2,1)S(1)}, u32[]{:S(2)}, u32[]{:S(2)}) collective-permute-start(bf16[256,2048]{1,0:T(8,128)(2,1)S(1)} %get-tuple-element.71), channel_id=1, source_target_pairs={{0,1},{1,0},{2,3},{3,2},{4,5},{5,4},{6,7},{7,6},{8,9},{9,8},{10,11... | collective-permute-start | bytes 3145736 | tf_op jit(solution)/shard_map/ppermute | solution.py:290
  116.5 29.1 %collective-permute-start.7 = (bf16[256,2048]{1,0:T(8,128)(2,1)S(1)}, bf16[256,2048]{1,0:T(8,128)(2,1)S(1)}, u32[]{:S(2)}, u32[]{:S(2)}) collective-permute-start(bf16[256,2048]{1,0:T(8,128)(2,1)S(1)} %get-tuple-element.71), channel_id=1, source_target_pairs={{0,2},{2,0},{4,6},{6,4},{1,3},{3,1},{5,7},{7,5},{8,10},{10,8},{12,... | collective-permute-start | bytes 3145736 | tf_op jit(solution)/shard_map/ppermute | solution.py:286
  117.7 28.9 %collective-permute-start.5 = (bf16[512,512]{0,1:T(8,128)(2,1)S(1)}, bf16[512,512]{0,1:T(8,128)(2,1)S(1)}, u32[]{:S(2)}, u32[]{:S(2)}) collective-permute-start(bf16[512,512]{0,1:T(8,128)(2,1)S(1)} %collective-permute-done.4), channel_id=1, source_target_pairs={{0,24},{8,0},{16,8},{24,16},{1,25},{9,1},{17,9},{25,17},{2,26},{10... | collective-permute-start | bytes 1572872 | tf_op jit(solution)/shard_map/ppermute | solution.py:295
  123.2 30.6 %collective-permute-start.64 = (bf16[128,2048]{1,0:T(8,128)(2,1)S(1)}, bf16[128,2048]{1,0:T(8,128)(2,1)S(1)}, u32[]{:S(2)}, u32[]{:S(2)}) collective-permute-start(bf16[128,2048]{1,0:T(8,128)(2,1)S(1)} %slice.521), channel_id=1, source_target_pairs={{0,2},{2,0},{4,6},{6,4},{1,3},{3,1},{5,7},{7,5},{8,10},{10,8},{12,... | collective-permute-start | bytes 1572872 | tf_op jit(solution)/shard_map/ppermute | solution.py:286
  140.5 66.3 %collective-permute-start.32 = (bf16[512,1536]{1,0:T(8,128)(2,1)S(1)}, bf16[512,1536]{1,0:T(8,128)(2,1)}, u32[]{:S(2)}, u32[]{:S(2)}) collective-permute-start(bf16[512,1536]{1,0:T(8,128)(2,1)S(1)} %pad_maximum_fusion.3), channel_id=1, source_target_pairs={{0,24},{8,0},{16,8},{24,16},{1,25},{9,1},{17,9},{25,17},{2,26},{10... | collective-permute-start | bytes 4718600 | tf_op jit(solution)/shard_map/ppermute | solution.py:295
  153.7 37.2 %collective-permute-start.6 = (bf16[512,512]{0,1:T(8,128)(2,1)S(1)}, bf16[512,512]{0,1:T(8,128)(2,1)S(1)}, u32[]{:S(2)}, u32[]{:S(2)}) collective-permute-start(bf16[512,512]{0,1:T(8,128)(2,1)S(1)} %collective-permute-done.5), channel_id=1, source_target_pairs={{0,24},{8,0},{16,8},{24,16},{1,25},{9,1},{17,9},{25,17},{2,26},{10... | collective-permute-start | bytes 1572872 | tf_op jit(solution)/shard_map/ppermute | solution.py:295
  159.7 45.9 %collective-permute-start.39 = (bf16[768,512]{1,0:T(8,128)(2,1)S(1)}, bf16[768,512]{1,0:T(8,128)(2,1)}, u32[]{:S(2)}, u32[]{:S(2)}) collective-permute-start(bf16[768,512]{1,0:T(8,128)(2,1)S(1)} %collective-permute-done.38), channel_id=1, source_target_pairs={{0,24},{8,0},{16,8},{24,16},{1,25},{9,1},{17,9},{25,17},{2,26},{10... | collective-permute-start | bytes 2359304 | tf_op jit(solution)/shard_map/ppermute | solution.py:295
  164.6 51.8 %collective-permute-start.69 = (bf16[256,2048]{1,0:T(8,128)(2,1)S(1)}, bf16[256,2048]{1,0:T(8,128)(2,1)S(1)}, u32[]{:S(2)}, u32[]{:S(2)}) collective-permute-start(bf16[256,2048]{1,0:T(8,128)(2,1)S(1)} %collective-permute-done.63), channel_id=1, source_target_pairs={{0,1},{1,0},{2,3},{3,2},{4,5},{5,4},{6,7},{7,6},{8,9},{9,8},{10,11... | collective-permute-start | bytes 3145736 | tf_op jit(solution)/shard_map/ppermute | solution.py:290
  168.4 40.5 %collective-permute-start.60 = (bf16[256,2048]{1,0:T(8,128)(2,1)S(1)}, bf16[256,2048]{1,0:T(8,128)(2,1)S(1)}, u32[]{:S(2)}, u32[]{:S(2)}) collective-permute-start(bf16[256,2048]{1,0:T(8,128)(2,1)S(1)} %collective-permute-done.59), channel_id=1, source_target_pairs={{0,1},{1,0},{2,3},{3,2},{4,5},{5,4},{6,7},{7,6},{8,9},{9,8},{10,11... | collective-permute-start | bytes 3145736 | tf_op jit(solution)/shard_map/ppermute | solution.py:290
  208.9 65.2 %collective-permute-start.40 = (bf16[768,512]{1,0:T(8,128)(2,1)}, bf16[768,512]{1,0:T(8,128)(2,1)}, u32[]{:S(2)}, u32[]{:S(2)}) collective-permute-start(bf16[768,512]{1,0:T(8,128)(2,1)} %collective-permute-done.39), channel_id=1, source_target_pairs={{0,24},{8,0},{16,8},{24,16},{1,25},{9,1},{17,9},{25,17},{2,26},{10... | collective-permute-start | bytes 2359304 | tf_op jit(solution)/shard_map/ppermute | solution.py:295
  215.5 59.9 %collective-permute-start.33 = (bf16[512,1536]{1,0:T(8,128)(2,1)}, bf16[512,1536]{1,0:T(8,128)(2,1)}, u32[]{:S(2)}, u32[]{:S(2)}) collective-permute-start(bf16[512,1536]{1,0:T(8,128)(2,1)} %collective-permute-done.32), channel_id=1, source_target_pairs={{0,24},{8,0},{16,8},{24,16},{1,25},{9,1},{17,9},{25,17},{2,26},{10... | collective-permute-start | bytes 4718600 | tf_op jit(solution)/shard_map/ppermute | solution.py:295
  249.3 26.6 %collective-permute-start.20 = (bf16[256,2048]{1,0:T(8,128)(2,1)S(1)}, bf16[256,2048]{1,0:T(8,128)(2,1)S(1)}, u32[]{:S(2)}, u32[]{:S(2)}) collective-permute-start(bf16[256,2048]{1,0:T(8,128)(2,1)S(1)} %convolution_convert_fusion.12), channel_id=1, source_target_pairs={{0,1},{1,0},{2,3},{3,2},{4,5},{5,4},{6,7},{7,6},{8,9},{9,8},{10,11... | collective-permute-start | bytes 3145736 | tf_op jit(solution)/shard_map/ppermute | solution.py:290
  275.4 37.5 %collective-permute-start.34 = (bf16[512,1536]{1,0:T(8,128)(2,1)}, bf16[512,1536]{1,0:T(8,128)(2,1)S(1)}, u32[]{:S(2)}, u32[]{:S(2)}) collective-permute-start(bf16[512,1536]{1,0:T(8,128)(2,1)} %collective-permute-done.33), channel_id=1, source_target_pairs={{0,24},{8,0},{16,8},{24,16},{1,25},{9,1},{17,9},{25,17},{2,26},{10... | collective-permute-start | bytes 4718600 | tf_op jit(solution)/shard_map/ppermute | solution.py:295
  298.0 25.3 %collective-permute-start.28 = (bf16[256,2048]{1,0:T(8,128)(2,1)S(1)}, bf16[256,2048]{1,0:T(8,128)(2,1)S(1)}, u32[]{:S(2)}, u32[]{:S(2)}) collective-permute-start(bf16[256,2048]{1,0:T(8,128)(2,1)S(1)} %get-tuple-element.67), channel_id=1, source_target_pairs={{0,1},{1,0},{2,3},{3,2},{4,5},{5,4},{6,7},{7,6},{8,9},{9,8},{10,11... | collective-permute-start | bytes 3145736 | tf_op jit(solution)/shard_map/ppermute | solution.py:290
  332.0 185.4 %collective-permute-start.58 = (bf16[256,2048]{1,0:T(8,128)(2,1)}, bf16[256,2048]{1,0:T(8,128)(2,1)}, u32[]{:S(2)}, u32[]{:S(2)}) collective-permute-start(bf16[256,2048]{1,0:T(8,128)(2,1)} %convolution_convert_fusion.8), channel_id=1, source_target_pairs={{0,1},{1,0},{2,3},{3,2},{4,5},{5,4},{6,7},{7,6},{8,9},{9,8},{10,11... | collective-permute-start | bytes 3145736 | tf_op jit(solution)/shard_map/ppermute | solution.py:290
  336.7 35.5 %collective-permute-start.48 = (bf16[256,2048]{1,0:T(8,128)(2,1)S(1)}, bf16[256,2048]{1,0:T(8,128)(2,1)S(1)}, u32[]{:S(2)}, u32[]{:S(2)}) collective-permute-start(bf16[256,2048]{1,0:T(8,128)(2,1)S(1)} %pad_maximum_fusion.9), channel_id=1, source_target_pairs={{0,1},{1,0},{2,3},{3,2},{4,5},{5,4},{6,7},{7,6},{8,9},{9,8},{10,11... | collective-permute-start | bytes 3145736 | tf_op jit(solution)/shard_map/ppermute | solution.py:290
  361.0 46.7 %collective-permute-start.44 = (bf16[256,2048]{1,0:T(8,128)(2,1)}, bf16[256,2048]{1,0:T(8,128)(2,1)}, u32[]{:S(2)}, u32[]{:S(2)}) collective-permute-start(bf16[256,2048]{1,0:T(8,128)(2,1)} %convolution_convert_fusion.15), channel_id=1, source_target_pairs={{0,1},{1,0},{2,3},{3,2},{4,5},{5,4},{6,7},{7,6},{8,9},{9,8},{10,11... | collective-permute-start | bytes 3145736 | tf_op jit(solution)/shard_map/ppermute | solution.py:290
  363.9 46.5 %collective-permute-start.61 = (bf16[256,2048]{1,0:T(8,128)(2,1)}, bf16[256,2048]{1,0:T(8,128)(2,1)}, u32[]{:S(2)}, u32[]{:S(2)}) collective-permute-start(bf16[256,2048]{1,0:T(8,128)(2,1)} %convolution_convert_fusion.7), channel_id=1, source_target_pairs={{0,1},{1,0},{2,3},{3,2},{4,5},{5,4},{6,7},{7,6},{8,9},{9,8},{10,11... | collective-permute-start | bytes 3145736 | tf_op jit(solution)/shard_map/ppermute | solution.py:290
  364.4 49.2 %collective-permute-start.53 = (bf16[256,2048]{1,0:T(8,128)(2,1)}, bf16[256,2048]{1,0:T(8,128)(2,1)}, u32[]{:S(2)}, u32[]{:S(2)}) collective-permute-start(bf16[256,2048]{1,0:T(8,128)(2,1)} %convolution_convert_fusion.13), channel_id=1, source_target_pairs={{0,1},{1,0},{2,3},{3,2},{4,5},{5,4},{6,7},{7,6},{8,9},{9,8},{10,11... | collective-permute-start | bytes 3145736 | tf_op jit(solution)/shard_map/ppermute | solution.py:290
  372.2 44.7 %collective-permute-start.70 = (bf16[256,2048]{1,0:T(8,128)(2,1)}, bf16[256,2048]{1,0:T(8,128)(2,1)}, u32[]{:S(2)}, u32[]{:S(2)}) collective-permute-start(bf16[256,2048]{1,0:T(8,128)(2,1)} %convolution_convert_fusion.5), channel_id=1, source_target_pairs={{0,1},{1,0},{2,3},{3,2},{4,5},{5,4},{6,7},{7,6},{8,9},{9,8},{10,11... | collective-permute-start | bytes 3145736 | tf_op jit(solution)/shard_map/ppermute | solution.py:290
  410.4 29.7 %collective-permute-start.49 = (bf16[256,2048]{1,0:T(8,128)(2,1)}, bf16[256,2048]{1,0:T(8,128)(2,1)}, u32[]{:S(2)}, u32[]{:S(2)}) collective-permute-start(bf16[256,2048]{1,0:T(8,128)(2,1)} %convolution_convert_fusion.14), channel_id=1, source_target_pairs={{0,1},{1,0},{2,3},{3,2},{4,5},{5,4},{6,7},{7,6},{8,9},{9,8},{10,11... | collective-permute-start | bytes 3145736 | tf_op jit(solution)/shard_map/ppermute | solution.py:290
  416.9 67.5 %collective-permute-start.109 = (bf16[512,1536]{1,0:T(8,128)(2,1)}, bf16[512,1536]{1,0:T(8,128)(2,1)}, u32[]{:S(2)}, u32[]{:S(2)}) collective-permute-start(bf16[512,1536]{1,0:T(8,128)(2,1)} %convolution_convert_fusion), channel_id=1, source_target_pairs={{0,24},{8,0},{16,8},{24,16},{1,25},{9,1},{17,9},{25,17},{2,26},{10... | collective-permute-start | bytes 4718600 | tf_op jit(solution)/shard_map/ppermute | solution.py:295
  434.0 44.4 %collective-permute-start.117 = (bf16[768,512]{1,0:T(8,128)(2,1)}, bf16[768,512]{1,0:T(8,128)(2,1)}, u32[]{:S(2)}, u32[]{:S(2)}) collective-permute-start(bf16[768,512]{1,0:T(8,128)(2,1)} %add_convert_fusion.2), channel_id=1, source_target_pairs={{0,24},{8,0},{16,8},{24,16},{1,25},{9,1},{17,9},{25,17},{2,26},{10... | collective-permute-start | bytes 2359304 | tf_op jit(solution)/shard_map/ppermute | solution.py:295
  466.1 52.2 %collective-permute-start.72 = (bf16[256,2048]{1,0:T(8,128)(2,1)S(1)}, bf16[256,2048]{1,0:T(8,128)(2,1)S(1)}, u32[]{:S(2)}, u32[]{:S(2)}) collective-permute-start(bf16[256,2048]{1,0:T(8,128)(2,1)S(1)} %pad_maximum_fusion.14), channel_id=1, source_target_pairs={{0,4},{2,6},{4,0},{6,2},{1,5},{3,7},{5,1},{7,3},{8,12},{10,14},{12... | collective-permute-start | bytes 3145736 | tf_op jit(solution)/shard_map/ppermute | solution.py:286
  466.7 55.8 %collective-permute-start.68 = (bf16[256,2048]{1,0:T(8,128)(2,1)S(1)}, bf16[256,2048]{1,0:T(8,128)(2,1)}, u32[]{:S(2)}, u32[]{:S(2)}) collective-permute-start(bf16[256,2048]{1,0:T(8,128)(2,1)S(1)} %pad_maximum_fusion.13), channel_id=1, source_target_pairs={{0,2},{2,0},{4,6},{6,4},{1,3},{3,1},{5,7},{7,5},{8,10},{10,8},{12,... | collective-permute-start | bytes 3145736 | tf_op jit(solution)/shard_map/ppermute | solution.py:286
  517.1 26.4 %collective-permute-start.55 = (bf16[256,2048]{1,0:T(8,128)(2,1)}, bf16[256,2048]{1,0:T(8,128)(2,1)}, u32[]{:S(2)}, u32[]{:S(2)}) collective-permute-start(bf16[256,2048]{1,0:T(8,128)(2,1)} %pad_maximum_fusion.11), channel_id=1, source_target_pairs={{0,4},{2,6},{4,0},{6,2},{1,5},{3,7},{5,1},{7,3},{8,12},{10,14},{12... | collective-permute-start | bytes 3145736 | tf_op jit(solution)/shard_map/ppermute | solution.py:286
  517.3 26.5 %collective-permute-start.51 = (bf16[256,2048]{1,0:T(8,128)(2,1)}, bf16[256,2048]{1,0:T(8,128)(2,1)}, u32[]{:S(2)}, u32[]{:S(2)}) collective-permute-start(bf16[256,2048]{1,0:T(8,128)(2,1)} %pad_maximum_fusion.10), channel_id=1, source_target_pairs={{0,2},{2,0},{4,6},{6,4},{1,3},{3,1},{5,7},{7,5},{8,10},{10,8},{12,... | collective-permute-start | bytes 3145736 | tf_op jit(solution)/shard_map/ppermute | solution.py:286
  518.3 35.8 %collective-permute-start.110 = (bf16[512,1536]{1,0:T(8,128)(2,1)}, bf16[512,1536]{1,0:T(8,128)(2,1)}, u32[]{:S(2)}, u32[]{:S(2)}) collective-permute-start(bf16[512,1536]{1,0:T(8,128)(2,1)} %fusion.2), channel_id=1, source_target_pairs={{0,24},{8,0},{16,8},{24,16},{1,25},{9,1},{17,9},{25,17},{2,26},{10... | collective-permute-start | bytes 4718600 | tf_op jit(solution)/shard_map/ppermute | solution.py:295
  528.4 35.2 %collective-permute-start.76 = (bf16[256,2048]{1,0:T(8,128)(2,1)S(1)}, bf16[256,2048]{1,0:T(8,128)(2,1)S(1)}, u32[]{:S(2)}, u32[]{:S(2)}) collective-permute-start(bf16[256,2048]{1,0:T(8,128)(2,1)S(1)} %get-tuple-element.69), channel_id=1, source_target_pairs={{0,4},{2,6},{4,0},{6,2},{1,5},{3,7},{5,1},{7,3},{8,12},{10,14},{12... | collective-permute-start | bytes 3145736 | tf_op jit(solution)/shard_map/ppermute | solution.py:286
  530.4 34.3 %collective-permute-start.74 = (bf16[256,2048]{1,0:T(8,128)(2,1)S(1)}, bf16[256,2048]{1,0:T(8,128)(2,1)S(1)}, u32[]{:S(2)}, u32[]{:S(2)}) collective-permute-start(bf16[256,2048]{1,0:T(8,128)(2,1)S(1)} %get-tuple-element.69), channel_id=1, source_target_pairs={{0,2},{2,0},{4,6},{6,4},{1,3},{3,1},{5,7},{7,5},{8,10},{10,8},{12,... | collective-permute-start | bytes 3145736 | tf_op jit(solution)/shard_map/ppermute | solution.py:286
  559.0 35.0 %collective-permute-start.111 = (bf16[512,1536]{1,0:T(8,128)(2,1)S(1)}, bf16[512,1536]{1,0:T(8,128)(2,1)S(1)}, u32[]{:S(2)}, u32[]{:S(2)}) collective-permute-start(bf16[512,1536]{1,0:T(8,128)(2,1)S(1)} %fusion.1), channel_id=1, source_target_pairs={{0,24},{8,0},{16,8},{24,16},{1,25},{9,1},{17,9},{25,17},{2,26},{10... | collective-permute-start | bytes 4718600 | tf_op jit(solution)/shard_map/ppermute | solution.py:295
  574.7 43.7 %collective-permute-start.80 = (bf16[256,2048]{1,0:T(8,128)(2,1)S(1)}, bf16[256,2048]{1,0:T(8,128)(2,1)S(1)}, u32[]{:S(2)}, u32[]{:S(2)}) collective-permute-start(bf16[256,2048]{1,0:T(8,128)(2,1)S(1)} %pad_maximum_fusion.15), channel_id=1, source_target_pairs={{0,1},{1,0},{2,3},{3,2},{4,5},{5,4},{6,7},{7,6},{8,9},{9,8},{10,11... | collective-permute-start | bytes 3145736 | tf_op jit(solution)/shard_map/ppermute | solution.py:290
  672.7 26.0 %collective-permute-start.83 = (bf16[256,2048]{1,0:T(8,128)(2,1)S(1)}, bf16[256,2048]{1,0:T(8,128)(2,1)S(1)}, u32[]{:S(2)}, u32[]{:S(2)}) collective-permute-start(bf16[256,2048]{1,0:T(8,128)(2,1)S(1)} %convolution_convert_fusion.2), channel_id=1, source_target_pairs={{0,1},{1,0},{2,3},{3,2},{4,5},{5,4},{6,7},{7,6},{8,9},{9,8},{10,11... | collective-permute-start | bytes 3145736 | tf_op jit(solution)/shard_map/ppermute | solution.py:290
  680.9 40.8 %collective-permute-start.81 = (bf16[256,2048]{1,0:T(8,128)(2,1)S(1)}, bf16[256,2048]{1,0:T(8,128)(2,1)S(1)}, u32[]{:S(2)}, u32[]{:S(2)}) collective-permute-start(bf16[256,2048]{1,0:T(8,128)(2,1)S(1)} %convolution_convert_fusion.4), channel_id=1, source_target_pairs={{0,1},{1,0},{2,3},{3,2},{4,5},{5,4},{6,7},{7,6},{8,9},{9,8},{10,11... | collective-permute-start | bytes 3145736 | tf_op jit(solution)/shard_map/ppermute | solution.py:290
  710.6 25.5 %collective-permute-start.85 = (bf16[256,2048]{1,0:T(8,128)(2,1)S(1)}, bf16[256,2048]{1,0:T(8,128)(2,1)S(1)}, u32[]{:S(2)}, u32[]{:S(2)}) collective-permute-start(bf16[256,2048]{1,0:T(8,128)(2,1)S(1)} %pad_maximum_fusion.16), channel_id=1, source_target_pairs={{0,2},{2,0},{4,6},{6,4},{1,3},{3,1},{5,7},{7,5},{8,10},{10,8},{12,... | collective-permute-start | bytes 3145736 | tf_op jit(solution)/shard_map/ppermute | solution.py:286
  717.4 30.2 %collective-permute-start.102 = (bf16[256,128]{1,0:T(8,128)(2,1)S(1)}, bf16[256,128]{1,0:T(8,128)(2,1)S(1)}, u32[]{:S(2)}, u32[]{:S(2)}) collective-permute-start(bf16[256,128]{1,0:T(8,128)(2,1)S(1)} %get-tuple-element.182), channel_id=1, source_target_pairs={{0,2},{2,0},{4,6},{6,4},{1,3},{3,1},{5,7},{7,5},{8,10},{10,8},{12,... | collective-permute-start | bytes 196616 | tf_op jit(solution)/shard_map/ppermute | solution.py:286
  718.3 30.0 %collective-permute-start.101 = (bf16[256,128]{1,0:T(8,128)(2,1)S(1)}, bf16[256,128]{1,0:T(8,128)(2,1)S(1)}, u32[]{:S(2)}, u32[]{:S(2)}) collective-permute-start(bf16[256,128]{1,0:T(8,128)(2,1)S(1)} %get-tuple-element.183), channel_id=1, source_target_pairs={{0,4},{2,6},{4,0},{6,2},{1,5},{3,7},{5,1},{7,3},{8,12},{10,14},{12... | collective-permute-start | bytes 196616 | tf_op jit(solution)/shard_map/ppermute | solution.py:286
  721.7 28.9 %collective-permute-start.100 = (bf16[256,128]{1,0:T(8,128)(2,1)S(1)}, bf16[256,128]{1,0:T(8,128)(2,1)S(1)}, u32[]{:S(2)}, u32[]{:S(2)}) collective-permute-start(bf16[256,128]{1,0:T(8,128)(2,1)S(1)} %get-tuple-element.184), channel_id=1, source_target_pairs={{0,6},{2,4},{4,2},{6,0},{1,7},{3,5},{5,3},{7,1},{8,14},{10,12},{12... | collective-permute-start | bytes 196616 | tf_op jit(solution)/shard_map/ppermute | solution.py:286
  (176 other events, 2990.9 us)

commit v2 on v1

v2 whole, which is shorter than its diff:
```python
import functools
import math

import jax
import jax.numpy as jnp
from jax import lax
from jax.experimental import pallas as pl
from jax.experimental.pallas import tpu as pltpu
from jax.sharding import PartitionSpec as P

BLK = 128
EPS = 1e-06
THETA = 1000000.0
CTX = 4
LIMIT = 56 * 2**20
TILE = 256


def _dot(a, b, dims):
    return lax.dot_general(a, b, (dims, ((), ())), preferred_element_type=jnp.float32)


def _starts(pieces):
    at, starts = 0, []
    for piece in pieces:
        starts.append(at)
        at += piece.shape[0]
    return starts


def _whole(count):
    return [pl.BlockSpec(memory_space=pltpu.VMEM)] * count


def _forward_kernel(heads, scale, info, *refs):
    pieces = refs[:-13]
    (weight_ref, cos_ref, sin_ref, qg_ref, kg_ref, proj_ref, low_ref, mixed_ref, mlow_ref, rtot_ref, q_s, k_s, v_s) = refs[
        -13:
    ]
    hd = cos_ref.shape[1]
    rows = cos_ref.shape[0]
    cols = proj_ref.shape[1]
    factor = scale * math.log2(math.e)

    for piece, start in zip(pieces, _starts(pieces)):
        proj_ref[start : start + piece.shape[0], :] = _dot(
            piece[...], weight_ref[:, :cols], ((1,), (0,))
        )

    @pl.loop(0, rows // BLK)
    def _(block):
        here = pl.ds(pl.multiple_of(block * BLK, BLK), BLK)
        cosine = cos_ref[here, :]
        sine = sin_ref[here, :]
        for h in range(heads + 1):
            u = proj_ref[here, h * hd : (h + 1) * hd]
            gain = qg_ref[...] if h < heads else kg_ref[...]
            n = u * lax.rsqrt(jnp.mean(u * u, axis=1, keepdims=True) + EPS) * gain
            o = (n * cosine + pltpu.roll(n, hd // 2, 1) * sine).astype(jnp.bfloat16)
            low_ref[here, h * hd : (h + 1) * hd] = o
            if h < heads:
                q_s[h, here, :] = o
            else:
                k_s[here, :] = o
        val = proj_ref[here, (heads + 1) * hd :].astype(jnp.bfloat16)
        low_ref[here, (heads + 1) * hd :] = val
        v_s[here, :] = val

    length = info[rows // BLK]
    per = TILE // BLK

    def gather(ref, tile, *lead):
        parts = [
            ref[lead + (pl.ds(pl.multiple_of(info[tile * per + b] * BLK, BLK), BLK), slice(None))]
            for b in range(per)
        ]
        return jnp.concatenate(parts, axis=0)

    @pl.loop(0, rows // TILE)
    def _(i):
        query = jnp.concatenate([gather(q_s, i, h) for h in range(heads)], axis=0)
        full = jnp.minimum(i, length // TILE)

        def scores(j):
            return jnp.exp2(_dot(query, gather(k_s, j), ((1,), (1,))) * factor)

        def take(expo, j, acc, tot):
            part = expo[:, :hd]
            for b in range(1, TILE // hd):
                part = part + expo[:, b * hd : (b + 1) * hd]
            acc = acc + _dot(expo.astype(jnp.bfloat16), gather(v_s, j), ((1,), (0,)))
            return acc, tot + part

        def step(j, carry):
            return take(scores(j), j, *carry)

        zero = jnp.zeros((heads * TILE, hd), jnp.float32)
        acc, tot = lax.fori_loop(0, full, step, (zero, zero))
        expo = scores(full)
        qpos = i * TILE + lax.rem(lax.broadcasted_iota(jnp.int32, expo.shape, 0), TILE)
        kpos = full * TILE + lax.broadcasted_iota(jnp.int32, expo.shape, 1)
        expo = jnp.where((kpos <= qpos) & (kpos < length), expo, 0.0)
        acc, tot = take(expo, full, acc, tot)
        recip = 1.0 / jnp.sum(tot, axis=1, keepdims=True)
        mixed = acc * recip
        recip = jnp.broadcast_to(recip, mixed.shape)
        for h in range(heads):
            for b in range(per):
                at = pl.ds(pl.multiple_of(info[i * per + b] * BLK, BLK), BLK)
                cut = slice(h * TILE + b * BLK, h * TILE + (b + 1) * BLK)
                lanes = slice(h * hd, (h + 1) * hd)
                mixed_ref[at, lanes] = mixed[cut]
                mlow_ref[at, lanes] = mixed[cut].astype(jnp.bfloat16)
                rtot_ref[at, lanes] = recip[cut]


def attend_forward(info, pieces, weight, cosine, sine, query_gain, key_gain, heads):
    rows, hd = cosine.shape
    cols = (heads + 2) * hd
    width = heads * hd
    pairs = rows * rows // 2 * heads
    return pl.pallas_call(
        functools.partial(_forward_kernel, heads, hd**-0.5),
        out_shape=(
            jax.ShapeDtypeStruct((rows, cols), jnp.float32),
            jax.ShapeDtypeStruct((rows, cols), jnp.bfloat16),
            jax.ShapeDtypeStruct((rows, width), jnp.float32),
            jax.ShapeDtypeStruct((rows, width), jnp.bfloat16),
            jax.ShapeDtypeStruct((rows, width), jnp.float32),
        ),
        in_specs=[pl.BlockSpec(memory_space=pltpu.SMEM)] + _whole(len(pieces) + 5),
        out_specs=_whole(5),
        scratch_shapes=[
            pltpu.VMEM((heads, rows, hd), jnp.bfloat16),
            pltpu.VMEM((rows, hd), jnp.bfloat16),
            pltpu.VMEM((rows, hd), jnp.bfloat16),
        ],
        compiler_params=pltpu.CompilerParams(vmem_limit_bytes=LIMIT),
        cost_estimate=pl.CostEstimate(
            flops=pairs * hd * 4 + 2 * rows * cols * weight.shape[0],
            bytes_accessed=rows * hd * 100,
            transcendentals=pairs,
        ),
        name="attend_forward",
    )(info, *pieces, weight, cosine, sine, query_gain, key_gain)


def _backward_kernel(heads, scale, info, *refs):
    pieces = refs[:-15]
    (weight_ref, proj_ref, low_ref, mixed_ref, rtot_ref, cos_ref, sin_ref, qg_ref, kg_ref, out_ref, gain_ref, gacc_s, dq_s, dk_s, dv_s) = refs[
        -15:
    ]
    hd = cos_ref.shape[1]
    rows = cos_ref.shape[0]
    factor = scale * math.log2(math.e)
    length = info[rows // BLK]
    per = TILE // BLK
    cols = (heads + 2) * hd

    dk_s[...] = jnp.zeros_like(dk_s)
    dv_s[...] = jnp.zeros_like(dv_s)
    gain_ref[...] = jnp.zeros_like(gain_ref)

    for piece, start in zip(pieces, _starts(pieces)):
        grad = _dot(piece[...], weight_ref[:, cols:], ((1,), (0,)))
        at = slice(start, start + piece.shape[0])
        for h in range(heads):
            lanes = slice(h * hd, (h + 1) * hd)
            g = grad[:, lanes] * rtot_ref[at, lanes]
            gacc_s[h, at, :] = g.astype(jnp.bfloat16)
            dq_s[h, at, :] = g * mixed_ref[at, lanes]

    def spots(tile):
        return [pl.ds(pl.multiple_of(info[tile * per + b] * BLK, BLK), BLK) for b in range(per)]

    @pl.loop(0, pl.cdiv(length, TILE))
    def _(i):
        at = spots(i)
        query = jnp.concatenate(
            [low_ref[s, h * hd : (h + 1) * hd] for h in range(heads) for s in at], axis=0
        )
        gacc = jnp.concatenate([gacc_s[h, s, :] for h in range(heads) for s in at], axis=0)
        terms = jnp.concatenate([dq_s[h, s, :] for h in range(heads) for s in at], axis=0)
        shift = jnp.sum(terms.T, axis=0, keepdims=True)

        def tile(j, dq, masked):
            spot = spots(j)
            key = jnp.concatenate([low_ref[s, heads * hd : (heads + 1) * hd] for s in spot], axis=0)
            val = jnp.concatenate([low_ref[s, (heads + 1) * hd :] for s in spot], axis=0)
            expo = jnp.exp2(_dot(key, query, ((1,), (1,))) * factor)
            if masked:
                kpos = j * TILE + lax.broadcasted_iota(jnp.int32, expo.shape, 0)
                qpos = i * TILE + lax.rem(lax.broadcasted_iota(jnp.int32, expo.shape, 1), TILE)
                expo = jnp.where((kpos <= qpos) & (kpos < length), expo, 0.0)
            probs = _dot(val, gacc, ((1,), (1,)))
            ds = (expo * (probs - shift)).astype(jnp.bfloat16)
            dv = _dot(expo.astype(jnp.bfloat16), gacc, ((1,), (0,)))
            dk = _dot(ds, query, ((1,), (0,)))
            for b, s in enumerate(spot):
                dv_s[s, :] += dv[b * BLK : (b + 1) * BLK]
                dk_s[s, :] += dk[b * BLK : (b + 1) * BLK]
            return dq + _dot(ds, key, ((0,), (0,)))

        zero = jnp.zeros((heads * TILE, hd), jnp.float32)
        dq = lax.fori_loop(0, i, lambda j, dq: tile(j, dq, False), zero)
        dq = tile(i, dq, True) * scale
        for h in range(heads):
            for b, s in enumerate(at):
                dq_s[h, s, :] = dq[h * TILE + b * BLK : h * TILE + (b + 1) * BLK]

    def finish(block):
        at = pl.ds(pl.multiple_of(block * BLK, BLK), BLK)
        cosine = cos_ref[at, :]
        sine = sin_ref[at, :]
        for h in range(heads + 1):
            lanes = slice(h * hd, (h + 1) * hd)
            u = proj_ref[at, lanes]
            r = lax.rsqrt(jnp.mean(u * u, axis=1, keepdims=True) + EPS)
            d = dq_s[h, at, :] if h < heads else dk_s[at, :] * scale
            dn = d * cosine - pltpu.roll(d, hd // 2, 1) * sine
            gain = qg_ref[...] if h < heads else kg_ref[...]
            hat = u * r
            row = 0 if h < heads else 1
            gain_ref[row : row + 1, :] += jnp.sum(dn * hat, axis=0, keepdims=True)
            dg = dn * gain
            du = r * (dg - hat * jnp.mean(dg * hat, axis=1, keepdims=True))
            out_ref[at, lanes] = du.astype(jnp.bfloat16)
        out_ref[at, (heads + 1) * hd :] = dv_s[at, :].astype(jnp.bfloat16)

    for b in range(rows // BLK):

        @pl.when(b * BLK >= pl.cdiv(length, TILE) * TILE)
        def _(b=b):
            at = pl.ds(pl.multiple_of(info[b] * BLK, BLK), BLK)
            for h in range(heads):
                dq_s[h, at, :] = jnp.zeros((BLK, hd), jnp.float32)

    @pl.loop(0, rows // BLK)
    def _(block):
        finish(block)


def attend_backward(
    info, pieces, weight, proj, low, mixed, rtot, cosine, sine, query_gain, key_gain, heads
):
    rows, hd = cosine.shape
    pairs = rows * rows // 2 * heads
    return pl.pallas_call(
        functools.partial(_backward_kernel, heads, hd**-0.5),
        out_shape=(
            jax.ShapeDtypeStruct((rows, (heads + 2) * hd), jnp.bfloat16),
            jax.ShapeDtypeStruct((8, hd), jnp.float32),
        ),
        in_specs=[pl.BlockSpec(memory_space=pltpu.SMEM)] + _whole(len(pieces) + 9),
        out_specs=_whole(2),
        scratch_shapes=[
            pltpu.VMEM((heads, rows, hd), jnp.bfloat16),
            pltpu.VMEM((heads, rows, hd), jnp.float32),
            pltpu.VMEM((rows, hd), jnp.float32),
            pltpu.VMEM((rows, hd), jnp.float32),
        ],
        compiler_params=pltpu.CompilerParams(vmem_limit_bytes=LIMIT),
        cost_estimate=pl.CostEstimate(
            flops=pairs * hd * 10 + 2 * rows * heads * hd * weight.shape[0],
            bytes_accessed=rows * hd * 140,
            transcendentals=pairs,
        ),
        name="attend_backward",
    )(info, *pieces, weight, proj, low, mixed, rtot, cosine, sine, query_gain, key_gain)


def _expand_kernel(counts, *refs):
    groups = []
    for count in counts:
        groups.append(refs[:count])
        refs = refs[count:]
    gate_w, up_w = refs[:2]
    slope_ref, silu_ref, inner_ref = refs[-3:]
    for row, pieces in enumerate(groups):

        @pl.when(pl.program_id(0) == row)
        def _(pieces=pieces):
            for piece, start in zip(pieces, _starts(pieces)):
                at = slice(start, start + piece.shape[0])
                gate = _dot(piece[...], gate_w[...], ((1,), (0,)))
                upper = _dot(piece[...], up_w[...], ((1,), (0,)))
                sigma = 1.0 / (1.0 + jnp.exp(-gate))
                silu = gate * sigma
                slope_ref[at, :] = upper * sigma * (1.0 + gate - silu)
                silu_ref[at, :] = silu
                inner_ref[at, :] = (silu * upper).astype(jnp.bfloat16)


def feed_expand(groups, first, weight, rows, filled=(), step=256):
    size = sum(p.shape[0] for p in groups[0])
    width, units = weight.shape[0], weight.shape[1] // 2
    steps = units // step
    pieces = [p for group in groups for p in group]
    tile = pl.BlockSpec((size, step), lambda r, n: (r + first, n))
    done = size * len(groups)
    return pl.pallas_call(
        functools.partial(_expand_kernel, [len(group) for group in groups]),
        grid=(len(groups), steps),
        out_shape=(
            jax.ShapeDtypeStruct((rows, units), jnp.float32),
            jax.ShapeDtypeStruct((rows, units), jnp.float32),
            jax.ShapeDtypeStruct((rows, units), jnp.bfloat16),
        ),
        in_specs=[
            pl.BlockSpec(p.shape, lambda r, n: (0, 0), pipeline_mode=pl.Buffered(1)) for p in pieces
        ]
        + [
            pl.BlockSpec((width, step), lambda r, n: (0, n)),
            pl.BlockSpec((width, step), lambda r, n: (0, n + steps)),
        ]
        + [pl.BlockSpec(memory_space=pl.ANY)] * len(filled),
        out_specs=(tile, tile, tile),
        input_output_aliases={len(pieces) + 2 + i: i for i in range(len(filled))},
        compiler_params=pltpu.CompilerParams(vmem_limit_bytes=LIMIT),
        cost_estimate=pl.CostEstimate(
            flops=4 * done * width * units,
            bytes_accessed=done * width * 2 + width * units * 4 + done * units * 10,
            transcendentals=done * units,
        ),
        name="feed_expand",
    )(*pieces, weight, weight, *filled)


def _shrink_kernel(count, *refs):
    pieces = refs[:count]
    weight, slope_ref, silu_ref, dgate_ref, dup_ref = refs[count:]
    for piece, start in zip(pieces, _starts(pieces)):
        at = slice(start, start + piece.shape[0])
        grad = _dot(piece[...], weight[...], ((1,), (0,)))
        dgate_ref[at, :] = (grad * slope_ref[at, :]).astype(jnp.bfloat16)
        dup_ref[at, :] = (grad * silu_ref[at, :]).astype(jnp.bfloat16)


def feed_back(pieces, weight, slope, silu, step=256):
    rows = sum(p.shape[0] for p in pieces)
    width, units = weight.shape
    tile = pl.BlockSpec((rows, step), lambda n: (0, n))
    return pl.pallas_call(
        functools.partial(_shrink_kernel, len(pieces)),
        grid=(units // step,),
        out_shape=(jax.ShapeDtypeStruct((rows, units), jnp.bfloat16),) * 2,
        in_specs=[pl.BlockSpec(p.shape, lambda n: (0, 0), pipeline_mode=pl.Buffered(1)) for p in pieces]
        + [pl.BlockSpec((width, step), lambda n: (0, n)), tile, tile],
        out_specs=(tile, tile),
        compiler_params=pltpu.CompilerParams(vmem_limit_bytes=LIMIT),
        cost_estimate=pl.CostEstimate(
            flops=2 * rows * width * units,
            bytes_accessed=rows * width * 2 + width * units * 2 + rows * units * 12,
            transcendentals=0,
        ),
        name="feed_back",
    )(*pieces, weight, slope, silu)


def _terms_kernel(groups, *refs):
    out_ref, hold_s = refs[-2:]
    refs = refs[:-2]
    column = 0
    for count, sides in groups:
        pieces, others, refs = refs[:count], refs[count : count + sides], refs[count + sides :]
        for piece, start in zip(pieces, _starts(pieces)):
            hold_s[start : start + piece.shape[0], :] = piece[...]
        for other in others:
            size = other.shape[1]
            out_ref[:, column : column + size] = _dot(
                hold_s[...], other[...], ((0,), (0,))
            ).astype(jnp.bfloat16)
            column += size


def weight_terms(groups, step=256):
    width = groups[0][0][0].shape[1]
    rows = groups[0][1][0].shape[0]
    specs, values = [], []
    for pieces, others in groups:
        specs += [pl.BlockSpec((p.shape[0], step), lambda n: (0, n)) for p in pieces]
        specs += [pl.BlockSpec(o.shape, lambda n: (0, 0), pipeline_mode=pl.Buffered(1)) for o in others]
        values += list(pieces) + list(others)
    total = sum(o.shape[1] for _, others in groups for o in others)
    return pl.pallas_call(
        functools.partial(_terms_kernel, [(len(p), len(o)) for p, o in groups]),
        grid=(width // step,),
        out_shape=jax.ShapeDtypeStruct((width, total), jnp.bfloat16),
        in_specs=specs,
        out_specs=pl.BlockSpec((step, total), lambda n: (n, 0)),
        scratch_shapes=[pltpu.VMEM((rows, step), jnp.bfloat16)],
        compiler_params=pltpu.CompilerParams(vmem_limit_bytes=LIMIT),
        cost_estimate=pl.CostEstimate(
            flops=2 * rows * width * total,
            bytes_accessed=sum(v.size * 2 for v in values) + width * total * 2,
            transcendentals=0,
        ),
        name="weight_terms",
    )(*values)


def _rows_kernel(sides, blocks, arrived, cuts, *refs):
    lefts, refs = refs[: sides * blocks], refs[sides * blocks :]
    weight, refs = refs[0], refs[1:]
    there, outs = (refs[0], refs[1:]) if arrived else (None, refs)
    size = lefts[0].shape[0]
    at = 0
    for block in range(blocks):
        column, total = 0, None
        for side in range(sides):
            left = lefts[side * blocks + block]
            depth = left.shape[1]
            term = _dot(left[...], weight[:, column : column + depth], ((1,), (1,)))
            total = term if total is None else total + term
            column += depth
        if arrived:
            total = total + there[block * size : (block + 1) * size, :].astype(jnp.float32)
        row = 0
        while row < size:
            out = outs[cuts[at][0]]
            first, length = cuts[at][1], cuts[at][2]
            out[first : first + length, :] = total[row : row + length].astype(out.dtype)
            row += length
            at += 1


def rows_product(lefts, weight, column, picks, outs, cuts, there=None, size=256, step=512):
    width = weight.shape[0]
    depth = sum(v.shape[1] for v in lefts)
    specs = [
        pl.BlockSpec((size, v.shape[1]), lambda n, p=p: (p, 0), pipeline_mode=pl.Buffered(1))
        for v in lefts
        for p in picks
    ]
    specs.append(pl.BlockSpec((step, depth), lambda n: (n, column)))
    values = [v for v in lefts for _ in picks] + [weight]
    if there is not None:
        specs.append(pl.BlockSpec((there.shape[0], step), lambda n: (0, n)))
        values.append(there)
    rows = size * len(picks)
    return pl.pallas_call(
        functools.partial(_rows_kernel, len(lefts), len(picks), there is not None, cuts),
        grid=(width // step,),
        out_shape=[jax.ShapeDtypeStruct((r, width), t) for r, t in outs],
        in_specs=specs,
        out_specs=[pl.BlockSpec((r, step), lambda n: (0, n)) for r, _ in outs],
        compiler_params=pltpu.CompilerParams(vmem_limit_bytes=LIMIT),
        cost_estimate=pl.CostEstimate(
            flops=2 * rows * width * depth,
            bytes_accessed=rows * depth * 2 + width * depth * 2 + rows * width * 6,
            transcendentals=0,
        ),
        name="rows_product",
    )(*values)


def _settle_kernel(mode, *refs):
    total_ref, x_top, x_bottom, y_top, y_bottom = refs[:5]
    rest = refs[5:]
    rows = total_ref.shape[0]
    step = 32
    for start in range(0, rows, step):
        here = slice(start, start + step)
        upper = start < rows // 2
        there = here if upper else slice(start - rows // 2, start - rows // 2 + step)
        by_x, by_y = (x_top, y_top) if upper else (x_bottom, y_bottom)
        total = total_ref[here, :] + by_x[there, :].astype(jnp.float32) + by_y[there, :].astype(jnp.float32)
        if mode == "add":
            base_ref, out_ref = rest
            out_ref[here, :] = (base_ref[here, :] + total).astype(out_ref.dtype)
        elif mode == "norm":
            base_ref, out_ref, hat_ref = rest
            hidden = base_ref[here, :].astype(jnp.float32) + total
            out_ref[here, :] = hidden
            rstd = lax.rsqrt(jnp.mean(hidden * hidden, axis=1, keepdims=True) + EPS)
            hat_ref[here, :] = (hidden * rstd).astype(jnp.bfloat16)
        else:
            source_ref, base_ref = rest[:2]
            source = source_ref[here, :].astype(jnp.float32)
            rstd = lax.rsqrt(jnp.mean(source * source, axis=1, keepdims=True) + EPS)
            hat = source * rstd
            grad = total - hat * jnp.mean(total * hat, axis=1, keepdims=True)
            out = base_ref[here, :].astype(jnp.float32) + rstd * grad
            rest[2][here, :] = out
            if len(rest) > 3:
                rest[3][here, :] = out.astype(jnp.bfloat16)


def settle(mode, sums, others, types):
    rows, width = sums[0].shape
    return pl.pallas_call(
        functools.partial(_settle_kernel, mode),
        out_shape=[jax.ShapeDtypeStruct((rows, width), t) for t in types],
        in_specs=_whole(5 + len(others)),
        out_specs=_whole(len(types)),
        compiler_params=pltpu.CompilerParams(vmem_limit_bytes=LIMIT),
        cost_estimate=pl.CostEstimate(
            flops=rows * width * 10, bytes_accessed=rows * width * 20, transcendentals=rows
        ),
        name="settle",
    )(*sums, *others)


def low(values):
    return values.astype(jnp.bfloat16)


def wide(values):
    return values.astype(jnp.float32)


def after(values, *others):
    return lax.optimization_barrier((values,) + others)[0]


def across(values, bits):
    return lax.ppermute(values, "ctx", [(i, i ^ bits) for i in range(CTX)])


def other_core(values):
    return lax.ppermute(values, "tp", [(0, 1), (1, 0)])


def in_order(pieces, spot, axis):
    for bit in (1, 2):
        odd = (spot & bit) != 0
        pieces = [jnp.where(odd, pieces[j ^ bit], pieces[j]) for j in range(CTX)]
    return jnp.concatenate(pieces, axis=axis)


def gather_near(own):
    return other_core(own), across(own, 1), across(own, 2)


def gather_far(by_x, by_y):
    half = by_x.shape[0] // 2
    return other_core(by_x), other_core(by_y), across(by_x[:half], 2), across(by_y[half:], 1)


def gather_rows(own, beside=()):
    own_other, by_x, by_y = gather_near(own)
    by_x, by_y = after((by_x, by_y), beside)
    x_other, y_other, far_top, far_bottom = gather_far(by_x, by_y)
    far = [far_top, far_bottom, other_core(far_top), other_core(far_bottom)]
    return [own, own_other, by_x, x_other, by_y, y_other] + far


def scatter_rows(lefts, weight, column, beside=()):
    size = lefts[0].shape[0] // (2 * CTX)
    half = size // 2
    far_there = rows_product(lefts, weight, column, (7,), [(size, jnp.bfloat16)], [(0, 0, size)])[0]
    rest_there = rows_product(
        lefts,
        after(weight, far_there),
        column,
        (1, 3, 5),
        [(3 * size, jnp.bfloat16)],
        [(0, i * size, size) for i in range(3)],
    )[0]
    far_there = after(other_core(far_there), rest_there)
    rest_there = other_core(rest_there)
    far_top, far_bottom = rows_product(
        lefts,
        weight,
        column,
        (6,),
        [(half, jnp.bfloat16)] * 2,
        [(0, 0, half), (1, 0, half)],
        far_there,
    )
    far_top, far_bottom = after((far_top, far_bottom), beside)
    to_y = across(far_top, 1)
    to_x = across(far_bottom, 2)
    own, x_top, x_bottom, y_top, y_bottom = rows_product(
        lefts,
        after(weight, far_top),
        column,
        (0, 2, 4),
        [(size, jnp.float32)]
        + [(half, t) for t in (jnp.bfloat16, jnp.float32, jnp.float32, jnp.bfloat16)],
        [(0, 0, size)] + [(i, 0, half) for i in range(1, 5)],
        rest_there,
    )
    return [own, across(x_top, 1), across(y_bottom, 2), to_x, to_y, x_bottom, y_top], far_top


def scatter_end(parts, beside=()):
    own, from_x_top, from_y_bottom, to_x, to_y, x_bottom, y_top = parts
    to_x, to_y = after((to_x, to_y), own, beside)
    x_bottom = low(x_bottom + wide(to_x))
    y_top = low(y_top + wide(to_y))
    return [own, from_x_top, across(x_bottom, 1), across(y_top, 2), from_y_bottom], (x_bottom, y_top)


def deal_out(values, spot, size, axis):
    got = []
    for j in range(CTX):
        piece = [
            lax.dynamic_slice_in_dim(v, (spot ^ j) * n, n, axis) for v, n in zip(values, size)
        ]
        piece = jnp.concatenate(piece, axis=axis) if len(piece) > 1 else piece[0]
        got.append(across(piece, j) if j else piece)
    return got


def gather_stages(shard):
    return lax.all_gather(shard, "fsdp", axis=0, tiled=True)


def sum_stages(values):
    return lax.psum_scatter(values, "fsdp", scatter_dimension=0, tiled=True)


def on_device(
    tokens,
    cotangent,
    lengths,
    deal,
    attn_gain,
    w_query,
    w_key,
    w_value,
    w_out,
    query_gain,
    key_gain,
    ffn_gain,
    w_gate,
    w_up,
    w_down,
):
    stages = lax.axis_size("fsdp")
    spot = lax.axis_index("ctx")
    core = lax.axis_index("tp")
    local_rows, width = tokens.shape
    head_size = query_gain.shape[0]
    half_rows = local_rows // 2
    heads = w_query.shape[1] // head_size // CTX
    query_cols = heads * head_size
    proj_cols = query_cols + 2 * head_size
    units = w_gate.shape[1] // CTX
    shard = width // stages // CTX

    def dealt_rows(values):
        got = [
            lax.dynamic_slice_in_dim(values, (spot ^ j) * shard, shard, 0) for j in range(CTX)
        ]
        return [across(v, j) if j else v for j, v in enumerate(got)]

    attn_scale = wide(attn_gain)[:, None]
    feed_scale = wide(ffn_gain)[:, None]
    scaled = [low(wide(w) * attn_scale) for w in (w_query, w_key, w_value)]
    dealt = deal_out(scaled + [w_out.T], spot, (query_cols, head_size, head_size, query_cols), 1)
    attn_weight = gather_stages(in_order(dealt, spot, 0))

    per_half = half_rows // BLK
    order = jnp.arange(deal.shape[1], dtype=jnp.int32).reshape(CTX, 2, per_half)
    chips = jnp.arange(CTX, dtype=jnp.int32) ^ spot
    cores = jnp.arange(2, dtype=jnp.int32) ^ core
    order = ((chips[:, None] * 2 + cores[None, :])[:, :, None] * per_half + order[0, 0]).reshape(-1)
    blocks = jnp.sum(
        jnp.where(order[:, None] == jnp.arange(order.shape[0])[None, :], deal[0][None, :], 0), axis=1
    )
    spots = jnp.arange(order.shape[0], dtype=jnp.int32)
    where_is = jnp.sum(
        jnp.where(blocks[None, :] == spots[:, None], spots[None, :], 0), axis=1
    ).astype(jnp.int32)
    info = jnp.concatenate([where_is, lengths])
    info, blocks = after((info, blocks), dealt)
    positions = (blocks[:, None] * BLK + jnp.arange(BLK, dtype=jnp.int32)[None, :]).reshape(-1)
    frequency = THETA ** (-(jnp.arange(head_size // 2, dtype=jnp.float32) * 2.0 / head_size))
    angles = wide(positions)[:, None] * frequency[None, :]
    cosine, sine = jnp.cos(angles), jnp.sin(angles)
    cosine = jnp.concatenate([cosine, cosine], axis=1)
    sine = jnp.concatenate([-sine, sine], axis=1)
    query_scale = wide(query_gain)[None, :]
    key_scale = wide(key_gain)[None, :]

    own = lax.dynamic_slice_in_dim(tokens, core * half_rows, half_rows, 0)
    inputs = wide(own)
    rstd = lax.rsqrt(jnp.mean(inputs * inputs, axis=1, keepdims=True) + EPS)
    normed = gather_rows(after(low(inputs * rstd), dealt), (info, cosine, sine))

    feed_dealt = deal_out(
        [low(wide(after(w, normed[2:6])) * feed_scale) for w in (w_gate, w_up)],
        spot,
        (units, units),
        1,
    )
    feed_weight = gather_stages(in_order(feed_dealt, spot, 0))
    down_dealt = deal_out([after(w_down, feed_dealt).T], spot, (units,), 1)

    valid = positions[:half_rows] < lengths[0]
    seed = lax.dynamic_slice_in_dim(cotangent, core * half_rows, half_rows, 0)
    seed = jnp.where(valid[:, None], seed, 0).astype(jnp.bfloat16)

    seed_own, seed_x, seed_y = gather_near(after(seed, normed[2:]))

    proj, qkv, mixed, mixed_low, recip = attend_forward(
        info, normed, attn_weight, cosine, sine, query_scale, key_scale, heads
    )
    mixed_low, seed_x, seed_y, down_dealt = lax.optimization_barrier(
        (mixed_low, seed_x, seed_y, down_dealt)
    )
    down_weight = gather_stages(in_order(down_dealt, spot, 0))
    seed_rest = gather_far(seed_x, seed_y)
    parts, _ = scatter_rows(
        [mixed_low], attn_weight, proj_cols // query_cols, (seed_own, seed_rest)
    )
    sums, _ = scatter_end(parts)
    seed_far = [other_core(v) for v in after(seed_rest[2:], parts[0])]
    seeds = [seed, seed_own, seed_x, seed_rest[0], seed_y, *seed_rest[1:]] + seed_far
    sums = after(sums, seed_far)
    hidden, hat_two = settle("norm", sums, (own,), (jnp.float32, jnp.bfloat16))

    other, by_x, by_y = gather_near(hat_two)
    filled = feed_expand([[hat_two, other]], 0, feed_weight, local_rows * CTX)
    by_x, by_y = after((by_x, by_y), filled[0])
    x_other, y_other, far_top, far_bottom = gather_far(by_x, by_y)
    filled = feed_expand([[by_x, x_other], [by_y, y_other]], 1, feed_weight, local_rows * CTX, filled)
    far = list(after((far_top, far_bottom), filled[0]))
    far += [other_core(v) for v in far]
    slope, silu, inner = feed_expand([far], 3, feed_weight, local_rows * CTX, filled)
    normed_two = [hat_two, other, by_x, x_other, by_y, y_other] + far
    grad_down = weight_terms([(seeds, [inner])])
    down_weight, grad_down = lax.optimization_barrier((down_weight, grad_down))
    grad_down = sum_stages(grad_down)
    dgate, dup = feed_back(seeds, down_weight, slope, silu)
    parts, _ = scatter_rows([dgate, dup], feed_weight, 0)
    sums, sent = scatter_end(parts)
    grad_feed = weight_terms([(normed_two, [after(dgate, sent), dup])])
    sums, grad_feed = lax.optimization_barrier((sums, grad_feed))
    grad_feed = sum_stages(after(grad_feed, grad_down))
    grad_hidden, grad_attn = settle("back", sums, (hidden, seed), (jnp.float32, jnp.bfloat16))

    feed_parts, _ = scatter_rows([after(inner, grad_attn)], down_weight, 0)
    grad_attn = gather_rows(grad_attn)
    grad_attn = after(grad_attn, feed_parts[0], feed_parts[5])
    grad_proj, gain_sums = attend_backward(
        info, grad_attn, attn_weight, proj, qkv, mixed, recip, cosine, sine, query_scale, key_scale, heads
    )
    down_pieces = dealt_rows(grad_down)
    grad_proj, down_pieces, feed_parts = lax.optimization_barrier(
        (grad_proj, down_pieces, feed_parts)
    )
    grad_attn_w = weight_terms([(normed, [grad_proj]), (grad_attn, [mixed_low])])
    parts, far = scatter_rows([grad_proj], after(attn_weight, grad_attn_w), 0)
    feed_sums, _ = scatter_end(feed_parts, far)
    sums, sent = scatter_end(parts, feed_sums[0])
    grad_attn_w = sum_stages(after(grad_attn_w, grad_feed))
    (grad_tokens_half,) = settle("back", sums, (own, grad_hidden), (jnp.float32,))
    (output_half,) = settle("add", after(feed_sums, grad_tokens_half), (hidden,), (jnp.bfloat16,))

    def whole_rows(values):
        other = other_core(values)
        first = core == 0
        return jnp.concatenate(
            [jnp.where(first, values, other), jnp.where(first, other, values)], axis=0
        )

    def cut(pieces, start, size):
        return wide(in_order([p[:, start : start + size] for p in pieces], spot, 1))

    grad_down_w = cut(down_pieces, 0, units).T
    feed_pieces = dealt_rows(after(grad_feed, sent))
    grad_gate_w = cut(feed_pieces, 0, units)
    grad_up_w = cut(feed_pieces, units, units)
    proj_pieces = dealt_rows(after(grad_attn_w, grad_gate_w, grad_up_w))
    grad_query_w = cut(proj_pieces, 0, query_cols)
    grad_key_w = cut(proj_pieces, query_cols, head_size)
    grad_value_w = cut(proj_pieces, query_cols + head_size, head_size)
    grad_out_w = cut(proj_pieces, proj_cols, query_cols).T

    def gain_part(pairs):
        return sum(jnp.sum(wide(w) * g, axis=1) for w, g in pairs)

    feed_gain = gain_part(((w_gate, grad_gate_w), (w_up, grad_up_w)))
    norm_gain = gain_part(((w_query, grad_query_w), (w_key, grad_key_w), (w_value, grad_value_w)))
    feed_gain = feed_gain + other_core(feed_gain)
    norm_gain = norm_gain + other_core(norm_gain)
    gain_sums = after(gain_sums, grad_tokens_half)
    gain_sums = gain_sums + other_core(gain_sums)
    for bit in (1, 2):
        gain_sums = gain_sums + across(gain_sums, bit)
    gain_sums = lax.psum(gain_sums, "fsdp")
    return (
        whole_rows(output_half),
        whole_rows(grad_tokens_half),
        norm_gain,
        grad_query_w * attn_scale,
        grad_key_w * attn_scale,
        grad_value_w * attn_scale,
        grad_out_w,
        gain_sums[0],
        gain_sums[1],
        feed_gain,
        grad_gate_w * feed_scale,
        grad_up_w * feed_scale,
        grad_down_w,
    )


def solution(mesh):
    return jax.shard_map(
        on_device,
        mesh=mesh,
        in_specs=(
            P(("fsdp", "ctx"), None),
            P(("fsdp", "ctx"), None),
            P("fsdp"),
            P("fsdp", None),
            P(("fsdp", "ctx")),
            P(("fsdp", "ctx"), "tp"),
            P(("fsdp", "ctx"), "tp"),
            P(("fsdp", "ctx"), "tp"),
            P("tp", ("fsdp", "ctx")),
            P(),
            P(),
            P(("fsdp", "ctx")),
            P(("fsdp", "ctx"), "tp"),
            P(("fsdp", "ctx"), "tp"),
            P("tp", ("fsdp", "ctx")),
        ),
        out_specs=(
            P(("fsdp", "ctx"), None),
            P(("fsdp", "ctx"), None),
            P(("fsdp", "ctx")),
            P(("fsdp", "ctx"), "tp"),
            P(("fsdp", "ctx"), "tp"),
            P(("fsdp", "ctx"), "tp"),
            P("tp", ("fsdp", "ctx")),
            P(),
            P(),
            P(("fsdp", "ctx")),
            P(("fsdp", "ctx"), "tp"),
            P(("fsdp", "ctx"), "tp"),
            P("tp", ("fsdp", "ctx")),
        ),
        check_vma=False,
    )
```

time: 768 us -> 683 us (0.89)
  Pallas kernels: 59.1 us -> 268 us
  matrix products: 146 us -> 0 us
  waiting for transfers between devices: 312 us -> 216 us
  starting transfers between devices: 134 us -> 73.7 us
  local copies, waits for them, and re-layouts: 54.1 us -> 30.1 us
  blocking collectives: 0 us -> 22.5 us
  between operations: 3.85 us -> 16.1 us
    pallas_call x0 -> x27, Pallas kernels: none -> 205 us  [the longest x16 92.9 us: rows_product(): pl.pallas_call(functools.partial(_rows_kernel, len(lefts), len(picks), th...]
    ppermute x27 -> x0, waiting for transfers between devices: 148 us -> none  [next_stage(): lax.ppermute(values, 'fsdp', [(i, (i - 1) % count) for i in range(count)])]
    dot_general x64 -> x0, matrix products: 146 us -> none  [the longest x24 51.5 us: right_transposed(): lax.dot_general(left, right, (((1,), (1,)), ((), ())), preferred_element_...]
    ppermute x27 -> x0, starting transfers between devices: 63.1 us -> none  [next_stage(): lax.ppermute(values, 'fsdp', [(i, (i - 1) % count) for i in range(count)])]
    ppermute x37 -> x33, waiting for transfers between devices: 2.46 us -> 33.6 us  [other_core(): return lax.ppermute(values, 'tp', [(0, 1), (1, 0)])]
    psum x0 -> x1, blocking collectives: none -> 22.5 us  [on_device(): gain_sums = lax.psum(gain_sums, 'fsdp')]
    ppermute x58 -> x60, waiting for transfers between devices: 161 us -> 182 us  [across(): return lax.ppermute(values, 'ctx', [(i, i ^ bits) for i in range(CTX)])]
    unnamed x246 -> x186, local copies, waits for them, and re-layouts: 39.1 us -> 20 us
  transfers between devices with their start and end apart: 122 -> 99, of which waited for: 52 -> 47; matrix products, arithmetic and copies ran while one was open for 32% -> 8% of each run, Pallas kernels for 3% -> 40%
where the time goes in v2:
time: 683 us; the launch traced here: 675 us
  Pallas kernels  268 us (39%)
  waiting for transfers between devices  216 us (32%)
  starting transfers between devices  73.7 us (11%)
  other arithmetic  49 us (7%)
  local copies, waits for them, and re-layouts  30.1 us (4%)
  blocking collectives  22.5 us (3%)
  between operations  16.1 us (2%)
    ppermute x60, waiting for transfers between devices, across(): return lax.ppermute(values, 'ctx', [(i, i ^ bits) for i in range(CTX)])  182 us
    pallas_call x16, Pallas kernels, rows_product(): pl.pallas_call(functools.partial(_rows_kernel, len(lefts), len(picks), th...  92.9 us
    ppermute x60, starting transfers between devices, across(): return lax.ppermute(values, 'ctx', [(i, i ^ bits) for i in range(CTX)])  66.4 us
    pallas_call x3, Pallas kernels, weight_terms(): pl.pallas_call(functools.partial(_terms_kernel, [(len(p), len(o)) for p,...  46 us
    ppermute x33, waiting for transfers between devices, other_core(): return lax.ppermute(values, 'tp', [(0, 1), (1, 0)])  33.6 us
    pallas_call x1, Pallas kernels, attend_forward(): pl.pallas_call(functools.partial(_forward_kernel, heads, hd ** (-0.5)), o...  31.8 us
    pallas_call x1, Pallas kernels, attend_backward(): pl.pallas_call(functools.partial(_backward_kernel, heads, hd ** (-0.5)),...  31.5 us
    pallas_call x3, Pallas kernels, feed_expand(): pl.pallas_call(functools.partial(_expand_kernel, [len(group) for group in...  29.9 us
  transfers between devices with their start and end apart: 99, of which 47 were waited for; matrix products, arithmetic and copies ran while one was open for 8% of the time, Pallas kernels for 40%

profile of v2, /device:TPU:0, one launch (start us, length us, event | category | flops | bytes accessed | tf_op | source)
XLA Modules:
  0.0 675.2 jit_solution(5935463815473948609)
XLA Ops:
  20.6 4.3 collective-permute-done.2
  37.4 14.6 %collective-permute-done.3.refs_2_ = bf16[256,2048]{1,0:T(8,128)(2,1)S(1)} collective-permute-done((bf16[256,2048]{1,0:T(8,128)(2,1)}, bf16[256,2048]{1,0:T(8,128)(2,1)S(1)}, u32[]{:S(2)}, u32[]{:S(2)}) %collective-permute-start.3) | collective-permute-done | bytes 1048608 | tf_op jit(solution)/shard_map/ppermute | solution.py:517
  62.2 9.2 %collective-permute-done.17 = bf16[128,1536]{1,0:T(8,128)(2,1)S(1)} collective-permute-done((bf16[128,1536]{1,0:T(8,128)(2,1)S(1)}, bf16[128,1536]{1,0:T(8,128)(2,1)S(1)}, u32[]{:S(2)}, u32[]{:S(2)}) %collective-permute-start.17) | collective-permute-done | bytes 393248 | tf_op jit(solution)/shard_map/ppermute | solution.py:517
  71.4 6.8 %collective-permute-done.16 = bf16[128,1536]{1,0:T(8,128)(2,1)S(1)} collective-permute-done((bf16[128,1536]{1,0:T(8,128)(2,1)S(1)}, bf16[128,1536]{1,0:T(8,128)(2,1)S(1)}, u32[]{:S(2)}, u32[]{:S(2)}) %collective-permute-start.16) | collective-permute-done | bytes 393248 | tf_op jit(solution)/shard_map/ppermute | solution.py:517
  83.6 11.5 %collective-permute-done.8.refs_7_ = bf16[128,2048]{1,0:T(8,128)(2,1)S(1)} collective-permute-done((bf16[128,2048]{1,0:T(8,128)(2,1)S(1)}, bf16[128,2048]{1,0:T(8,128)(2,1)S(1)}, u32[]{:S(2)}, u32[]{:S(2)}) %collective-permute-start.8) | collective-permute-done | bytes 524320 | tf_op jit(solution)/shard_map/ppermute | solution.py:517
  106.9 31.8 %attend_forward.1 = (f32[2048,512]{1,0:T(8,128)}, bf16[2048,512]{1,0:T(8,128)(2,1)}, f32[2048,256]{1,0:T(8,128)}, bf16[2048,256]{1,0:T(8,128)(2,1)}, f32[2048,256]{1,0:T(8,128)}) custom-call(s32[17]{0:T(128)} %pad_add_fusion.info, bf16[256,2048]{1,0:T(8,128)(2,1)} %fusion.1.refs_0_, bf16[256,2048]{1,0:T(8,128)(2,1)} %collective-permute-done.12.refs_1_, ...), custom_call_target="tpu_custom_call" | custom-call | flops 6442450944 | bytes 26214400 | tf_op jit(solution)/shard_map/attend_forward/pallas_call | solution.py:122
  138.8 4.3 rows_product.16
  143.2 4.8 rows_product.17
  150.2 7.5 %collective-permute-done.11.refs_1_ = bf16[256,2048]{1,0:T(8,128)(2,1)S(1)} collective-permute-done((bf16[256,2048]{1,0:T(8,128)(2,1)S(1)}, bf16[256,2048]{1,0:T(8,128)(2,1)S(1)}, u32[]{:S(2)}, u32[]{:S(2)}) %collective-permute-start.11) | collective-permute-done | bytes 1048608 | tf_op jit(solution)/shard_map/ppermute | solution.py:521
  164.1 7.8 %collective-permute-done.23.refs_6_ = bf16[128,2048]{1,0:T(8,128)(2,1)S(1)} collective-permute-done((bf16[128,2048]{1,0:T(8,128)(2,1)S(1)}, bf16[128,2048]{1,0:T(8,128)(2,1)S(1)}, u32[]{:S(2)}, u32[]{:S(2)}) %collective-permute-start.23) | collective-permute-done | bytes 524320 | tf_op jit(solution)/shard_map/ppermute | solution.py:517
  176.5 5.6 rows_product.19
  182.1 4.1 collective-permute-done.30
  192.9 7.5 %collective-permute-done.33.refs_3_ = bf16[128,2048]{1,0:T(8,128)(2,1)S(1)} collective-permute-done((bf16[128,2048]{1,0:T(8,128)(2,1)S(1)}, bf16[128,2048]{1,0:T(8,128)(2,1)S(1)}, u32[]{:S(2)}, u32[]{:S(2)}) %collective-permute-start.33) | collective-permute-done | bytes 524320 | tf_op jit(solution)/shard_map/ppermute | solution.py:517
  205.5 8.1 %collective-permute-done.29.refs_1_ = bf16[128,2048]{1,0:T(8,128)(2,1)} collective-permute-done((bf16[128,2048]{1,0:T(8,128)(2,1)}, bf16[128,2048]{1,0:T(8,128)(2,1)}, u32[]{:S(2)}, u32[]{:S(2)}) %collective-permute-start.29) | collective-permute-done | bytes 524320 | tf_op jit(solution)/shard_map/ppermute | solution.py:517
  213.7 4.8 settle.4
  222.4 8.1 %feed_expand.3 = (f32[2048,768]{1,0:T(8,128)}, f32[2048,768]{1,0:T(8,128)}, bf16[2048,768]{1,0:T(8,128)(2,1)}) custom-call(bf16[256,2048]{1,0:T(8,128)(2,1)} %get-tuple-element.195.refs_0_, bf16[256,2048]{1,0:T(8,128)(2,1)} %copy-done.17, bf16[2048,1536]{1,0:T(8,128)(2,1)} %all-gather.8.cloned.1.call-done.refs_2_.refs_3_.refs_4_.refs_5_.refs_6_, ...), custom_call_target="tpu_custom_call" | custom-call | flops 3221225472 | bytes 12320768 | tf_op jit(solution)/shard_map/feed_expand/pallas_call | solution.py:301
  230.5 13.8 %collective-permute-done.35.refs_0_.refs_2_ = bf16[256,2048]{1,0:T(8,128)(2,1)S(1)} collective-permute-done((bf16[256,2048]{1,0:T(8,128)(2,1)}, bf16[256,2048]{1,0:T(8,128)(2,1)S(1)}, u32[]{:S(2)}, u32[]{:S(2)}) %collective-permute-start.35) | collective-permute-done | bytes 1048608 | tf_op jit(solution)/shard_map/ppermute | solution.py:517
  250.4 13.8 %feed_expand.4 = (f32[2048,768]{1,0:T(8,128)}, f32[2048,768]{1,0:T(8,128)}, bf16[2048,768]{1,0:T(8,128)(2,1)}) custom-call(bf16[256,2048]{1,0:T(8,128)(2,1)} %copy-done.15, bf16[256,2048]{1,0:T(8,128)(2,1)} %copy-done.19, bf16[256,2048]{1,0:T(8,128)(2,1)} %copy-done.16, ...), custom_call_target="tpu_custom_call", output_to_operand_aliasing={{0}: (6, {}), {1}: (7, {}), {2}: (8, {})} | custom-call | flops 6442450944 | bytes 18350080 | tf_op jit(solution)/shard_map/feed_expand/pallas_call | solution.py:301
  267.8 8.0 %feed_expand.5 = (f32[2048,768]{1,0:T(8,128)}, f32[2048,768]{1,0:T(8,128)}, bf16[2048,768]{1,0:T(8,128)(2,1)}) custom-call(bf16[128,2048]{1,0:T(8,128)(2,1)} %copy-done.55, bf16[128,2048]{1,0:T(8,128)(2,1)} %copy-done.56, bf16[128,2048]{1,0:T(8,128)(2,1)} %copy-done.57, ...), custom_call_target="tpu_custom_call", output_to_operand_aliasing={{0}: (6, {}), {1}: (7, {}), {2}: (8, {})} | custom-call | flops 3221225472 | bytes 12320768 | tf_op jit(solution)/shard_map/feed_expand/pallas_call | solution.py:301
  275.8 12.7 %weight_terms.3 = bf16[2048,768]{1,0:T(8,128)(2,1)} custom-call(bf16[256,2048]{1,0:T(8,128)(2,1)} %copy-done.1, bf16[256,2048]{1,0:T(8,128)(2,1)} %copy-done.18, bf16[256,2048]{1,0:T(8,128)(2,1)} %copy-done.14, bf16[256,2048]{1,0:T(8,128)(2,1)} %collective-permute-done.21.refs_3_, bf16[256,2048]{1,0:T(8,128)(2,1)} %collective-permute-done.14.refs_4_, ...), custom_call_target="tpu_custom_call" | custom-call | flops 6442450944 | bytes 14680064 | tf_op jit(solution)/shard_map/weight_terms/pallas_call | solution.py:385
  288.7 15.1 %feed_back.1 = (bf16[2048,768]{1,0:T(8,128)(2,1)}, bf16[2048,768]{1,0:T(8,128)(2,1)}) custom-call(bf16[256,2048]{1,0:T(8,128)(2,1)} %copy-done.1, bf16[256,2048]{1,0:T(8,128)(2,1)} %copy-done.18, bf16[256,2048]{1,0:T(8,128)(2,1)} %copy-done.14, bf16[256,2048]{1,0:T(8,128)(2,1)} %collective-permute-done.21.refs_3_, ...), custom_call_target="tpu_custom_call" | custom-call | flops 6442450944 | bytes 30408704 | tf_op jit(solution)/shard_map/feed_back/pallas_call | solution.py:343
  303.9 5.8 rows_product.20
  309.7 9.1 %rows_product.21 = bf16[768,2048]{1,0:T(8,128)(2,1)} custom-call(bf16[2048,768]{1,0:T(8,128)(2,1)} %get-tuple-element.224.refs_0_.refs_1_.refs_2_.refs_10_, bf16[2048,768]{1,0:T(8,128)(2,1)} %get-tuple-element.224.refs_0_.refs_1_.refs_2_.refs_10_, bf16[2048,768]{1,0:T(8,128)(2,1)} %get-tuple-element.224.refs_0_.refs_1_.refs_2_.refs_10_, ...), custom_call_target="tpu_custom_call" | custom-call | flops 4831838208 | bytes 18087936 | tf_op jit(solution)/shard_map/rows_product/pallas_call | solution.py:441
  319.4 6.5 collective-permute-done.44.refs_3_
  326.8 5.9 rows_product.22
  336.5 9.5 %rows_product.23 = (f32[256,2048]{1,0:T(8,128)}, bf16[128,2048]{1,0:T(8,128)(2,1)}, f32[128,2048]{1,0:T(8,128)}, f32[128,2048]{1,0:T(8,128)}, bf16[128,2048]{1,0:T(8,128)(2,1)}) custom-call(bf16[2048,768]{1,0:T(8,128)(2,1)} %get-tuple-element.224.refs_0_.refs_1_.refs_2_.refs_10_, bf16[2048,768]{1,0:T(8,128)(2,1)} %get-tuple-element.224.refs_0_.refs_1_.refs_2_.refs_10_, ...), custom_call_target="tpu_custom_call" | custom-call | flops 4831838208 | bytes 18087936 | tf_op jit(solution)/shard_map/rows_product/pallas_call | solution.py:441
  353.3 19.3 %weight_terms.4 = bf16[2048,1536]{1,0:T(8,128)(2,1)} custom-call(bf16[256,2048]{1,0:T(8,128)(2,1)} %get-tuple-element.195.refs_0_, bf16[256,2048]{1,0:T(8,128)(2,1)} %copy-done.17, bf16[256,2048]{1,0:T(8,128)(2,1)} %copy-done.15, bf16[256,2048]{1,0:T(8,128)(2,1)} %copy-done.19, bf16[256,2048]{1,0:T(8,128)(2,1)} %copy-done.16, bf16[256,2048]{1,0:T(8,128)(2,1)} %copy-done.20, ...), custom_call_target="tpu_custom_call" | custom-call | flops 12884901888 | bytes 20971520 | tf_op jit(solution)/shard_map/weight_terms/pallas_call | solution.py:385
  375.7 6.1 settle.5
  381.8 5.0 rows_product.24
  386.8 6.5 rows_product.25
  395.7 23.3 %collective-permute-done.53.refs_2_.refs_13_ = bf16[256,2048]{1,0:T(8,128)(2,1)} collective-permute-done((bf16[256,2048]{1,0:T(8,128)(2,1)S(1)}, bf16[256,2048]{1,0:T(8,128)(2,1)}, u32[]{:S(2)}, u32[]{:S(2)}) %collective-permute-start.53) | collective-permute-done | bytes 1048608 | tf_op jit(solution)/shard_map/ppermute | solution.py:517
  424.1 9.6 %collective-permute-done.57.refs_6_.refs_17_ = bf16[128,2048]{1,0:T(8,128)(2,1)S(1)} collective-permute-done((bf16[128,2048]{1,0:T(8,128)(2,1)S(1)}, bf16[128,2048]{1,0:T(8,128)(2,1)S(1)}, u32[]{:S(2)}, u32[]{:S(2)}) %collective-permute-start.57) | collective-permute-done | bytes 524320 | tf_op jit(solution)/shard_map/ppermute | solution.py:517
  435.8 4.8 rows_product.26
  444.1 6.8 %rows_product.27 = (f32[256,2048]{1,0:T(8,128)}, bf16[128,2048]{1,0:T(8,128)(2,1)}, f32[128,2048]{1,0:T(8,128)}, f32[128,2048]{1,0:T(8,128)}, bf16[128,2048]{1,0:T(8,128)(2,1)}) custom-call(bf16[2048,768]{1,0:T(8,128)(2,1)} %get-tuple-element.234.refs_10_.refs_0_.refs_1_.refs_2_, bf16[2048,768]{1,0:T(8,128)(2,1)} %get-tuple-element.234.refs_10_.refs_0_.refs_1_.refs_2_, ...), custom_call_target="tpu_custom_call" | custom-call | flops 2415919104 | bytes 13762560 | tf_op jit(solution)/shard_map/rows_product/pallas_call | solution.py:441
  458.6 31.5 %attend_backward.1 = (bf16[2048,512]{1,0:T(8,128)(2,1)}, f32[8,128]{1,0:T(8,128)}) custom-call(s32[17]{0:T(128)} %pad_add_fusion.info, bf16[256,2048]{1,0:T(8,128)(2,1)} %get-tuple-element.241.refs_0_.refs_11_, bf16[256,2048]{1,0:T(8,128)(2,1)} %copy-done.78, bf16[256,2048]{1,0:T(8,128)(2,1)} %collective-permute-done.53.refs_2_.refs_13_, ...), custom_call_target="tpu_custom_call" | custom-call | flops 7516192768 | bytes 36700160 | tf_op jit(solution)/shard_map/attend_backward/pallas_call | solution.py:248
  490.9 13.9 %weight_terms.5 = bf16[2048,768]{1,0:T(8,128)(2,1)} custom-call(bf16[256,2048]{1,0:T(8,128)(2,1)} %fusion.1.refs_0_, bf16[256,2048]{1,0:T(8,128)(2,1)} %collective-permute-done.12.refs_1_, bf16[256,2048]{1,0:T(8,128)(2,1)} %copy-done.59, bf16[256,2048]{1,0:T(8,128)(2,1)} %collective-permute-done.5.refs_3_, bf16[256,2048]{1,0:T(8,128)(2,1)} %collective-permute-done.4.refs_4_, ...), custom_call_target="tpu_custom_call" | custom-call | flops 6442450944 | bytes 23068672 | tf_op jit(solution)/shard_map/weight_terms/pallas_call | solution.py:385
  504.9 4.3 rows_product.28
  509.2 5.4 rows_product.29
  515.1 6.3 collective-permute-done.70.refs_2_
  522.4 4.4 rows_product.30
  532.8 6.3 rows_product.31
  549.8 15.2 %collective-permute-done.78.refs_3_ = bf16[128,2048]{1,0:T(8,128)(2,1)S(1)} collective-permute-done((bf16[128,2048]{1,0:T(8,128)(2,1)S(1)}, bf16[128,2048]{1,0:T(8,128)(2,1)S(1)}, u32[]{:S(2)}, u32[]{:S(2)}) %collective-permute-start.78) | collective-permute-done | bytes 524320 | tf_op jit(solution)/shard_map/ppermute | solution.py:517
  566.3 6.8 %collective-permute-done.74.refs_1_ = bf16[128,2048]{1,0:T(8,128)(2,1)S(1)} collective-permute-done((bf16[128,2048]{1,0:T(8,128)(2,1)S(1)}, bf16[128,2048]{1,0:T(8,128)(2,1)S(1)}, u32[]{:S(2)}, u32[]{:S(2)}) %collective-permute-start.74) | collective-permute-done | bytes 524320 | tf_op jit(solution)/shard_map/ppermute | solution.py:517
  576.2 5.8 settle.6
  583.5 4.2 settle.7
  600.7 22.5 %psum.7 = f32[8,128]{1,0:T(8,128)S(1)} all-reduce(f32[8,128]{1,0:T(8,128)S(1)} %add.234), channel_id=1, replica_groups=mesh['fsdp'=4,'ctx'=4,'tp'=2] {'fsdp'}, use_global_device_ids=true, to_apply=%region_9.10 | all-reduce | flops 1024 | bytes 8192 | tf_op jit(solution)/shard_map/psum | solution.py:784
  634.7 5.3 collective-permute-done.82
  640.0 4.2 collective-permute-done.83
  (461 shorter events, 199.9 us)
Async XLA Ops:
  7.2 99.7 %all-gather.4.cloned.1.call-start = ((), (), s32[]{:S(2)}) async-start(), calls=%async_computation.3 | async-start | bytes 3932160 | tf_op jit(solution)/shard_map/all_gather | solution.py:607
  27.6 24.4 %collective-permute-start.3 = (bf16[256,2048]{1,0:T(8,128)(2,1)}, bf16[256,2048]{1,0:T(8,128)(2,1)S(1)}, u32[]{:S(2)}, u32[]{:S(2)}) collective-permute-start(bf16[256,2048]{1,0:T(8,128)(2,1)} %fusion.1.refs_0_), channel_id=1, source_target_pairs={{0,2},{2,0},{4,6},{6,4},{1,3},{3,1},{5,7},{7,5},{8,10},{10,8},{12,... | collective-permute-start | bytes 3145736 | tf_op jit(solution)/shard_map/ppermute | solution.py:517
  29.2 24.1 %collective-permute-start.4 = (bf16[256,2048]{1,0:T(8,128)(2,1)}, bf16[256,2048]{1,0:T(8,128)(2,1)}, u32[]{:S(2)}, u32[]{:S(2)}) collective-permute-start(bf16[256,2048]{1,0:T(8,128)(2,1)} %fusion.1.refs_0_), channel_id=1, source_target_pairs={{0,4},{2,6},{4,0},{6,2},{1,5},{3,7},{5,1},{7,3},{8,12},{10,14},{12... | collective-permute-start | bytes 3145736 | tf_op jit(solution)/shard_map/ppermute | solution.py:517
  30.9 190.5 %all-gather.8.cloned.1.call-start = ((), (), s32[]{:S(2)}) async-start(), calls=%async_computation.5 | async-start | bytes 7864320 | tf_op jit(solution)/shard_map/all_gather | solution.py:607
  58.9 19.4 %collective-permute-start.16 = (bf16[128,1536]{1,0:T(8,128)(2,1)S(1)}, bf16[128,1536]{1,0:T(8,128)(2,1)S(1)}, u32[]{:S(2)}, u32[]{:S(2)}) collective-permute-start(bf16[128,1536]{1,0:T(8,128)(2,1)S(1)} %pad_maximum_fusion.9), channel_id=1, source_target_pairs={{0,4},{2,6},{4,0},{6,2},{1,5},{3,7},{5,1},{7,3},{8,12},{10,14},{12... | collective-permute-start | bytes 1179656 | tf_op jit(solution)/shard_map/ppermute | solution.py:517
  60.6 17.6 %collective-permute-start.15 = (bf16[128,1536]{1,0:T(8,128)(2,1)S(1)}, bf16[128,1536]{1,0:T(8,128)(2,1)S(1)}, u32[]{:S(2)}, u32[]{:S(2)}) collective-permute-start(bf16[128,1536]{1,0:T(8,128)(2,1)S(1)} %pad_maximum_fusion.8), channel_id=1, source_target_pairs={{0,2},{2,0},{4,6},{6,4},{1,3},{3,1},{5,7},{7,5},{8,10},{10,8},{12,... | collective-permute-start | bytes 1179656 | tf_op jit(solution)/shard_map/ppermute | solution.py:517
  79.9 208.6 %all-gather.6.cloned.1.call-start = ((), (), s32[]{:S(2)}) async-start(), calls=%async_computation.4 | async-start | bytes 3932160 | tf_op jit(solution)/shard_map/all_gather | solution.py:607
  83.6 21.7 %collective-permute-start.12 = (bf16[256,2048]{1,0:T(8,128)(2,1)}, bf16[256,2048]{1,0:T(8,128)(2,1)}, u32[]{:S(2)}, u32[]{:S(2)}) collective-permute-start(bf16[256,2048]{1,0:T(8,128)(2,1)} %fusion.1.refs_0_), channel_id=1, source_target_pairs={{0,1},{1,0},{2,3},{3,2},{4,5},{5,4},{6,7},{7,6},{8,9},{9,8},{10,11... | collective-permute-start | bytes 3145736 | tf_op jit(solution)/shard_map/ppermute | solution.py:521
  98.6 40.2 %collective-permute-start.13 = (bf16[256,2048]{1,0:T(8,128)(2,1)S(1)}, bf16[256,2048]{1,0:T(8,128)(2,1)S(1)}, u32[]{:S(2)}, u32[]{:S(2)}) collective-permute-start(bf16[256,2048]{1,0:T(8,128)(2,1)S(1)} %dynamic-slice_select_fusion.refs_0_.refs_6_), channel_id=1, source_target_pairs={{0,2},{2,0},{4,6},{6,4},{1,3},{3,1},{5,7},{7,5},{8,10},{10,8},{12,... | collective-permute-start | bytes 3145736 | tf_op jit(solution)/shard_map/ppermute | solution.py:517
  99.5 39.3 %collective-permute-start.14 = (bf16[256,2048]{1,0:T(8,128)(2,1)S(1)}, bf16[256,2048]{1,0:T(8,128)(2,1)}, u32[]{:S(2)}, u32[]{:S(2)}) collective-permute-start(bf16[256,2048]{1,0:T(8,128)(2,1)S(1)} %dynamic-slice_select_fusion.refs_0_.refs_6_), channel_id=1, source_target_pairs={{0,4},{2,6},{4,0},{6,2},{1,5},{3,7},{5,1},{7,3},{8,12},{10,14},{12... | collective-permute-start | bytes 3145736 | tf_op jit(solution)/shard_map/ppermute | solution.py:517
  103.4 35.3 %collective-permute-start.18 = (bf16[128,768]{1,0:T(8,128)(2,1)}, bf16[128,768]{1,0:T(8,128)(2,1)S(1)}, u32[]{:S(2)}, u32[]{:S(2)}) collective-permute-start(bf16[128,768]{1,0:T(8,128)(2,1)} %get-tuple-element.406), channel_id=1, source_target_pairs={{0,2},{2,0},{4,6},{6,4},{1,3},{3,1},{5,7},{7,5},{8,10},{10,8},{12,... | collective-permute-start | bytes 589832 | tf_op jit(solution)/shard_map/ppermute | solution.py:517
  104.2 34.5 %collective-permute-start.19 = (bf16[128,768]{1,0:T(8,128)(2,1)S(1)}, bf16[128,768]{1,0:T(8,128)(2,1)S(1)}, u32[]{:S(2)}, u32[]{:S(2)}) collective-permute-start(bf16[128,768]{1,0:T(8,128)(2,1)S(1)} %get-tuple-element.405), channel_id=1, source_target_pairs={{0,4},{2,6},{4,0},{6,2},{1,5},{3,7},{5,1},{7,3},{8,12},{10,14},{12... | collective-permute-start | bytes 589832 | tf_op jit(solution)/shard_map/ppermute | solution.py:517
  105.4 33.4 %collective-permute-start.20 = (bf16[128,768]{1,0:T(8,128)(2,1)S(1)}, bf16[128,768]{1,0:T(8,128)(2,1)S(1)}, u32[]{:S(2)}, u32[]{:S(2)}) collective-permute-start(bf16[128,768]{1,0:T(8,128)(2,1)S(1)} %get-tuple-element.404), channel_id=1, source_target_pairs={{0,6},{2,4},{4,2},{6,0},{1,7},{3,5},{5,3},{7,1},{8,14},{10,12},{12... | collective-permute-start | bytes 589832 | tf_op jit(solution)/shard_map/ppermute | solution.py:517
  147.9 26.9 %collective-permute-start.26 = (bf16[768,2048]{1,0:T(8,128)(2,1)}, bf16[768,2048]{1,0:T(8,128)(2,1)S(1)}, u32[]{:S(2)}, u32[]{:S(2)}) collective-permute-start(bf16[768,2048]{1,0:T(8,128)(2,1)} %rows_product.17), channel_id=1, source_target_pairs={{0,1},{1,0},{2,3},{3,2},{4,5},{5,4},{6,7},{7,6},{8,9},{9,8},{10,11... | collective-permute-start | bytes 9437192 | tf_op jit(solution)/shard_map/ppermute | solution.py:521
  148.5 24.2 %collective-permute-start.21 = (bf16[256,2048]{1,0:T(8,128)(2,1)S(1)}, bf16[256,2048]{1,0:T(8,128)(2,1)}, u32[]{:S(2)}, u32[]{:S(2)}) collective-permute-start(bf16[256,2048]{1,0:T(8,128)(2,1)S(1)} %collective-permute-done.13.refs_2_), channel_id=1, source_target_pairs={{0,1},{1,0},{2,3},{3,2},{4,5},{5,4},{6,7},{7,6},{8,9},{9,8},{10,11... | collective-permute-start | bytes 3145736 | tf_op jit(solution)/shard_map/ppermute | solution.py:521
  149.0 23.8 %collective-permute-start.22 = (bf16[256,2048]{1,0:T(8,128)(2,1)}, bf16[256,2048]{1,0:T(8,128)(2,1)}, u32[]{:S(2)}, u32[]{:S(2)}) collective-permute-start(bf16[256,2048]{1,0:T(8,128)(2,1)} %collective-permute-done.14.refs_4_), channel_id=1, source_target_pairs={{0,1},{1,0},{2,3},{3,2},{4,5},{5,4},{6,7},{7,6},{8,9},{9,8},{10,11... | collective-permute-start | bytes 3145736 | tf_op jit(solution)/shard_map/ppermute | solution.py:521
  192.0 21.7 %collective-permute-start.29 = (bf16[128,2048]{1,0:T(8,128)(2,1)}, bf16[128,2048]{1,0:T(8,128)(2,1)}, u32[]{:S(2)}, u32[]{:S(2)}) collective-permute-start(bf16[128,2048]{1,0:T(8,128)(2,1)} %get-tuple-element.183), channel_id=1, source_target_pairs={{0,2},{2,0},{4,6},{6,4},{1,3},{3,1},{5,7},{7,5},{8,10},{10,8},{12,... | collective-permute-start | bytes 1572872 | tf_op jit(solution)/shard_map/ppermute | solution.py:517
  202.6 172.0 %reduce-scatter.4.cloned.1.call-start = ((), (), s32[]{:S(2)}) async-start(), calls=%async_computation.6 | async-start | bytes 3932160 | tf_op jit(solution)/shard_map/reduce_scatter | solution.py:611
  218.6 25.8 %collective-permute-start.35 = (bf16[256,2048]{1,0:T(8,128)(2,1)}, bf16[256,2048]{1,0:T(8,128)(2,1)S(1)}, u32[]{:S(2)}, u32[]{:S(2)}) collective-permute-start(bf16[256,2048]{1,0:T(8,128)(2,1)} %get-tuple-element.195.refs_0_), channel_id=1, source_target_pairs={{0,2},{2,0},{4,6},{6,4},{1,3},{3,1},{5,7},{7,5},{8,10},{10,8},{12,... | collective-permute-start | bytes 3145736 | tf_op jit(solution)/shard_map/ppermute | solution.py:517
  219.8 25.4 %collective-permute-start.36 = (bf16[256,2048]{1,0:T(8,128)(2,1)}, bf16[256,2048]{1,0:T(8,128)(2,1)S(1)}, u32[]{:S(2)}, u32[]{:S(2)}) collective-permute-start(bf16[256,2048]{1,0:T(8,128)(2,1)} %get-tuple-element.195.refs_0_), channel_id=1, source_target_pairs={{0,4},{2,6},{4,0},{6,2},{1,5},{3,7},{5,1},{7,3},{8,12},{10,14},{12... | collective-permute-start | bytes 3145736 | tf_op jit(solution)/shard_map/ppermute | solution.py:517
  245.8 18.4 %collective-permute-start.38 = (bf16[128,2048]{1,0:T(8,128)(2,1)S(1)}, bf16[128,2048]{1,0:T(8,128)(2,1)S(1)}, u32[]{:S(2)}, u32[]{:S(2)}) collective-permute-start(bf16[128,2048]{1,0:T(8,128)(2,1)S(1)} %slice.115), channel_id=1, source_target_pairs={{0,4},{2,6},{4,0},{6,2},{1,5},{3,7},{5,1},{7,3},{8,12},{10,14},{12... | collective-permute-start | bytes 1572872 | tf_op jit(solution)/shard_map/ppermute | solution.py:517
  246.7 17.5 %collective-permute-start.39 = (bf16[128,2048]{1,0:T(8,128)(2,1)S(1)}, bf16[128,2048]{1,0:T(8,128)(2,1)S(1)}, u32[]{:S(2)}, u32[]{:S(2)}) collective-permute-start(bf16[128,2048]{1,0:T(8,128)(2,1)S(1)} %slice.116), channel_id=1, source_target_pairs={{0,2},{2,0},{4,6},{6,4},{1,3},{3,1},{5,7},{7,5},{8,10},{10,8},{12,... | collective-permute-start | bytes 1572872 | tf_op jit(solution)/shard_map/ppermute | solution.py:517
  288.5 240.4 %reduce-scatter.6.cloned.1.call-start = ((), (), s32[]{:S(2)}) async-start(), calls=%async_computation.7 | async-start | bytes 7864320 | tf_op jit(solution)/shard_map/reduce_scatter | solution.py:611
  349.0 23.6 %collective-permute-start.50 = (bf16[128,2048]{1,0:T(8,128)(2,1)S(1)}, bf16[128,2048]{1,0:T(8,128)(2,1)S(1)}, u32[]{:S(2)}, u32[]{:S(2)}) collective-permute-start(bf16[128,2048]{1,0:T(8,128)(2,1)S(1)} %add_convert_fusion.4), channel_id=1, source_target_pairs={{0,4},{2,6},{4,0},{6,2},{1,5},{3,7},{5,1},{7,3},{8,12},{10,14},{12... | collective-permute-start | bytes 1572872 | tf_op jit(solution)/shard_map/ppermute | solution.py:517
  350.4 22.2 %collective-permute-start.49 = (bf16[128,2048]{1,0:T(8,128)(2,1)S(1)}, bf16[128,2048]{1,0:T(8,128)(2,1)S(1)}, u32[]{:S(2)}, u32[]{:S(2)}) collective-permute-start(bf16[128,2048]{1,0:T(8,128)(2,1)S(1)} %add_convert_fusion.5), channel_id=1, source_target_pairs={{0,2},{2,0},{4,6},{6,4},{1,3},{3,1},{5,7},{7,5},{8,10},{10,8},{12,... | collective-permute-start | bytes 1572872 | tf_op jit(solution)/shard_map/ppermute | solution.py:517
  351.3 23.2 %collective-permute-start.46 = (bf16[128,2048]{1,0:T(8,128)(2,1)}, bf16[128,2048]{1,0:T(8,128)(2,1)S(1)}, u32[]{:S(2)}, u32[]{:S(2)}) collective-permute-start(bf16[128,2048]{1,0:T(8,128)(2,1)} %get-tuple-element.217), channel_id=1, source_target_pairs={{0,2},{2,0},{4,6},{6,4},{1,3},{3,1},{5,7},{7,5},{8,10},{10,8},{12,... | collective-permute-start | bytes 1572872 | tf_op jit(solution)/shard_map/ppermute | solution.py:517
  352.5 22.0 %collective-permute-start.51 = (bf16[128,2048]{1,0:T(8,128)(2,1)}, bf16[128,2048]{1,0:T(8,128)(2,1)S(1)}, u32[]{:S(2)}, u32[]{:S(2)}) collective-permute-start(bf16[128,2048]{1,0:T(8,128)(2,1)} %get-tuple-element.223), channel_id=1, source_target_pairs={{0,4},{2,6},{4,0},{6,2},{1,5},{3,7},{5,1},{7,3},{8,12},{10,14},{12... | collective-permute-start | bytes 1572872 | tf_op jit(solution)/shard_map/ppermute | solution.py:517
  375.5 271.8 %reduce-scatter.8.cloned.1.call-start = ((), (), s32[]{:S(2)}) async-start(), calls=%async_computation.8 | async-start | bytes 3932160 | tf_op jit(solution)/shard_map/reduce_scatter | solution.py:611
  393.3 49.0 %collective-permute-start.62 = (bf16[768,2048]{1,0:T(8,128)(2,1)}, bf16[768,2048]{1,0:T(8,128)(2,1)S(1)}, u32[]{:S(2)}, u32[]{:S(2)}) collective-permute-start(bf16[768,2048]{1,0:T(8,128)(2,1)} %rows_product.25), channel_id=1, source_target_pairs={{0,1},{1,0},{2,3},{3,2},{4,5},{5,4},{6,7},{7,6},{8,9},{9,8},{10,11... | collective-permute-start | bytes 9437192 | tf_op jit(solution)/shard_map/ppermute | solution.py:521
  393.3 25.7 %collective-permute-start.53 = (bf16[256,2048]{1,0:T(8,128)(2,1)S(1)}, bf16[256,2048]{1,0:T(8,128)(2,1)}, u32[]{:S(2)}, u32[]{:S(2)}) collective-permute-start(bf16[256,2048]{1,0:T(8,128)(2,1)S(1)} %copy-done.77), channel_id=1, source_target_pairs={{0,2},{2,0},{4,6},{6,4},{1,3},{3,1},{5,7},{7,5},{8,10},{10,8},{12,... | collective-permute-start | bytes 3145736 | tf_op jit(solution)/shard_map/ppermute | solution.py:517
  394.1 25.3 %collective-permute-start.54 = (bf16[256,2048]{1,0:T(8,128)(2,1)S(1)}, bf16[256,2048]{1,0:T(8,128)(2,1)}, u32[]{:S(2)}, u32[]{:S(2)}) collective-permute-start(bf16[256,2048]{1,0:T(8,128)(2,1)S(1)} %copy-done.77), channel_id=1, source_target_pairs={{0,4},{2,6},{4,0},{6,2},{1,5},{3,7},{5,1},{7,3},{8,12},{10,14},{12... | collective-permute-start | bytes 3145736 | tf_op jit(solution)/shard_map/ppermute | solution.py:517
  395.2 28.4 %collective-permute-start.61 = (bf16[256,2048]{1,0:T(8,128)(2,1)S(1)}, bf16[256,2048]{1,0:T(8,128)(2,1)S(1)}, u32[]{:S(2)}, u32[]{:S(2)}) collective-permute-start(bf16[256,2048]{1,0:T(8,128)(2,1)S(1)} %copy-done.22), channel_id=1, source_target_pairs={{0,1},{1,0},{2,3},{3,2},{4,5},{5,4},{6,7},{7,6},{8,9},{9,8},{10,11... | collective-permute-start | bytes 3145736 | tf_op jit(solution)/shard_map/ppermute | solution.py:521
  395.2 28.4 %collective-permute-start.52 = (bf16[256,2048]{1,0:T(8,128)(2,1)S(1)}, bf16[256,2048]{1,0:T(8,128)(2,1)S(1)}, u32[]{:S(2)}, u32[]{:S(2)}) collective-permute-start(bf16[256,2048]{1,0:T(8,128)(2,1)S(1)} %copy-done.77), channel_id=1, source_target_pairs={{0,1},{1,0},{2,3},{3,2},{4,5},{5,4},{6,7},{7,6},{8,9},{9,8},{10,11... | collective-permute-start | bytes 3145736 | tf_op jit(solution)/shard_map/ppermute | solution.py:521
  423.6 28.7 %collective-permute-start.55 = (bf16[256,2048]{1,0:T(8,128)(2,1)}, bf16[256,2048]{1,0:T(8,128)(2,1)S(1)}, u32[]{:S(2)}, u32[]{:S(2)}) collective-permute-start(bf16[256,2048]{1,0:T(8,128)(2,1)} %collective-permute-done.53.refs_2_.refs_13_), channel_id=1, source_target_pairs={{0,1},{1,0},{2,3},{3,2},{4,5},{5,4},{6,7},{7,6},{8,9},{9,8},{10,11... | collective-permute-start | bytes 3145736 | tf_op jit(solution)/shard_map/ppermute | solution.py:521
  423.7 29.3 %collective-permute-start.56 = (bf16[256,2048]{1,0:T(8,128)(2,1)}, bf16[256,2048]{1,0:T(8,128)(2,1)}, u32[]{:S(2)}, u32[]{:S(2)}) collective-permute-start(bf16[256,2048]{1,0:T(8,128)(2,1)} %collective-permute-done.54.refs_4_.refs_15_), channel_id=1, source_target_pairs={{0,1},{1,0},{2,3},{3,2},{4,5},{5,4},{6,7},{7,6},{8,9},{9,8},{10,11... | collective-permute-start | bytes 3145736 | tf_op jit(solution)/shard_map/ppermute | solution.py:521
  451.0 39.2 %collective-permute-start.63 = (bf16[128,768]{1,0:T(8,128)(2,1)S(1)}, bf16[128,768]{1,0:T(8,128)(2,1)S(1)}, u32[]{:S(2)}, u32[]{:S(2)}) collective-permute-start(bf16[128,768]{1,0:T(8,128)(2,1)S(1)} %get-tuple-element.390), channel_id=1, source_target_pairs={{0,2},{2,0},{4,6},{6,4},{1,3},{3,1},{5,7},{7,5},{8,10},{10,8},{12,... | collective-permute-start | bytes 589832 | tf_op jit(solution)/shard_map/ppermute | solution.py:517
  452.3 37.8 %collective-permute-start.64 = (bf16[128,768]{1,0:T(8,128)(2,1)S(1)}, bf16[128,768]{1,0:T(8,128)(2,1)S(1)}, u32[]{:S(2)}, u32[]{:S(2)}) collective-permute-start(bf16[128,768]{1,0:T(8,128)(2,1)S(1)} %get-tuple-element.389), channel_id=1, source_target_pairs={{0,4},{2,6},{4,0},{6,2},{1,5},{3,7},{5,1},{7,3},{8,12},{10,14},{12... | collective-permute-start | bytes 589832 | tf_op jit(solution)/shard_map/ppermute | solution.py:517
  452.9 37.3 %collective-permute-start.65 = (bf16[128,768]{1,0:T(8,128)(2,1)S(1)}, bf16[128,768]{1,0:T(8,128)(2,1)S(1)}, u32[]{:S(2)}, u32[]{:S(2)}) collective-permute-start(bf16[128,768]{1,0:T(8,128)(2,1)S(1)} %get-tuple-element.388), channel_id=1, source_target_pairs={{0,6},{2,4},{4,2},{6,0},{1,7},{3,5},{5,3},{7,1},{8,14},{10,12},{12... | collective-permute-start | bytes 589832 | tf_op jit(solution)/shard_map/ppermute | solution.py:517
  456.3 34.6 %collective-permute-start.66 = (bf16[128,2048]{1,0:T(8,128)(2,1)}, bf16[128,2048]{1,0:T(8,128)(2,1)}, u32[]{:S(2)}, u32[]{:S(2)}) collective-permute-start(bf16[128,2048]{1,0:T(8,128)(2,1)} %get-tuple-element.257), channel_id=1, source_target_pairs={{0,2},{2,0},{4,6},{6,4},{1,3},{3,1},{5,7},{7,5},{8,10},{10,8},{12,... | collective-permute-start | bytes 1572872 | tf_op jit(solution)/shard_map/ppermute | solution.py:517
  457.3 33.6 %collective-permute-start.67 = (bf16[128,2048]{1,0:T(8,128)(2,1)}, bf16[128,2048]{1,0:T(8,128)(2,1)}, u32[]{:S(2)}, u32[]{:S(2)}) collective-permute-start(bf16[128,2048]{1,0:T(8,128)(2,1)} %get-tuple-element.258), channel_id=1, source_target_pairs={{0,4},{2,6},{4,0},{6,2},{1,5},{3,7},{5,1},{7,3},{8,12},{10,14},{12... | collective-permute-start | bytes 1572872 | tf_op jit(solution)/shard_map/ppermute | solution.py:517
  530.4 51.6 %collective-permute-start.72 = (bf16[128,2048]{1,0:T(8,128)(2,1)S(1)}, bf16[128,2048]{1,0:T(8,128)(2,1)S(1)}, u32[]{:S(2)}, u32[]{:S(2)}) collective-permute-start(bf16[128,2048]{1,0:T(8,128)(2,1)S(1)} %add_convert_fusion.2), channel_id=1, source_target_pairs={{0,4},{2,6},{4,0},{6,2},{1,5},{3,7},{5,1},{7,3},{8,12},{10,14},{12... | collective-permute-start | bytes 1572872 | tf_op jit(solution)/shard_map/ppermute | solution.py:517
  544.3 20.7 %collective-permute-start.78 = (bf16[128,2048]{1,0:T(8,128)(2,1)S(1)}, bf16[128,2048]{1,0:T(8,128)(2,1)S(1)}, u32[]{:S(2)}, u32[]{:S(2)}) collective-permute-start(bf16[128,2048]{1,0:T(8,128)(2,1)S(1)} %add_convert_fusion), channel_id=1, source_target_pairs={{0,4},{2,6},{4,0},{6,2},{1,5},{3,7},{5,1},{7,3},{8,12},{10,14},{12... | collective-permute-start | bytes 1572872 | tf_op jit(solution)/shard_map/ppermute | solution.py:517
  547.0 19.4 %collective-permute-start.77 = (bf16[128,2048]{1,0:T(8,128)(2,1)S(1)}, bf16[128,2048]{1,0:T(8,128)(2,1)S(1)}, u32[]{:S(2)}, u32[]{:S(2)}) collective-permute-start(bf16[128,2048]{1,0:T(8,128)(2,1)S(1)} %add_convert_fusion.1), channel_id=1, source_target_pairs={{0,2},{2,0},{4,6},{6,4},{1,3},{3,1},{5,7},{7,5},{8,10},{10,8},{12,... | collective-permute-start | bytes 1572872 | tf_op jit(solution)/shard_map/ppermute | solution.py:517
  547.7 25.4 %collective-permute-start.74 = (bf16[128,2048]{1,0:T(8,128)(2,1)S(1)}, bf16[128,2048]{1,0:T(8,128)(2,1)S(1)}, u32[]{:S(2)}, u32[]{:S(2)}) collective-permute-start(bf16[128,2048]{1,0:T(8,128)(2,1)S(1)} %copy-done.87), channel_id=1, source_target_pairs={{0,2},{2,0},{4,6},{6,4},{1,3},{3,1},{5,7},{7,5},{8,10},{10,8},{12,... | collective-permute-start | bytes 1572872 | tf_op jit(solution)/shard_map/ppermute | solution.py:517
  549.1 26.3 %collective-permute-start.79 = (bf16[128,2048]{1,0:T(8,128)(2,1)S(1)}, bf16[128,2048]{1,0:T(8,128)(2,1)S(1)}, u32[]{:S(2)}, u32[]{:S(2)}) collective-permute-start(bf16[128,2048]{1,0:T(8,128)(2,1)S(1)} %copy-done.86), channel_id=1, source_target_pairs={{0,4},{2,6},{4,0},{6,2},{1,5},{3,7},{5,1},{7,3},{8,12},{10,14},{12... | collective-permute-start | bytes 1572872 | tf_op jit(solution)/shard_map/ppermute | solution.py:517
  565.0 17.0 %collective-permute-start.71 = (bf16[128,2048]{1,0:T(8,128)(2,1)S(1)}, bf16[128,2048]{1,0:T(8,128)(2,1)S(1)}, u32[]{:S(2)}, u32[]{:S(2)}) collective-permute-start(bf16[128,2048]{1,0:T(8,128)(2,1)S(1)} %add_convert_fusion.3), channel_id=1, source_target_pairs={{0,2},{2,0},{4,6},{6,4},{1,3},{3,1},{5,7},{7,5},{8,10},{10,8},{12,... | collective-permute-start | bytes 1572872 | tf_op jit(solution)/shard_map/ppermute | solution.py:517
  587.8 35.9 %collective-permute-start.80 = (bf16[256,2048]{1,0:T(8,128)(2,1)}, bf16[256,2048]{1,0:T(8,128)(2,1)}, u32[]{:S(2)}, u32[]{:S(2)}) collective-permute-start(bf16[256,2048]{1,0:T(8,128)(2,1)} %settle.7), channel_id=1, source_target_pairs={{0,1},{1,0},{2,3},{3,2},{4,5},{5,4},{6,7},{7,6},{8,9},{9,8},{10,11... | collective-permute-start | bytes 3145736 | tf_op jit(solution)/shard_map/ppermute | solution.py:521
  587.8 42.9 %collective-permute-start.81 = (f32[256,2048]{1,0:T(8,128)S(1)}, f32[256,2048]{1,0:T(8,128)}, u32[]{:S(2)}, u32[]{:S(2)}) collective-permute-start(f32[256,2048]{1,0:T(8,128)S(1)} %copy-done.2), channel_id=1, source_target_pairs={{0,1},{1,0},{2,3},{3,2},{4,5},{5,4},{6,7},{7,6},{8,9},{9,8},{10,11... | collective-permute-start | bytes 6291464 | tf_op jit(solution)/shard_map/ppermute | solution.py:521
  (141 other events, 1307.6 us)
Sparse Core Ops, SparseCore 0:
  31.0 63.8 all-gather.3
  97.0 113.9 all-gather.7
  212.6 61.7 all-gather.5
  288.6 61.6 reduce-scatter.3
  374.7 112.1 reduce-scatter.5
  529.0 70.9 reduce-scatter.7

commit v3 on v2

--- a/solution.py
+++ b/solution.py
@@ -13,7 +13,8 @@
 THETA = 1000000.0
 CTX = 4
 LIMIT = 56 * 2**20
-TILE = 256
+TILE = 512
+CHUNK = 512
 
 
 def _dot(a, b, dims):
@@ -32,20 +33,41 @@
     return [pl.BlockSpec(memory_space=pltpu.VMEM)] * count
 
 
-def _forward_kernel(heads, scale, info, *refs):
-    pieces = refs[:-13]
-    (weight_ref, cos_ref, sin_ref, qg_ref, kg_ref, proj_ref, low_ref, mixed_ref, mlow_ref, rtot_ref, q_s, k_s, v_s) = refs[
-        -13:
-    ]
+def _fetch(pairs, sem):
+    copies = [pltpu.make_async_copy(source, target, sem.at[i]) for i, (source, target) in enumerate(pairs)]
+    for copy in copies:
+        copy.start()
+    return copies
+
+
+def _forward_kernel(heads, scale, count, info, *refs):
+    pieces, refs = refs[:count], refs[count:]
+    weight_hbm, cos_hbm, sin_hbm, qg_ref, kg_ref, proj_hbm, low_hbm, mlow_ref, rtot_ref = refs[:9]
+    x_s, weight_s, cos_ref, sin_ref, proj_ref, low_ref, q_s, k_s, v_s, sem, out_sem = refs[9:]
     hd = cos_ref.shape[1]
     rows = cos_ref.shape[0]
     cols = proj_ref.shape[1]
     factor = scale * math.log2(math.e)
-
-    for piece, start in zip(pieces, _starts(pieces)):
-        proj_ref[start : start + piece.shape[0], :] = _dot(
-            piece[...], weight_ref[:, :cols], ((1,), (0,))
-        )
+    starts = _starts(pieces)
+
+    copies = _fetch(
+        [(weight_hbm, weight_s)]
+        + [(p, x_s.at[pl.ds(at, p.shape[0])]) for p, at in zip(pieces, starts)]
+        + [(cos_hbm, cos_ref), (sin_hbm, sin_ref)],
+        sem,
+    )
+    copies[0].wait()
+    done = 0
+    for i, (piece, start) in enumerate(zip(pieces, starts)):
+        copies[i + 1].wait()
+        end = start + piece.shape[0]
+        if end - done >= CHUNK:
+            proj_ref[done:end, :] = _dot(x_s[done:end, :], weight_s[:, :cols], ((1,), (0,)))
+            done = end
+    copies[-2].wait()
+    copies[-1].wait()
+    proj_out = pltpu.make_async_copy(proj_ref, proj_hbm, out_sem.at[0])
+    proj_out.start()
 
     @pl.loop(0, rows // BLK)
     def _(block):
@@ -66,6 +88,8 @@
         low_ref[here, (heads + 1) * hd :] = val
         v_s[here, :] = val
 
+    low_out = pltpu.make_async_copy(low_ref, low_hbm, out_sem.at[1])
+    low_out.start()
     length = info[rows // BLK]
     per = TILE // BLK
 
@@ -109,9 +133,11 @@
                 at = pl.ds(pl.multiple_of(info[i * per + b] * BLK, BLK), BLK)
                 cut = slice(h * TILE + b * BLK, h * TILE + (b + 1) * BLK)
                 lanes = slice(h * hd, (h + 1) * hd)
-                mixed_ref[at, lanes] = mixed[cut]
                 mlow_ref[at, lanes] = mixed[cut].astype(jnp.bfloat16)
                 rtot_ref[at, lanes] = recip[cut]
+
+    proj_out.wait()
+    low_out.wait()
 
 
 def attend_forward(info, pieces, weight, cosine, sine, query_gain, key_gain, heads):
@@ -119,21 +145,29 @@
     cols = (heads + 2) * hd
     width = heads * hd
     pairs = rows * rows // 2 * heads
+    anywhere = pl.BlockSpec(memory_space=pl.ANY)
     return pl.pallas_call(
-        functools.partial(_forward_kernel, heads, hd**-0.5),
+        functools.partial(_forward_kernel, heads, hd**-0.5, len(pieces)),
         out_shape=(
             jax.ShapeDtypeStruct((rows, cols), jnp.float32),
             jax.ShapeDtypeStruct((rows, cols), jnp.bfloat16),
-            jax.ShapeDtypeStruct((rows, width), jnp.float32),
             jax.ShapeDtypeStruct((rows, width), jnp.bfloat16),
             jax.ShapeDtypeStruct((rows, width), jnp.float32),
         ),
-        in_specs=[pl.BlockSpec(memory_space=pltpu.SMEM)] + _whole(len(pieces) + 5),
-        out_specs=_whole(5),
+        in_specs=[pl.BlockSpec(memory_space=pltpu.SMEM)] + [anywhere] * (len(pieces) + 3) + _whole(2),
+        out_specs=[anywhere] * 2 + _whole(2),
         scratch_shapes=[
+            pltpu.VMEM((rows, weight.shape[0]), jnp.bfloat16),
+            pltpu.VMEM(weight.shape, jnp.bfloat16),
+            pltpu.VMEM((rows, hd), jnp.float32),
+            pltpu.VMEM((rows, hd), jnp.float32),
+            pltpu.VMEM((rows, cols), jnp.float32),
+            pltpu.VMEM((rows, cols), jnp.bfloat16),
             pltpu.VMEM((heads, rows, hd), jnp.bfloat16),
             pltpu.VMEM((rows, hd), jnp.bfloat16),
             pltpu.VMEM((rows, hd), jnp.bfloat16),
+            pltpu.SemaphoreType.DMA((len(pieces) + 3,)),
+            pltpu.SemaphoreType.DMA((2,)),
         ],
         compiler_params=pltpu.CompilerParams(vmem_limit_bytes=LIMIT),
         cost_estimate=pl.CostEstimate(
@@ -145,30 +179,52 @@
     )(info, *pieces, weight, cosine, sine, query_gain, key_gain)
 
 
-def _backward_kernel(heads, scale, info, *refs):
-    pieces = refs[:-15]
-    (weight_ref, proj_ref, low_ref, mixed_ref, rtot_ref, cos_ref, sin_ref, qg_ref, kg_ref, out_ref, gain_ref, gacc_s, dq_s, dk_s, dv_s) = refs[
-        -15:
-    ]
+def _backward_kernel(heads, scale, count, info, *refs):
+    pieces, refs = refs[:count], refs[count:]
+    inputs, qg_ref, kg_ref, out_ref, gain_ref = refs[:7], refs[7], refs[8], refs[9], refs[10]
+    x_s, weight_ref, low_ref, mixed_ref, rtot_ref, proj_ref, cos_ref, sin_ref = refs[11:19]
+    gacc_s, dq_s, dk_s, dv_s, sem = refs[19:]
     hd = cos_ref.shape[1]
     rows = cos_ref.shape[0]
     factor = scale * math.log2(math.e)
     length = info[rows // BLK]
     per = TILE // BLK
-    cols = (heads + 2) * hd
-
+    starts = _starts(pieces)
+
+    targets = (weight_ref, low_ref, mixed_ref, rtot_ref, proj_ref, cos_ref, sin_ref)
+    loads = list(zip(inputs, targets))
+    copies = _fetch(
+        loads[:1]
+        + [(p, x_s.at[pl.ds(at, p.shape[0])]) for p, at in zip(pieces, starts)]
+        + [loads[i] for i in (2, 3, 1, 4, 5, 6)],
+        sem,
+    )
     dk_s[...] = jnp.zeros_like(dk_s)
     dv_s[...] = jnp.zeros_like(dv_s)
     gain_ref[...] = jnp.zeros_like(gain_ref)
-
-    for piece, start in zip(pieces, _starts(pieces)):
-        grad = _dot(piece[...], weight_ref[:, cols:], ((1,), (0,)))
-        at = slice(start, start + piece.shape[0])
+    copies[0].wait()
+    done = 0
+    for i, (piece, start) in enumerate(zip(pieces, starts)):
+        copies[i + 1].wait()
+        end = start + piece.shape[0]
+        if end - done >= CHUNK:
+            grad = _dot(x_s[done:end, :], weight_ref[:, (heads + 2) * hd :], ((1,), (0,)))
+            for h in range(heads):
+                dq_s[h, done:end, :] = grad[:, h * hd : (h + 1) * hd]
+            done = end
+    copies[count + 1].wait()
+    copies[count + 2].wait()
+
+    @pl.loop(0, rows // BLK)
+    def _(block):
+        at = pl.ds(pl.multiple_of(block * BLK, BLK), BLK)
         for h in range(heads):
             lanes = slice(h * hd, (h + 1) * hd)
-            g = grad[:, lanes] * rtot_ref[at, lanes]
+            g = dq_s[h, at, :] * rtot_ref[at, lanes]
             gacc_s[h, at, :] = g.astype(jnp.bfloat16)
-            dq_s[h, at, :] = g * mixed_ref[at, lanes]
+            dq_s[h, at, :] = g * mixed_ref[at, lanes].astype(jnp.float32)
+
+    copies[count + 3].wait()
 
     def spots(tile):
         return [pl.ds(pl.multiple_of(info[tile * per + b] * BLK, BLK), BLK) for b in range(per)]
@@ -235,6 +291,9 @@
             for h in range(heads):
                 dq_s[h, at, :] = jnp.zeros((BLK, hd), jnp.float32)
 
+    for copy in copies[count + 4 :]:
+        copy.wait()
+
     @pl.loop(0, rows // BLK)
     def _(block):
         finish(block)
@@ -245,19 +304,24 @@
 ):
     rows, hd = cosine.shape
     pairs = rows * rows // 2 * heads
+    anywhere = pl.BlockSpec(memory_space=pl.ANY)
+    inputs = (weight, low, mixed, rtot, proj, cosine, sine)
     return pl.pallas_call(
-        functools.partial(_backward_kernel, heads, hd**-0.5),
+        functools.partial(_backward_kernel, heads, hd**-0.5, len(pieces)),
         out_shape=(
             jax.ShapeDtypeStruct((rows, (heads + 2) * hd), jnp.bfloat16),
             jax.ShapeDtypeStruct((8, hd), jnp.float32),
         ),
-        in_specs=[pl.BlockSpec(memory_space=pltpu.SMEM)] + _whole(len(pieces) + 9),
+        in_specs=[pl.BlockSpec(memory_space=pltpu.SMEM)] + [anywhere] * (len(pieces) + 7) + _whole(2),
         out_specs=_whole(2),
-        scratch_shapes=[
+        scratch_shapes=[pltpu.VMEM((rows, weight.shape[0]), jnp.bfloat16)]
+        + [pltpu.VMEM(v.shape, v.dtype) for v in inputs]
+        + [
             pltpu.VMEM((heads, rows, hd), jnp.bfloat16),
             pltpu.VMEM((heads, rows, hd), jnp.float32),
             pltpu.VMEM((rows, hd), jnp.float32),
             pltpu.VMEM((rows, hd), jnp.float32),
+            pltpu.SemaphoreType.DMA((len(pieces) + 7,)),
         ],
         compiler_params=pltpu.CompilerParams(vmem_limit_bytes=LIMIT),
         cost_estimate=pl.CostEstimate(
@@ -266,7 +330,7 @@
             transcendentals=pairs,
         ),
         name="attend_backward",
-    )(info, *pieces, weight, proj, low, mixed, rtot, cosine, sine, query_gain, key_gain)
+    )(info, *pieces, *inputs, query_gain, key_gain)
 
 
 def _expand_kernel(counts, *refs):
@@ -286,8 +350,8 @@
                 upper = _dot(piece[...], up_w[...], ((1,), (0,)))
                 sigma = 1.0 / (1.0 + jnp.exp(-gate))
                 silu = gate * sigma
-                slope_ref[at, :] = upper * sigma * (1.0 + gate - silu)
-                silu_ref[at, :] = silu
+                slope_ref[at, :] = (upper * sigma * (1.0 + gate - silu)).astype(jnp.bfloat16)
+                silu_ref[at, :] = silu.astype(jnp.bfloat16)
                 inner_ref[at, :] = (silu * upper).astype(jnp.bfloat16)
 
 
@@ -302,8 +366,8 @@
         functools.partial(_expand_kernel, [len(group) for group in groups]),
         grid=(len(groups), steps),
         out_shape=(
-            jax.ShapeDtypeStruct((rows, units), jnp.float32),
-            jax.ShapeDtypeStruct((rows, units), jnp.float32),
+            jax.ShapeDtypeStruct((rows, units), jnp.bfloat16),
+            jax.ShapeDtypeStruct((rows, units), jnp.bfloat16),
             jax.ShapeDtypeStruct((rows, units), jnp.bfloat16),
         ),
         in_specs=[
@@ -332,8 +396,8 @@
     for piece, start in zip(pieces, _starts(pieces)):
         at = slice(start, start + piece.shape[0])
         grad = _dot(piece[...], weight[...], ((1,), (0,)))
-        dgate_ref[at, :] = (grad * slope_ref[at, :]).astype(jnp.bfloat16)
-        dup_ref[at, :] = (grad * silu_ref[at, :]).astype(jnp.bfloat16)
+        dgate_ref[at, :] = (grad * slope_ref[at, :].astype(jnp.float32)).astype(jnp.bfloat16)
+        dup_ref[at, :] = (grad * silu_ref[at, :].astype(jnp.float32)).astype(jnp.bfloat16)
 
 
 def feed_back(pieces, weight, slope, silu, step=256):
@@ -454,51 +518,79 @@
     )(*values)
 
 
-def _settle_kernel(mode, *refs):
+def _settle_kernel(mode, twice, place, *refs):
     total_ref, x_top, x_bottom, y_top, y_bottom = refs[:5]
     rest = refs[5:]
-    rows = total_ref.shape[0]
-    step = 32
-    for start in range(0, rows, step):
-        here = slice(start, start + step)
-        upper = start < rows // 2
-        there = here if upper else slice(start - rows // 2, start - rows // 2 + step)
-        by_x, by_y = (x_top, y_top) if upper else (x_bottom, y_bottom)
-        total = total_ref[here, :] + by_x[there, :].astype(jnp.float32) + by_y[there, :].astype(jnp.float32)
-        if mode == "add":
-            base_ref, out_ref = rest
-            out_ref[here, :] = (base_ref[here, :] + total).astype(out_ref.dtype)
-        elif mode == "norm":
-            base_ref, out_ref, hat_ref = rest
-            hidden = base_ref[here, :].astype(jnp.float32) + total
-            out_ref[here, :] = hidden
-            rstd = lax.rsqrt(jnp.mean(hidden * hidden, axis=1, keepdims=True) + EPS)
-            hat_ref[here, :] = (hidden * rstd).astype(jnp.bfloat16)
-        else:
-            source_ref, base_ref = rest[:2]
-            source = source_ref[here, :].astype(jnp.float32)
-            rstd = lax.rsqrt(jnp.mean(source * source, axis=1, keepdims=True) + EPS)
-            hat = source * rstd
-            grad = total - hat * jnp.mean(total * hat, axis=1, keepdims=True)
-            out = base_ref[here, :].astype(jnp.float32) + rstd * grad
-            rest[2][here, :] = out
-            if len(rest) > 3:
-                rest[3][here, :] = out.astype(jnp.bfloat16)
-
-
-def settle(mode, sums, others, types):
+    if twice:
+        rest, full_ref = rest[:-1], rest[-1]
+
+    def finish(by_x, by_y):
+        step = 16
+        for start in range(0, total_ref.shape[0], step):
+            here = slice(start, start + step)
+            total = total_ref[here, :] + by_x[here, :].astype(jnp.float32) + by_y[here, :].astype(jnp.float32)
+            if mode == "add":
+                base_ref, out_ref = rest
+                out = (base_ref[here, :] + total).astype(out_ref.dtype)
+                out_ref[here, :] = out
+            elif mode == "norm":
+                base_ref, out_ref, hat_ref = rest
+                hidden = base_ref[here, :].astype(jnp.float32) + total
+                out_ref[here, :] = hidden
+                rstd = lax.rsqrt(jnp.mean(hidden * hidden, axis=1, keepdims=True) + EPS)
+                hat_ref[here, :] = (hidden * rstd).astype(jnp.bfloat16)
+            else:
+                source_ref, base_ref = rest[:2]
+                source = source_ref[here, :].astype(jnp.float32)
+                rstd = lax.rsqrt(jnp.mean(source * source, axis=1, keepdims=True) + EPS)
+                hat = source * rstd
+                grad = total - hat * jnp.mean(total * hat, axis=1, keepdims=True)
+                out = base_ref[here, :].astype(jnp.float32) + rstd * grad
+                rest[2][here, :] = out
+                if len(rest) > 3:
+                    rest[3][here, :] = out.astype(jnp.bfloat16)
+            if twice:
+                full_ref[here, :] = out
+
+    upper = pl.program_id(0) < pl.num_programs(0) // 2
+
+    @pl.when(upper)
+    def _():
+        finish(x_top, y_top)
+
+    @pl.when(jnp.logical_not(upper))
+    def _():
+        finish(x_bottom, y_bottom)
+
+
+def settle(mode, sums, others, types, core=None, steps=4):
     rows, width = sums[0].shape
+    block = (rows // steps, width)
+    half = steps // 2
+    straight = pl.BlockSpec(block, lambda i, place: (i, 0))
+    first = pl.BlockSpec(block, lambda i, place: (jnp.minimum(i, half - 1), 0))
+    second = pl.BlockSpec(block, lambda i, place: (jnp.maximum(i - half, 0), 0))
+    shapes = [jax.ShapeDtypeStruct((rows, width), t) for t in types]
+    out_specs = [straight] * len(types)
+    if core is not None:
+        shapes.append(jax.ShapeDtypeStruct((2 * rows, width), types[0]))
+        out_specs.append(pl.BlockSpec(block, lambda i, place: (place[0] * steps + i, 0)))
+    place = jnp.zeros((1,), jnp.int32) if core is None else core.astype(jnp.int32).reshape(1)
     return pl.pallas_call(
-        functools.partial(_settle_kernel, mode),
-        out_shape=[jax.ShapeDtypeStruct((rows, width), t) for t in types],
-        in_specs=_whole(5 + len(others)),
-        out_specs=_whole(len(types)),
+        functools.partial(_settle_kernel, mode, core is not None),
+        out_shape=shapes,
+        grid_spec=pltpu.PrefetchScalarGridSpec(
+            num_scalar_prefetch=1,
+            grid=(steps,),
+            in_specs=[straight, first, second, first, second] + [straight] * len(others),
+            out_specs=out_specs,
+        ),
         compiler_params=pltpu.CompilerParams(vmem_limit_bytes=LIMIT),
         cost_estimate=pl.CostEstimate(
             flops=rows * width * 10, bytes_accessed=rows * width * 20, transcendentals=rows
         ),
         name="settle",
-    )(*sums, *others)
+    )(place, *sums, *others)
 
 
 def low(values):
@@ -537,18 +629,22 @@
     return other_core(by_x), other_core(by_y), across(by_x[:half], 2), across(by_y[half:], 1)
 
 
-def gather_rows(own, beside=()):
+def gather_rows(own, beside=(), beside_far=()):
     own_other, by_x, by_y = gather_near(own)
     by_x, by_y = after((by_x, by_y), beside)
     x_other, y_other, far_top, far_bottom = gather_far(by_x, by_y)
+    far_top, far_bottom = after((far_top, far_bottom), beside_far)
     far = [far_top, far_bottom, other_core(far_top), other_core(far_bottom)]
     return [own, own_other, by_x, x_other, by_y, y_other] + far
 
 
-def scatter_rows(lefts, weight, column, beside=()):
+def scatter_rows(lefts, weight, column):
     size = lefts[0].shape[0] // (2 * CTX)
     half = size // 2
-    far_there = rows_product(lefts, weight, column, (7,), [(size, jnp.bfloat16)], [(0, 0, size)])[0]
+    wide_step = weight.shape[0] // 2
+    far_there = rows_product(
+        lefts, weight, column, (7,), [(size, jnp.bfloat16)], [(0, 0, size)], step=wide_step
+    )[0]
     rest_there = rows_product(
         lefts,
         after(weight, far_there),
@@ -567,10 +663,8 @@
         [(half, jnp.bfloat16)] * 2,
         [(0, 0, half), (1, 0, half)],
         far_there,
+        step=wide_step,
     )
-    far_top, far_bottom = after((far_top, far_bottom), beside)
-    to_y = across(far_top, 1)
-    to_x = across(far_bottom, 2)
     own, x_top, x_bottom, y_top, y_bottom = rows_product(
         lefts,
         after(weight, far_top),
@@ -581,7 +675,14 @@
         [(0, 0, size)] + [(i, 0, half) for i in range(1, 5)],
         rest_there,
     )
-    return [own, across(x_top, 1), across(y_bottom, 2), to_x, to_y, x_bottom, y_top], far_top
+    return far_top, far_bottom, own, x_top, x_bottom, y_top, y_bottom
+
+
+def scatter_send(parts):
+    far_top, far_bottom, own, x_top, x_bottom, y_top, y_bottom = parts
+    to_y = across(far_top, 1)
+    to_x = across(far_bottom, 2)
+    return own, across(x_top, 1), across(y_bottom, 2), to_x, to_y, x_bottom, y_top
 
 
 def scatter_end(parts, beside=()):
@@ -609,6 +710,17 @@
 
 def sum_stages(values):
     return lax.psum_scatter(values, "fsdp", scatter_dimension=0, tiled=True)
+
+
+def sum_small(values):
+    count = lax.axis_size("fsdp")
+    if count & (count - 1):
+        return lax.psum(values, "fsdp")
+    bit = 1
+    while bit < count:
+        values = values + lax.ppermute(values, "fsdp", [(i, i ^ bit) for i in range(count)])
+        bit *= 2
+    return values
 
 
 def on_device(
@@ -678,113 +790,120 @@
     own = lax.dynamic_slice_in_dim(tokens, core * half_rows, half_rows, 0)
     inputs = wide(own)
     rstd = lax.rsqrt(jnp.mean(inputs * inputs, axis=1, keepdims=True) + EPS)
-    normed = gather_rows(after(low(inputs * rstd), dealt), (info, cosine, sine))
-
+    normed_own = after(low(inputs * rstd), dealt)
+    other, by_x, by_y = gather_near(normed_own)
+    by_x, by_y = after((by_x, by_y), info, cosine, sine)
+    feed_scaled = [low(wide(after(w, dealt)) * feed_scale) for w in (w_gate, w_up)]
+    down_turned = after(w_down, dealt).T
+    by_x, by_y = after((by_x, by_y), feed_scaled, down_turned)
     feed_dealt = deal_out(
-        [low(wide(after(w, normed[2:6])) * feed_scale) for w in (w_gate, w_up)],
-        spot,
-        (units, units),
-        1,
+        [after(w, by_x) for w in feed_scaled + [down_turned]], spot, (units,) * 3, 1
     )
-    feed_weight = gather_stages(in_order(feed_dealt, spot, 0))
-    down_dealt = deal_out([after(w_down, feed_dealt).T], spot, (units,), 1)
+    x_other, y_other, far_top, far_bottom = gather_far(by_x, by_y)
+    far = [far_top, far_bottom, other_core(far_top), other_core(far_bottom)]
+    normed = [normed_own, other, by_x, x_other, by_y, y_other] + far
+    feed_weight = gather_stages(in_order([v[:, : 2 * units] for v in feed_dealt], spot, 0))
+    down_weight = gather_stages(in_order([v[:, 2 * units :] for v in feed_dealt], spot, 0))
 
     valid = positions[:half_rows] < lengths[0]
     seed = lax.dynamic_slice_in_dim(cotangent, core * half_rows, half_rows, 0)
     seed = jnp.where(valid[:, None], seed, 0).astype(jnp.bfloat16)
 
-    seed_own, seed_x, seed_y = gather_near(after(seed, normed[2:]))
-
-    proj, qkv, mixed, mixed_low, recip = attend_forward(
+    seed_other, seed_x, seed_y = gather_near(after(seed, far_top, far_bottom))
+    proj, qkv, mixed_low, recip = attend_forward(
         info, normed, attn_weight, cosine, sine, query_scale, key_scale, heads
     )
-    mixed_low, seed_x, seed_y, down_dealt = lax.optimization_barrier(
-        (mixed_low, seed_x, seed_y, down_dealt)
-    )
-    down_weight = gather_stages(in_order(down_dealt, spot, 0))
-    seed_rest = gather_far(seed_x, seed_y)
-    parts, _ = scatter_rows(
-        [mixed_low], attn_weight, proj_cols // query_cols, (seed_own, seed_rest)
-    )
+    out_column = proj_cols // query_cols
+    mixed_low, seed_x, seed_y = lax.optimization_barrier((mixed_low, seed_x, seed_y))
+    seed_far = gather_far(seed_x, seed_y)
+    parts = list(scatter_rows([mixed_low], attn_weight, out_column))
+    parts[0], seed_far = lax.optimization_barrier((parts[0], seed_far))
+    parts = scatter_send(parts)
     sums, _ = scatter_end(parts)
-    seed_far = [other_core(v) for v in after(seed_rest[2:], parts[0])]
-    seeds = [seed, seed_own, seed_x, seed_rest[0], seed_y, *seed_rest[1:]] + seed_far
-    sums = after(sums, seed_far)
+    seeds = [seed, seed_other, seed_x, seed_far[0], seed_y, *seed_far[1:]]
+    seeds += [other_core(v) for v in seed_far[2:]]
     hidden, hat_two = settle("norm", sums, (own,), (jnp.float32, jnp.bfloat16))
 
+    total = local_rows * CTX
     other, by_x, by_y = gather_near(hat_two)
-    filled = feed_expand([[hat_two, other]], 0, feed_weight, local_rows * CTX)
-    by_x, by_y = after((by_x, by_y), filled[0])
     x_other, y_other, far_top, far_bottom = gather_far(by_x, by_y)
-    filled = feed_expand([[by_x, x_other], [by_y, y_other]], 1, feed_weight, local_rows * CTX, filled)
+    filled = feed_expand([[hat_two, other]], 0, feed_weight, total)
+    filled = feed_expand([[by_x, x_other], [by_y, y_other]], 1, feed_weight, total, filled)
     far = list(after((far_top, far_bottom), filled[0]))
     far += [other_core(v) for v in far]
-    slope, silu, inner = feed_expand([far], 3, feed_weight, local_rows * CTX, filled)
     normed_two = [hat_two, other, by_x, x_other, by_y, y_other] + far
+    slope, silu, inner = feed_expand([far], 3, feed_weight, total, filled)
     grad_down = weight_terms([(seeds, [inner])])
     down_weight, grad_down = lax.optimization_barrier((down_weight, grad_down))
     grad_down = sum_stages(grad_down)
     dgate, dup = feed_back(seeds, down_weight, slope, silu)
-    parts, _ = scatter_rows([dgate, dup], feed_weight, 0)
-    sums, sent = scatter_end(parts)
+    sums, sent = scatter_end(scatter_send(scatter_rows([dgate, dup], feed_weight, 0)))
     grad_feed = weight_terms([(normed_two, [after(dgate, sent), dup])])
     sums, grad_feed = lax.optimization_barrier((sums, grad_feed))
     grad_feed = sum_stages(after(grad_feed, grad_down))
     grad_hidden, grad_attn = settle("back", sums, (hidden, seed), (jnp.float32, jnp.bfloat16))
 
-    feed_parts, _ = scatter_rows([after(inner, grad_attn)], down_weight, 0)
-    grad_attn = gather_rows(grad_attn)
-    grad_attn = after(grad_attn, feed_parts[0], feed_parts[5])
+    feed_parts = scatter_rows([after(inner, grad_attn)], down_weight, 0)
+    grad_attn = gather_rows(grad_attn, feed_parts[:2], feed_parts[2])
+    feed_parts = scatter_send(after(feed_parts, grad_attn[6:8]))
     grad_proj, gain_sums = attend_backward(
-        info, grad_attn, attn_weight, proj, qkv, mixed, recip, cosine, sine, query_scale, key_scale, heads
+        info,
+        grad_attn,
+        attn_weight,
+        proj,
+        qkv,
+        mixed_low,
+        recip,
+        cosine,
+        sine,
+        query_scale,
+        key_scale,
+        heads,
     )
-    down_pieces = dealt_rows(grad_down)
-    grad_proj, down_pieces, feed_parts = lax.optimization_barrier(
-        (grad_proj, down_pieces, feed_parts)
-    )
+    grad_proj, feed_parts = lax.optimization_barrier((grad_proj, feed_parts))
+    down_pieces = dealt_rows(after(grad_down, grad_proj))
     grad_attn_w = weight_terms([(normed, [grad_proj]), (grad_attn, [mixed_low])])
-    parts, far = scatter_rows([grad_proj], after(attn_weight, grad_attn_w), 0)
-    feed_sums, _ = scatter_end(feed_parts, far)
-    sums, sent = scatter_end(parts, feed_sums[0])
+    weight = after(attn_weight, grad_attn_w)
     grad_attn_w = sum_stages(after(grad_attn_w, grad_feed))
-    (grad_tokens_half,) = settle("back", sums, (own, grad_hidden), (jnp.float32,))
-    (output_half,) = settle("add", after(feed_sums, grad_tokens_half), (hidden,), (jnp.bfloat16,))
-
-    def whole_rows(values):
-        other = other_core(values)
-        first = core == 0
-        return jnp.concatenate(
-            [jnp.where(first, values, other), jnp.where(first, other, values)], axis=0
-        )
+    feed_sums, feed_sent = scatter_end(feed_parts, down_pieces)
+    feed_pieces = dealt_rows(after(grad_feed, feed_sent))
+    parts = list(scatter_rows([grad_proj], after(weight, feed_sent), 0))
+    parts[0], feed_pieces = lax.optimization_barrier((parts[0], feed_pieces))
+    sums, sent = scatter_end(scatter_send(parts), feed_sums)
+    gain_sums = after(gain_sums, sent)
+    gain_sums = gain_sums + other_core(gain_sums)
+    for bit in (1, 2):
+        gain_sums = gain_sums + across(gain_sums, bit)
+    gain_sums = sum_small(gain_sums)
+    tokens_half, grad_tokens = settle("back", sums, (own, grad_hidden), (jnp.float32,), core)
+    feed_sums = after(feed_sums, tokens_half)
+    output_half, output = settle("add", feed_sums, (hidden,), (jnp.bfloat16,), core)
+
+    def whole_rows(both, half):
+        return lax.dynamic_update_slice_in_dim(both, other_core(half), (1 - core) * half_rows, 0)
 
     def cut(pieces, start, size):
         return wide(in_order([p[:, start : start + size] for p in pieces], spot, 1))
 
     grad_down_w = cut(down_pieces, 0, units).T
-    feed_pieces = dealt_rows(after(grad_feed, sent))
     grad_gate_w = cut(feed_pieces, 0, units)
     grad_up_w = cut(feed_pieces, units, units)
-    proj_pieces = dealt_rows(after(grad_attn_w, grad_gate_w, grad_up_w))
+    output = whole_rows(output, output_half)
+    grad_tokens = whole_rows(grad_tokens, tokens_half)
+    feed_gain = jnp.sum(wide(w_gate) * grad_gate_w + wide(w_up) * grad_up_w, axis=1)
+    feed_gain = feed_gain + other_core(feed_gain)
+    proj_pieces = dealt_rows(grad_attn_w)
     grad_query_w = cut(proj_pieces, 0, query_cols)
     grad_key_w = cut(proj_pieces, query_cols, head_size)
     grad_value_w = cut(proj_pieces, query_cols + head_size, head_size)
     grad_out_w = cut(proj_pieces, proj_cols, query_cols).T
 
-    def gain_part(pairs):
-        return sum(jnp.sum(wide(w) * g, axis=1) for w, g in pairs)
-
-    feed_gain = gain_part(((w_gate, grad_gate_w), (w_up, grad_up_w)))
-    norm_gain = gain_part(((w_query, grad_query_w), (w_key, grad_key_w), (w_value, grad_value_w)))
-    feed_gain = feed_gain + other_core(feed_gain)
+    pairs = ((w_query, grad_query_w), (w_key, grad_key_w), (w_value, grad_value_w))
+    norm_gain = sum(jnp.sum(wide(w) * g, axis=1) for w, g in pairs)
     norm_gain = norm_gain + other_core(norm_gain)
-    gain_sums = after(gain_sums, grad_tokens_half)
-    gain_sums = gain_sums + other_core(gain_sums)
-    for bit in (1, 2):
-        gain_sums = gain_sums + across(gain_sums, bit)
-    gain_sums = lax.psum(gain_sums, "fsdp")
     return (
-        whole_rows(output_half),
-        whole_rows(grad_tokens_half),
+        output,
+        grad_tokens,
         norm_gain,
         grad_query_w * attn_scale,
         grad_key_w * attn_scale,

time: 683 us -> 624 us (0.914)
  blocking collectives: 22.5 us -> 0 us
  Pallas kernels: 268 us -> 251 us
  other arithmetic: 49 us -> 35.3 us
  waiting for transfers between devices: 216 us -> 203 us
  local copies, waits for them, and re-layouts: 30.1 us -> 40 us
    psum x1 -> x0, blocking collectives: 22.5 us -> none  [on_device(): gain_sums = lax.psum(gain_sums, 'fsdp')]
    ppermute x33, waiting for transfers between devices: 33.6 us -> 20.8 us  [other_core(): return lax.ppermute(values, 'tp', [(0, 1), (1, 0)])]
    pallas_call x16, Pallas kernels: 92.9 us -> 83.3 us  [rows_product(): pl.pallas_call(functools.partial(_rows_kernel, len(lefts), len(picks), th...]
    ppermute x60 -> x57, starting transfers between devices: 66.4 us -> 60.1 us  [across(): return lax.ppermute(values, 'ctx', [(i, i ^ bits) for i in range(CTX)])]
    unnamed x186 -> x192, local copies, waits for them, and re-layouts: 20 us -> 22 us
    ppermute x60 -> x57, waiting for transfers between devices: 182 us -> 182 us  [across(): return lax.ppermute(values, 'ctx', [(i, i ^ bits) for i in range(CTX)])]
  transfers between devices with their start and end apart: 99 -> 98, of which waited for: 47 -> 42; matrix products, arithmetic and copies ran while one was open for 8% -> 8% of each run, Pallas kernels for 40% -> 41%
where the time goes in v3:
time: 624 us; the launch traced here: 616 us
  Pallas kernels  251 us (40%)
  waiting for transfers between devices  203 us (33%)
  starting transfers between devices  70.2 us (11%)
  local copies, waits for them, and re-layouts  40 us (6%)
  other arithmetic  35.3 us (6%)
  between operations  16.6 us (3%)
    ppermute x57, waiting for transfers between devices, across(): return lax.ppermute(values, 'ctx', [(i, i ^ bits) for i in range(CTX)])  182 us
    pallas_call x16, Pallas kernels, rows_product(): pl.pallas_call(functools.partial(_rows_kernel, len(lefts), len(picks), th...  83.3 us
    ppermute x57, starting transfers between devices, across(): return lax.ppermute(values, 'ctx', [(i, i ^ bits) for i in range(CTX)])  60.1 us
    pallas_call x3, Pallas kernels, weight_terms(): pl.pallas_call(functools.partial(_terms_kernel, [(len(p), len(o)) for p,...  45.9 us
    pallas_call x1, Pallas kernels, attend_backward(): pl.pallas_call(functools.partial(_backward_kernel, heads, hd ** (-0.5), l...  34 us
    pallas_call x3, Pallas kernels, feed_expand(): pl.pallas_call(functools.partial(_expand_kernel, [len(group) for group in...  28.6 us
    pallas_call x1, Pallas kernels, attend_forward(): pl.pallas_call(functools.partial(_forward_kernel, heads, hd ** (-0.5), le...  23.8 us
    unnamed x192, local copies, waits for them, and re-layouts  22 us
  transfers between devices with their start and end apart: 98, of which 42 were waited for; matrix products, arithmetic and copies ran while one was open for 8% of the time, Pallas kernels for 41%

profile of v3, /device:TPU:0, one launch (start us, length us, event | category | flops | bytes accessed | tf_op | source)
XLA Modules:
  0.0 615.6 jit_solution(4360256546984466966)
XLA Ops:
  20.2 3.7 collective-permute-done.2
  29.1 3.7 fusion.6
  37.9 11.9 %collective-permute-done.3.refs_2_ = bf16[256,2048]{1,0:T(8,128)(2,1)} collective-permute-done((bf16[256,2048]{1,0:T(8,128)(2,1)}, bf16[256,2048]{1,0:T(8,128)(2,1)}, u32[]{:S(2)}, u32[]{:S(2)}) %collective-permute-start.3) | collective-permute-done | bytes 1048608 | tf_op jit(solution)/shard_map/ppermute | solution.py:609
  55.1 12.6 %collective-permute-done.24 = bf16[128,2304]{1,0:T(8,128)(2,1)S(1)} collective-permute-done((bf16[128,2304]{1,0:T(8,128)(2,1)S(1)}, bf16[128,2304]{1,0:T(8,128)(2,1)S(1)}, u32[]{:S(2)}, u32[]{:S(2)}) %collective-permute-start.24) | collective-permute-done | bytes 589856 | tf_op jit(solution)/shard_map/ppermute | solution.py:609
  67.6 9.1 %collective-permute-done.22 = bf16[128,2304]{1,0:T(8,128)(2,1)S(1)} collective-permute-done((bf16[128,2304]{1,0:T(8,128)(2,1)S(1)}, bf16[128,2304]{1,0:T(8,128)(2,1)S(1)}, u32[]{:S(2)}, u32[]{:S(2)}) %collective-permute-start.22) | collective-permute-done | bytes 589856 | tf_op jit(solution)/shard_map/ppermute | solution.py:609
  85.7 10.6 %collective-permute-done.5.refs_6_ = bf16[128,2048]{1,0:T(8,128)(2,1)S(1)} collective-permute-done((bf16[128,2048]{1,0:T(8,128)(2,1)S(1)}, bf16[128,2048]{1,0:T(8,128)(2,1)S(1)}, u32[]{:S(2)}, u32[]{:S(2)}) %collective-permute-start.5) | collective-permute-done | bytes 524320 | tf_op jit(solution)/shard_map/ppermute | solution.py:609
  102.5 23.8 %attend_forward.1 = (f32[2048,512]{1,0:T(8,128)}, bf16[2048,512]{1,0:T(8,128)(2,1)}, bf16[2048,256]{1,0:T(8,128)(2,1)}, f32[2048,256]{1,0:T(8,128)}) custom-call(s32[17]{0:T(128)} %pad_add_fusion.info, bf16[256,2048]{1,0:T(8,128)(2,1)} %fusion.1.refs_0_, bf16[256,2048]{1,0:T(8,128)(2,1)} %copy-done.72, bf16[256,2048]{1,0:T(8,128)(2,1)} %collective-permute-done.3.refs_2_, ...), custom_call_target="tpu_custom_call" | custom-call | flops 6442450944 | bytes 26214400 | tf_op jit(solution)/shard_map/attend_forward/pallas_call | solution.py:149
  129.0 4.9 rows_product.17
  138.6 5.4 collective-permute-done.15.refs_2_
  147.7 3.7 collective-permute-done.18.refs_6_
  151.4 6.6 %collective-permute-done.19.refs_7_ = bf16[128,2048]{1,0:T(8,128)(2,1)S(1)} collective-permute-done((bf16[128,2048]{1,0:T(8,128)(2,1)S(1)}, bf16[128,2048]{1,0:T(8,128)(2,1)S(1)}, u32[]{:S(2)}, u32[]{:S(2)}) %collective-permute-start.19) | collective-permute-done | bytes 524320 | tf_op jit(solution)/shard_map/ppermute | solution.py:609
  163.6 5.7 rows_product.19
  178.4 10.6 %collective-permute-done.30.refs_3_ = bf16[128,2048]{1,0:T(8,128)(2,1)S(1)} collective-permute-done((bf16[128,2048]{1,0:T(8,128)(2,1)S(1)}, bf16[128,2048]{1,0:T(8,128)(2,1)S(1)}, u32[]{:S(2)}, u32[]{:S(2)}) %collective-permute-start.30) | collective-permute-done | bytes 524320 | tf_op jit(solution)/shard_map/ppermute | solution.py:609
  190.9 8.5 %collective-permute-done.26.refs_1_ = bf16[128,2048]{1,0:T(8,128)(2,1)S(1)} collective-permute-done((bf16[128,2048]{1,0:T(8,128)(2,1)S(1)}, bf16[128,2048]{1,0:T(8,128)(2,1)S(1)}, u32[]{:S(2)}, u32[]{:S(2)}) %collective-permute-start.26) | collective-permute-done | bytes 524320 | tf_op jit(solution)/shard_map/ppermute | solution.py:609
  201.0 5.1 settle.4
  207.0 21.8 %collective-permute-done.32.refs_0_.refs_2_ = bf16[256,2048]{1,0:T(8,128)(2,1)S(1)} collective-permute-done((bf16[256,2048]{1,0:T(8,128)(2,1)}, bf16[256,2048]{1,0:T(8,128)(2,1)S(1)}, u32[]{:S(2)}, u32[]{:S(2)}) %collective-permute-start.32) | collective-permute-done | bytes 1048608 | tf_op jit(solution)/shard_map/ppermute | solution.py:609
  233.7 7.8 %feed_expand.3 = (bf16[2048,768]{1,0:T(8,128)(2,1)}, bf16[2048,768]{1,0:T(8,128)(2,1)}, bf16[2048,768]{1,0:T(8,128)(2,1)}) custom-call(bf16[256,2048]{1,0:T(8,128)(2,1)} %get-tuple-element.191.refs_0_, bf16[256,2048]{1,0:T(8,128)(2,1)} %collective-permute-done.38.refs_1_, ...), custom_call_target="tpu_custom_call" | custom-call | flops 3221225472 | bytes 12320768 | tf_op jit(solution)/shard_map/feed_expand/pallas_call | solution.py:365
  241.5 13.3 %feed_expand.4 = (bf16[2048,768]{1,0:T(8,128)(2,1)}, bf16[2048,768]{1,0:T(8,128)(2,1)}, bf16[2048,768]{1,0:T(8,128)(2,1)}) custom-call(bf16[256,2048]{1,0:T(8,128)(2,1)} %copy-done.9, bf16[256,2048]{1,0:T(8,128)(2,1)} %collective-permute-done.36.refs_1_.refs_3_, ...), custom_call_target="tpu_custom_call", output_to_operand_aliasing={{0}: (6, {}), {1}: (7, {}), {2}: (8, {})} | custom-call | flops 6442450944 | bytes 18350080 | tf_op jit(solution)/shard_map/feed_expand/pallas_call | solution.py:365
  259.3 7.6 %feed_expand.5 = (bf16[2048,768]{1,0:T(8,128)(2,1)}, bf16[2048,768]{1,0:T(8,128)(2,1)}, bf16[2048,768]{1,0:T(8,128)(2,1)}) custom-call(bf16[128,2048]{1,0:T(8,128)(2,1)} %collective-permute-done.33.refs_0_.refs_6_, bf16[128,2048]{1,0:T(8,128)(2,1)} %collective-permute-done.35.refs_1_.refs_7_, ...), custom_call_target="tpu_custom_call", output_to_operand_aliasing={{0}: (6, {}), {1}: (7, {}), {2}: (8, {})} | custom-call | flops 3221225472 | bytes 12320768 | tf_op jit(solution)/shard_map/feed_expand/pallas_call | solution.py:365
  267.8 12.7 %weight_terms.3 = bf16[2048,768]{1,0:T(8,128)(2,1)} custom-call(bf16[256,2048]{1,0:T(8,128)(2,1)} %copy-done.1, bf16[256,2048]{1,0:T(8,128)(2,1)} %collective-permute-done.7.refs_1_, bf16[256,2048]{1,0:T(8,128)(2,1)} %collective-permute-done.13.refs_2_, bf16[256,2048]{1,0:T(8,128)(2,1)} %copy-done.75, bf16[256,2048]{1,0:T(8,128)(2,1)} %collective-permute-done.14.refs_4_, ...), custom_call_target="tpu_custom_call" | custom-call | flops 6442450944 | bytes 14680064 | tf_op jit(solution)/shard_map/weight_terms/pallas_call | solution.py:449
  280.8 13.8 %feed_back.1 = (bf16[2048,768]{1,0:T(8,128)(2,1)}, bf16[2048,768]{1,0:T(8,128)(2,1)}) custom-call(bf16[256,2048]{1,0:T(8,128)(2,1)} %copy-done.1, bf16[256,2048]{1,0:T(8,128)(2,1)} %collective-permute-done.7.refs_1_, bf16[256,2048]{1,0:T(8,128)(2,1)} %collective-permute-done.13.refs_2_, bf16[256,2048]{1,0:T(8,128)(2,1)} %copy-done.75, ...), custom_call_target="tpu_custom_call" | custom-call | flops 6442450944 | bytes 30408704 | tf_op jit(solution)/shard_map/feed_back/pallas_call | solution.py:407
  294.5 4.9 rows_product.20
  299.4 9.1 %rows_product.21 = bf16[768,2048]{1,0:T(8,128)(2,1)} custom-call(bf16[2048,768]{1,0:T(8,128)(2,1)} %get-tuple-element.218.refs_0_.refs_1_.refs_2_.refs_10_, bf16[2048,768]{1,0:T(8,128)(2,1)} %get-tuple-element.218.refs_0_.refs_1_.refs_2_.refs_10_, bf16[2048,768]{1,0:T(8,128)(2,1)} %get-tuple-element.218.refs_0_.refs_1_.refs_2_.refs_10_, ...), custom_call_target="tpu_custom_call" | custom-call | flops 4831838208 | bytes 18087936 | tf_op jit(solution)/shard_map/rows_product/pallas_call | solution.py:505
  309.1 6.4 %collective-permute-done.41.refs_3_ = bf16[256,2048]{1,0:T(8,128)(2,1)S(1)} collective-permute-done((bf16[256,2048]{1,0:T(8,128)(2,1)S(1)}, bf16[256,2048]{1,0:T(8,128)(2,1)S(1)}, u32[]{:S(2)}, u32[]{:S(2)}) %collective-permute-start.41) | collective-permute-done | bytes 1048608 | tf_op jit(solution)/shard_map/ppermute | solution.py:613
  316.4 5.2 rows_product.22
  325.2 9.4 %rows_product.23 = (f32[256,2048]{1,0:T(8,128)}, bf16[128,2048]{1,0:T(8,128)(2,1)}, f32[128,2048]{1,0:T(8,128)}, f32[128,2048]{1,0:T(8,128)}, bf16[128,2048]{1,0:T(8,128)(2,1)}) custom-call(bf16[2048,768]{1,0:T(8,128)(2,1)} %get-tuple-element.218.refs_0_.refs_1_.refs_2_.refs_10_, bf16[2048,768]{1,0:T(8,128)(2,1)} %get-tuple-element.218.refs_0_.refs_1_.refs_2_.refs_10_, ...), custom_call_target="tpu_custom_call" | custom-call | flops 4831838208 | bytes 18087936 | tf_op jit(solution)/shard_map/rows_product/pallas_call | solution.py:505
  342.5 19.3 %weight_terms.4 = bf16[2048,1536]{1,0:T(8,128)(2,1)} custom-call(bf16[256,2048]{1,0:T(8,128)(2,1)} %get-tuple-element.191.refs_0_, bf16[256,2048]{1,0:T(8,128)(2,1)} %collective-permute-done.38.refs_1_, bf16[256,2048]{1,0:T(8,128)(2,1)} %copy-done.9, bf16[256,2048]{1,0:T(8,128)(2,1)} %collective-permute-done.36.refs_1_.refs_3_, ...), custom_call_target="tpu_custom_call" | custom-call | flops 12884901888 | bytes 20971520 | tf_op jit(solution)/shard_map/weight_terms/pallas_call | solution.py:449
  364.7 5.6 settle.5
  370.3 3.8 rows_product.24
  374.1 6.4 %rows_product.25 = bf16[768,2048]{1,0:T(8,128)(2,1)} custom-call(bf16[2048,768]{1,0:T(8,128)(2,1)} %get-tuple-element.226.refs_10_.refs_0_.refs_1_.refs_2_, bf16[2048,768]{1,0:T(8,128)(2,1)} %get-tuple-element.226.refs_10_.refs_0_.refs_1_.refs_2_, bf16[2048,768]{1,0:T(8,128)(2,1)} %get-tuple-element.226.refs_10_.refs_0_.refs_1_.refs_2_, ...), custom_call_target="tpu_custom_call" | custom-call | flops 2415919104 | bytes 13762560 | tf_op jit(solution)/shard_map/rows_product/pallas_call | solution.py:505
  383.5 5.3 collective-permute-done.52.refs_2_
  389.8 3.8 rows_product.26
  393.6 12.8 %collective-permute-done.50.refs_2_.refs_13_ = bf16[256,2048]{1,0:T(8,128)(2,1)S(1)} collective-permute-done((bf16[256,2048]{1,0:T(8,128)(2,1)}, bf16[256,2048]{1,0:T(8,128)(2,1)S(1)}, u32[]{:S(2)}, u32[]{:S(2)}) %collective-permute-start.50) | collective-permute-done | bytes 1048608 | tf_op jit(solution)/shard_map/ppermute | solution.py:609
  411.4 6.9 %rows_product.27 = (f32[256,2048]{1,0:T(8,128)}, bf16[128,2048]{1,0:T(8,128)(2,1)}, f32[128,2048]{1,0:T(8,128)}, f32[128,2048]{1,0:T(8,128)}, bf16[128,2048]{1,0:T(8,128)(2,1)}) custom-call(bf16[2048,768]{1,0:T(8,128)(2,1)} %get-tuple-element.226.refs_10_.refs_0_.refs_1_.refs_2_, bf16[2048,768]{1,0:T(8,128)(2,1)} %get-tuple-element.226.refs_10_.refs_0_.refs_1_.refs_2_, ...), custom_call_target="tpu_custom_call" | custom-call | flops 2415919104 | bytes 13762560 | tf_op jit(solution)/shard_map/rows_product/pallas_call | solution.py:505
  418.4 3.3 collective-permute-done.55.refs_6_.refs_17_
  428.5 34.0 %attend_backward.1 = (bf16[2048,512]{1,0:T(8,128)(2,1)}, f32[8,128]{1,0:T(8,128)}) custom-call(s32[17]{0:T(128)} %pad_add_fusion.info, bf16[256,2048]{1,0:T(8,128)(2,1)} %get-tuple-element.225.refs_0_.refs_11_, bf16[256,2048]{1,0:T(8,128)(2,1)} %collective-permute-done.49.refs_1_.refs_12_, bf16[256,2048]{1,0:T(8,128)(2,1)} %copy-done.65, ...), custom_call_target="tpu_custom_call" | custom-call | flops 7516192768 | bytes 36700160 | tf_op jit(solution)/shard_map/attend_backward/pallas_call | solution.py:309
  467.0 13.9 %weight_terms.5 = bf16[2048,768]{1,0:T(8,128)(2,1)} custom-call(bf16[256,2048]{1,0:T(8,128)(2,1)} %fusion.1.refs_0_, bf16[256,2048]{1,0:T(8,128)(2,1)} %copy-done.72, bf16[256,2048]{1,0:T(8,128)(2,1)} %collective-permute-done.3.refs_2_, bf16[256,2048]{1,0:T(8,128)(2,1)} %copy-done.74, bf16[256,2048]{1,0:T(8,128)(2,1)} %collective-permute-done.4.refs_4_, ...), custom_call_target="tpu_custom_call" | custom-call | flops 6442450944 | bytes 23068672 | tf_op jit(solution)/shard_map/weight_terms/pallas_call | solution.py:449
  487.3 5.4 rows_product.29
  504.2 3.5 collective-permute-done.73
  508.7 8.2 %collective-permute-done.74 = bf16[128,1536]{1,0:T(8,128)(2,1)S(1)} collective-permute-done((bf16[128,1536]{1,0:T(8,128)(2,1)S(1)}, bf16[128,1536]{1,0:T(8,128)(2,1)S(1)}, u32[]{:S(2)}, u32[]{:S(2)}) %collective-permute-start.74) | collective-permute-done | bytes 393248 | tf_op jit(solution)/shard_map/ppermute | solution.py:609
  520.4 6.4 %rows_product.31 = (f32[256,2048]{1,0:T(8,128)}, bf16[128,2048]{1,0:T(8,128)(2,1)}, f32[128,2048]{1,0:T(8,128)}, f32[128,2048]{1,0:T(8,128)}, bf16[128,2048]{1,0:T(8,128)(2,1)}) custom-call(bf16[2048,512]{1,0:T(8,128)(2,1)} %get-tuple-element.258.refs_10_.refs_0_.refs_1_.refs_2_, bf16[2048,512]{1,0:T(8,128)(2,1)} %get-tuple-element.258.refs_10_.refs_0_.refs_1_.refs_2_, ...), custom_call_target="tpu_custom_call" | custom-call | flops 1610612736 | bytes 12320768 | tf_op jit(solution)/shard_map/rows_product/pallas_call | solution.py:505
  529.1 10.2 %collective-permute-done.72 = bf16[128,2048]{1,0:T(8,128)(2,1)S(1)} collective-permute-done((bf16[128,2048]{1,0:T(8,128)(2,1)}, bf16[128,2048]{1,0:T(8,128)(2,1)S(1)}, u32[]{:S(2)}, u32[]{:S(2)}) %collective-permute-start.72) | collective-permute-done | bytes 524320 | tf_op jit(solution)/shard_map/ppermute | solution.py:609
  542.7 7.2 %collective-permute-done.71.refs_1_ = bf16[128,2048]{1,0:T(8,128)(2,1)S(1)} collective-permute-done((bf16[128,2048]{1,0:T(8,128)(2,1)}, bf16[128,2048]{1,0:T(8,128)(2,1)S(1)}, u32[]{:S(2)}, u32[]{:S(2)}) %collective-permute-start.71) | collective-permute-done | bytes 524320 | tf_op jit(solution)/shard_map/ppermute | solution.py:609
  550.6 10.0 %collective-permute-done.78.refs_3_ = bf16[128,2048]{1,0:T(8,128)(2,1)S(1)} collective-permute-done((bf16[128,2048]{1,0:T(8,128)(2,1)S(1)}, bf16[128,2048]{1,0:T(8,128)(2,1)S(1)}, u32[]{:S(2)}, u32[]{:S(2)}) %collective-permute-start.78) | collective-permute-done | bytes 524320 | tf_op jit(solution)/shard_map/ppermute | solution.py:609
  561.7 6.0 settle.6
  572.2 4.7 settle.7
  581.0 3.2 collective-permute-start.90
  598.0 3.2 collective-permute-done.83
  (465 shorter events, 178.4 us)
Async XLA Ops:
  7.2 95.3 %all-gather.4.cloned.1.call-start = ((), (), s32[]{:S(2)}) async-start(), calls=%async_computation.3 | async-start | bytes 3932160 | tf_op jit(solution)/shard_map/all_gather | solution.py:708
  25.8 24.1 %collective-permute-start.3 = (bf16[256,2048]{1,0:T(8,128)(2,1)}, bf16[256,2048]{1,0:T(8,128)(2,1)}, u32[]{:S(2)}, u32[]{:S(2)}) collective-permute-start(bf16[256,2048]{1,0:T(8,128)(2,1)} %fusion.1.refs_0_), channel_id=1, source_target_pairs={{0,2},{2,0},{4,6},{6,4},{1,3},{3,1},{5,7},{7,5},{8,10},{10,8},{12,... | collective-permute-start | bytes 3145736 | tf_op jit(solution)/shard_map/ppermute | solution.py:609
  27.3 23.7 %collective-permute-start.4 = (bf16[256,2048]{1,0:T(8,128)(2,1)}, bf16[256,2048]{1,0:T(8,128)(2,1)}, u32[]{:S(2)}, u32[]{:S(2)}) collective-permute-start(bf16[256,2048]{1,0:T(8,128)(2,1)} %fusion.1.refs_0_), channel_id=1, source_target_pairs={{0,4},{2,6},{4,0},{6,2},{1,5},{3,7},{5,1},{7,3},{8,12},{10,14},{12... | collective-permute-start | bytes 3145736 | tf_op jit(solution)/shard_map/ppermute | solution.py:609
  29.1 204.6 %all-gather.8.cloned.1.call-start = ((), (), s32[]{:S(2)}) async-start(), calls=%async_computation.5 | async-start | bytes 7864320 | tf_op jit(solution)/shard_map/all_gather | solution.py:708
  52.0 24.8 %collective-permute-start.22 = (bf16[128,2304]{1,0:T(8,128)(2,1)S(1)}, bf16[128,2304]{1,0:T(8,128)(2,1)S(1)}, u32[]{:S(2)}, u32[]{:S(2)}) collective-permute-start(bf16[128,2304]{1,0:T(8,128)(2,1)S(1)} %pad_maximum_fusion.7), channel_id=1, source_target_pairs={{0,6},{2,4},{4,2},{6,0},{1,7},{3,5},{5,3},{7,1},{8,14},{10,12},{12... | collective-permute-start | bytes 1769480 | tf_op jit(solution)/shard_map/ppermute | solution.py:609
  53.5 24.8 %collective-permute-start.23 = (bf16[128,2304]{1,0:T(8,128)(2,1)S(1)}, bf16[128,2304]{1,0:T(8,128)(2,1)S(1)}, u32[]{:S(2)}, u32[]{:S(2)}) collective-permute-start(bf16[128,2304]{1,0:T(8,128)(2,1)S(1)} %pad_maximum_fusion.8), channel_id=1, source_target_pairs={{0,4},{2,6},{4,0},{6,2},{1,5},{3,7},{5,1},{7,3},{8,12},{10,14},{12... | collective-permute-start | bytes 1769480 | tf_op jit(solution)/shard_map/ppermute | solution.py:609
  80.4 200.2 %all-gather.6.cloned.1.call-start = ((), (), s32[]{:S(2)}) async-start(), calls=%async_computation.4 | async-start | bytes 3932160 | tf_op jit(solution)/shard_map/all_gather | solution.py:708
  99.1 27.3 %collective-permute-start.13 = (bf16[256,2048]{1,0:T(8,128)(2,1)S(1)}, bf16[256,2048]{1,0:T(8,128)(2,1)}, u32[]{:S(2)}, u32[]{:S(2)}) collective-permute-start(bf16[256,2048]{1,0:T(8,128)(2,1)S(1)} %dynamic-slice_select_fusion.refs_0_.refs_6_), channel_id=1, source_target_pairs={{0,2},{2,0},{4,6},{6,4},{1,3},{3,1},{5,7},{7,5},{8,10},{10,8},{12,... | collective-permute-start | bytes 3145736 | tf_op jit(solution)/shard_map/ppermute | solution.py:609
  99.7 26.7 %collective-permute-start.14 = (bf16[256,2048]{1,0:T(8,128)(2,1)S(1)}, bf16[256,2048]{1,0:T(8,128)(2,1)}, u32[]{:S(2)}, u32[]{:S(2)}) collective-permute-start(bf16[256,2048]{1,0:T(8,128)(2,1)S(1)} %dynamic-slice_select_fusion.refs_0_.refs_6_), channel_id=1, source_target_pairs={{0,4},{2,6},{4,0},{6,2},{1,5},{3,7},{5,1},{7,3},{8,12},{10,14},{12... | collective-permute-start | bytes 3145736 | tf_op jit(solution)/shard_map/ppermute | solution.py:609
  133.8 29.7 %collective-permute-start.25 = (bf16[768,2048]{1,0:T(8,128)(2,1)}, bf16[768,2048]{1,0:T(8,128)(2,1)}, u32[]{:S(2)}, u32[]{:S(2)}) collective-permute-start(bf16[768,2048]{1,0:T(8,128)(2,1)} %rows_product.17), channel_id=1, source_target_pairs={{0,1},{1,0},{2,3},{3,2},{4,5},{5,4},{6,7},{7,6},{8,9},{9,8},{10,11... | collective-permute-start | bytes 9437192 | tf_op jit(solution)/shard_map/ppermute | solution.py:613
  134.4 23.6 %collective-permute-start.16 = (bf16[256,2048]{1,0:T(8,128)(2,1)}, bf16[256,2048]{1,0:T(8,128)(2,1)S(1)}, u32[]{:S(2)}, u32[]{:S(2)}) collective-permute-start(bf16[256,2048]{1,0:T(8,128)(2,1)} %collective-permute-done.13.refs_2_), channel_id=1, source_target_pairs={{0,1},{1,0},{2,3},{3,2},{4,5},{5,4},{6,7},{7,6},{8,9},{9,8},{10,11... | collective-permute-start | bytes 3145736 | tf_op jit(solution)/shard_map/ppermute | solution.py:613
  134.8 23.2 %collective-permute-start.17 = (bf16[256,2048]{1,0:T(8,128)(2,1)}, bf16[256,2048]{1,0:T(8,128)(2,1)}, u32[]{:S(2)}, u32[]{:S(2)}) collective-permute-start(bf16[256,2048]{1,0:T(8,128)(2,1)} %collective-permute-done.14.refs_4_), channel_id=1, source_target_pairs={{0,1},{1,0},{2,3},{3,2},{4,5},{5,4},{6,7},{7,6},{8,9},{9,8},{10,11... | collective-permute-start | bytes 3145736 | tf_op jit(solution)/shard_map/ppermute | solution.py:613
  163.0 200.5 %reduce-scatter.4.cloned.1.call-start = ((), (), s32[]{:S(2)}) async-start(), calls=%async_computation.6 | async-start | bytes 3932160 | tf_op jit(solution)/shard_map/reduce_scatter | solution.py:712
  176.6 22.8 %collective-permute-start.26 = (bf16[128,2048]{1,0:T(8,128)(2,1)S(1)}, bf16[128,2048]{1,0:T(8,128)(2,1)S(1)}, u32[]{:S(2)}, u32[]{:S(2)}) collective-permute-start(bf16[128,2048]{1,0:T(8,128)(2,1)S(1)} %copy-done.90), channel_id=1, source_target_pairs={{0,2},{2,0},{4,6},{6,4},{1,3},{3,1},{5,7},{7,5},{8,10},{10,8},{12,... | collective-permute-start | bytes 1572872 | tf_op jit(solution)/shard_map/ppermute | solution.py:609
  178.1 21.3 %collective-permute-start.31 = (bf16[128,2048]{1,0:T(8,128)(2,1)S(1)}, bf16[128,2048]{1,0:T(8,128)(2,1)S(1)}, u32[]{:S(2)}, u32[]{:S(2)}) collective-permute-start(bf16[128,2048]{1,0:T(8,128)(2,1)S(1)} %copy-done.89), channel_id=1, source_target_pairs={{0,4},{2,6},{4,0},{6,2},{1,5},{3,7},{5,1},{7,3},{8,12},{10,14},{12... | collective-permute-start | bytes 1572872 | tf_op jit(solution)/shard_map/ppermute | solution.py:609
  206.1 22.7 %collective-permute-start.32 = (bf16[256,2048]{1,0:T(8,128)(2,1)}, bf16[256,2048]{1,0:T(8,128)(2,1)S(1)}, u32[]{:S(2)}, u32[]{:S(2)}) collective-permute-start(bf16[256,2048]{1,0:T(8,128)(2,1)} %get-tuple-element.191.refs_0_), channel_id=1, source_target_pairs={{0,2},{2,0},{4,6},{6,4},{1,3},{3,1},{5,7},{7,5},{8,10},{10,8},{12,... | collective-permute-start | bytes 3145736 | tf_op jit(solution)/shard_map/ppermute | solution.py:609
  206.7 22.5 %collective-permute-start.34 = (bf16[256,2048]{1,0:T(8,128)(2,1)}, bf16[256,2048]{1,0:T(8,128)(2,1)S(1)}, u32[]{:S(2)}, u32[]{:S(2)}) collective-permute-start(bf16[256,2048]{1,0:T(8,128)(2,1)} %get-tuple-element.191.refs_0_), channel_id=1, source_target_pairs={{0,4},{2,6},{4,0},{6,2},{1,5},{3,7},{5,1},{7,3},{8,12},{10,14},{12... | collective-permute-start | bytes 3145736 | tf_op jit(solution)/shard_map/ppermute | solution.py:609
  207.0 25.1 %collective-permute-start.38 = (bf16[256,2048]{1,0:T(8,128)(2,1)}, bf16[256,2048]{1,0:T(8,128)(2,1)}, u32[]{:S(2)}, u32[]{:S(2)}) collective-permute-start(bf16[256,2048]{1,0:T(8,128)(2,1)} %get-tuple-element.191.refs_0_), channel_id=1, source_target_pairs={{0,1},{1,0},{2,3},{3,2},{4,5},{5,4},{6,7},{7,6},{8,9},{9,8},{10,11... | collective-permute-start | bytes 3145736 | tf_op jit(solution)/shard_map/ppermute | solution.py:613
  229.4 37.5 %collective-permute-start.7 = (bf16[256,2048]{1,0:T(8,128)(2,1)S(1)}, bf16[256,2048]{1,0:T(8,128)(2,1)}, u32[]{:S(2)}, u32[]{:S(2)}) collective-permute-start(bf16[256,2048]{1,0:T(8,128)(2,1)S(1)} %dynamic-slice_select_fusion.refs_0_.refs_6_), channel_id=1, source_target_pairs={{0,1},{1,0},{2,3},{3,2},{4,5},{5,4},{6,7},{7,6},{8,9},{9,8},{10,11... | collective-permute-start | bytes 3145736 | tf_op jit(solution)/shard_map/ppermute | solution.py:613
  230.6 24.2 %collective-permute-start.33 = (bf16[128,2048]{1,0:T(8,128)(2,1)}, bf16[128,2048]{1,0:T(8,128)(2,1)}, u32[]{:S(2)}, u32[]{:S(2)}) collective-permute-start(bf16[128,2048]{1,0:T(8,128)(2,1)} %slice.173), channel_id=1, source_target_pairs={{0,4},{2,6},{4,0},{6,2},{1,5},{3,7},{5,1},{7,3},{8,12},{10,14},{12... | collective-permute-start | bytes 1572872 | tf_op jit(solution)/shard_map/ppermute | solution.py:609
  232.1 22.7 %collective-permute-start.35 = (bf16[128,2048]{1,0:T(8,128)(2,1)}, bf16[128,2048]{1,0:T(8,128)(2,1)}, u32[]{:S(2)}, u32[]{:S(2)}) collective-permute-start(bf16[128,2048]{1,0:T(8,128)(2,1)} %slice.174), channel_id=1, source_target_pairs={{0,2},{2,0},{4,6},{6,4},{1,3},{3,1},{5,7},{7,5},{8,10},{10,8},{12,... | collective-permute-start | bytes 1572872 | tf_op jit(solution)/shard_map/ppermute | solution.py:609
  280.6 212.1 %reduce-scatter.6.cloned.1.call-start = ((), (), s32[]{:S(2)}) async-start(), calls=%async_computation.7 | async-start | bytes 7864320 | tf_op jit(solution)/shard_map/reduce_scatter | solution.py:712
  338.2 23.6 %collective-permute-start.47 = (bf16[128,2048]{1,0:T(8,128)(2,1)S(1)}, bf16[128,2048]{1,0:T(8,128)(2,1)S(1)}, u32[]{:S(2)}, u32[]{:S(2)}) collective-permute-start(bf16[128,2048]{1,0:T(8,128)(2,1)S(1)} %add_convert_fusion.4), channel_id=1, source_target_pairs={{0,4},{2,6},{4,0},{6,2},{1,5},{3,7},{5,1},{7,3},{8,12},{10,14},{12... | collective-permute-start | bytes 1572872 | tf_op jit(solution)/shard_map/ppermute | solution.py:609
  339.3 22.5 %collective-permute-start.46 = (bf16[128,2048]{1,0:T(8,128)(2,1)S(1)}, bf16[128,2048]{1,0:T(8,128)(2,1)S(1)}, u32[]{:S(2)}, u32[]{:S(2)}) collective-permute-start(bf16[128,2048]{1,0:T(8,128)(2,1)S(1)} %add_convert_fusion.5), channel_id=1, source_target_pairs={{0,2},{2,0},{4,6},{6,4},{1,3},{3,1},{5,7},{7,5},{8,10},{10,8},{12,... | collective-permute-start | bytes 1572872 | tf_op jit(solution)/shard_map/ppermute | solution.py:609
  339.8 23.7 %collective-permute-start.43 = (bf16[128,2048]{1,0:T(8,128)(2,1)}, bf16[128,2048]{1,0:T(8,128)(2,1)S(1)}, u32[]{:S(2)}, u32[]{:S(2)}) collective-permute-start(bf16[128,2048]{1,0:T(8,128)(2,1)} %get-tuple-element.211), channel_id=1, source_target_pairs={{0,2},{2,0},{4,6},{6,4},{1,3},{3,1},{5,7},{7,5},{8,10},{10,8},{12,... | collective-permute-start | bytes 1572872 | tf_op jit(solution)/shard_map/ppermute | solution.py:609
  341.4 22.1 %collective-permute-start.48 = (bf16[128,2048]{1,0:T(8,128)(2,1)}, bf16[128,2048]{1,0:T(8,128)(2,1)S(1)}, u32[]{:S(2)}, u32[]{:S(2)}) collective-permute-start(bf16[128,2048]{1,0:T(8,128)(2,1)} %get-tuple-element.217), channel_id=1, source_target_pairs={{0,4},{2,6},{4,0},{6,2},{1,5},{3,7},{5,1},{7,3},{8,12},{10,14},{12... | collective-permute-start | bytes 1572872 | tf_op jit(solution)/shard_map/ppermute | solution.py:609
  364.5 223.6 %reduce-scatter.8.cloned.1.call-start = ((), (), s32[]{:S(2)}) async-start(), calls=%async_computation.8 | async-start | bytes 3932160 | tf_op jit(solution)/shard_map/reduce_scatter | solution.py:712
  380.5 29.3 %collective-permute-start.57 = (bf16[768,2048]{1,0:T(8,128)(2,1)}, bf16[768,2048]{1,0:T(8,128)(2,1)S(1)}, u32[]{:S(2)}, u32[]{:S(2)}) collective-permute-start(bf16[768,2048]{1,0:T(8,128)(2,1)} %rows_product.25), channel_id=1, source_target_pairs={{0,1},{1,0},{2,3},{3,2},{4,5},{5,4},{6,7},{7,6},{8,9},{9,8},{10,11... | collective-permute-start | bytes 9437192 | tf_op jit(solution)/shard_map/ppermute | solution.py:613
  381.0 25.3 %collective-permute-start.50 = (bf16[256,2048]{1,0:T(8,128)(2,1)}, bf16[256,2048]{1,0:T(8,128)(2,1)S(1)}, u32[]{:S(2)}, u32[]{:S(2)}) collective-permute-start(bf16[256,2048]{1,0:T(8,128)(2,1)} %get-tuple-element.225.refs_0_.refs_11_), channel_id=1, source_target_pairs={{0,2},{2,0},{4,6},{6,4},{1,3},{3,1},{5,7},{7,5},{8,10},{10,8},{12,... | collective-permute-start | bytes 3145736 | tf_op jit(solution)/shard_map/ppermute | solution.py:609
  382.1 25.1 %collective-permute-start.51 = (bf16[256,2048]{1,0:T(8,128)(2,1)}, bf16[256,2048]{1,0:T(8,128)(2,1)S(1)}, u32[]{:S(2)}, u32[]{:S(2)}) collective-permute-start(bf16[256,2048]{1,0:T(8,128)(2,1)} %get-tuple-element.225.refs_0_.refs_11_), channel_id=1, source_target_pairs={{0,4},{2,6},{4,0},{6,2},{1,5},{3,7},{5,1},{7,3},{8,12},{10,14},{12... | collective-permute-start | bytes 3145736 | tf_op jit(solution)/shard_map/ppermute | solution.py:609
  383.5 40.0 %collective-permute-start.49 = (bf16[256,2048]{1,0:T(8,128)(2,1)}, bf16[256,2048]{1,0:T(8,128)(2,1)}, u32[]{:S(2)}, u32[]{:S(2)}) collective-permute-start(bf16[256,2048]{1,0:T(8,128)(2,1)} %get-tuple-element.225.refs_0_.refs_11_), channel_id=1, source_target_pairs={{0,1},{1,0},{2,3},{3,2},{4,5},{5,4},{6,7},{7,6},{8,9},{9,8},{10,11... | collective-permute-start | bytes 3145736 | tf_op jit(solution)/shard_map/ppermute | solution.py:613
  423.5 38.9 %collective-permute-start.60 = (bf16[128,2048]{1,0:T(8,128)(2,1)}, bf16[128,2048]{1,0:T(8,128)(2,1)S(1)}, u32[]{:S(2)}, u32[]{:S(2)}) collective-permute-start(bf16[128,2048]{1,0:T(8,128)(2,1)} %get-tuple-element.246), channel_id=1, source_target_pairs={{0,2},{2,0},{4,6},{6,4},{1,3},{3,1},{5,7},{7,5},{8,10},{10,8},{12,... | collective-permute-start | bytes 1572872 | tf_op jit(solution)/shard_map/ppermute | solution.py:609
  424.4 38.1 %collective-permute-start.61 = (bf16[128,2048]{1,0:T(8,128)(2,1)}, bf16[128,2048]{1,0:T(8,128)(2,1)S(1)}, u32[]{:S(2)}, u32[]{:S(2)}) collective-permute-start(bf16[128,2048]{1,0:T(8,128)(2,1)} %get-tuple-element.247), channel_id=1, source_target_pairs={{0,4},{2,6},{4,0},{6,2},{1,5},{3,7},{5,1},{7,3},{8,12},{10,14},{12... | collective-permute-start | bytes 1572872 | tf_op jit(solution)/shard_map/ppermute | solution.py:609
  425.1 37.4 %collective-permute-start.62 = (bf16[128,2048]{1,0:T(8,128)(2,1)}, bf16[128,2048]{1,0:T(8,128)(2,1)S(1)}, u32[]{:S(2)}, u32[]{:S(2)}) collective-permute-start(bf16[128,2048]{1,0:T(8,128)(2,1)} %get-tuple-element.248), channel_id=1, source_target_pairs={{0,4},{2,6},{4,0},{6,2},{1,5},{3,7},{5,1},{7,3},{8,12},{10,14},{12... | collective-permute-start | bytes 1572872 | tf_op jit(solution)/shard_map/ppermute | solution.py:609
  426.5 36.1 %collective-permute-start.63 = (bf16[128,2048]{1,0:T(8,128)(2,1)}, bf16[128,2048]{1,0:T(8,128)(2,1)S(1)}, u32[]{:S(2)}, u32[]{:S(2)}) collective-permute-start(bf16[128,2048]{1,0:T(8,128)(2,1)} %get-tuple-element.249), channel_id=1, source_target_pairs={{0,2},{2,0},{4,6},{6,4},{1,3},{3,1},{5,7},{7,5},{8,10},{10,8},{12,... | collective-permute-start | bytes 1572872 | tf_op jit(solution)/shard_map/ppermute | solution.py:609
  492.7 26.0 %collective-permute-start.70 = (bf16[768,2048]{1,0:T(8,128)(2,1)}, bf16[768,2048]{1,0:T(8,128)(2,1)S(1)}, u32[]{:S(2)}, u32[]{:S(2)}) collective-permute-start(bf16[768,2048]{1,0:T(8,128)(2,1)} %rows_product.29), channel_id=1, source_target_pairs={{0,1},{1,0},{2,3},{3,2},{4,5},{5,4},{6,7},{7,6},{8,9},{9,8},{10,11... | collective-permute-start | bytes 9437192 | tf_op jit(solution)/shard_map/ppermute | solution.py:613
  496.5 20.4 %collective-permute-start.74 = (bf16[128,1536]{1,0:T(8,128)(2,1)S(1)}, bf16[128,1536]{1,0:T(8,128)(2,1)S(1)}, u32[]{:S(2)}, u32[]{:S(2)}) collective-permute-start(bf16[128,1536]{1,0:T(8,128)(2,1)S(1)} %get-tuple-element.358), channel_id=1, source_target_pairs={{0,4},{2,6},{4,0},{6,2},{1,5},{3,7},{5,1},{7,3},{8,12},{10,14},{12... | collective-permute-start | bytes 1179656 | tf_op jit(solution)/shard_map/ppermute | solution.py:609
  497.2 20.4 %collective-permute-start.75 = (bf16[128,1536]{1,0:T(8,128)(2,1)S(1)}, bf16[128,1536]{1,0:T(8,128)(2,1)S(1)}, u32[]{:S(2)}, u32[]{:S(2)}) collective-permute-start(bf16[128,1536]{1,0:T(8,128)(2,1)S(1)} %get-tuple-element.357), channel_id=1, source_target_pairs={{0,6},{2,4},{4,2},{6,0},{1,7},{3,5},{5,3},{7,1},{8,14},{10,12},{12... | collective-permute-start | bytes 1179656 | tf_op jit(solution)/shard_map/ppermute | solution.py:609
  500.1 28.1 %collective-permute-start.68 = (bf16[128,2048]{1,0:T(8,128)(2,1)S(1)}, bf16[128,2048]{1,0:T(8,128)(2,1)S(1)}, u32[]{:S(2)}, u32[]{:S(2)}) collective-permute-start(bf16[128,2048]{1,0:T(8,128)(2,1)S(1)} %copy-done.46), channel_id=1, source_target_pairs={{0,4},{2,6},{4,0},{6,2},{1,5},{3,7},{5,1},{7,3},{8,12},{10,14},{12... | collective-permute-start | bytes 1572872 | tf_op jit(solution)/shard_map/ppermute | solution.py:609
  507.7 21.4 %collective-permute-start.67 = (bf16[128,2048]{1,0:T(8,128)(2,1)S(1)}, bf16[128,2048]{1,0:T(8,128)(2,1)S(1)}, u32[]{:S(2)}, u32[]{:S(2)}) collective-permute-start(bf16[128,2048]{1,0:T(8,128)(2,1)S(1)} %copy-done.45), channel_id=1, source_target_pairs={{0,2},{2,0},{4,6},{6,4},{1,3},{3,1},{5,7},{7,5},{8,10},{10,8},{12,... | collective-permute-start | bytes 1572872 | tf_op jit(solution)/shard_map/ppermute | solution.py:609
  516.9 22.5 %collective-permute-start.72 = (bf16[128,2048]{1,0:T(8,128)(2,1)}, bf16[128,2048]{1,0:T(8,128)(2,1)S(1)}, u32[]{:S(2)}, u32[]{:S(2)}) collective-permute-start(bf16[128,2048]{1,0:T(8,128)(2,1)} %get-tuple-element.273), channel_id=1, source_target_pairs={{0,4},{2,6},{4,0},{6,2},{1,5},{3,7},{5,1},{7,3},{8,12},{10,14},{12... | collective-permute-start | bytes 1572872 | tf_op jit(solution)/shard_map/ppermute | solution.py:609
  517.7 21.7 %collective-permute-start.76 = (bf16[128,2048]{1,0:T(8,128)(2,1)}, bf16[128,2048]{1,0:T(8,128)(2,1)S(1)}, u32[]{:S(2)}, u32[]{:S(2)}) collective-permute-start(bf16[128,2048]{1,0:T(8,128)(2,1)} %get-tuple-element.277), channel_id=1, source_target_pairs={{0,2},{2,0},{4,6},{6,4},{1,3},{3,1},{5,7},{7,5},{8,10},{10,8},{12,... | collective-permute-start | bytes 1572872 | tf_op jit(solution)/shard_map/ppermute | solution.py:609
  526.8 23.1 %collective-permute-start.71 = (bf16[128,2048]{1,0:T(8,128)(2,1)}, bf16[128,2048]{1,0:T(8,128)(2,1)S(1)}, u32[]{:S(2)}, u32[]{:S(2)}) collective-permute-start(bf16[128,2048]{1,0:T(8,128)(2,1)} %get-tuple-element.271), channel_id=1, source_target_pairs={{0,2},{2,0},{4,6},{6,4},{1,3},{3,1},{5,7},{7,5},{8,10},{10,8},{12,... | collective-permute-start | bytes 1572872 | tf_op jit(solution)/shard_map/ppermute | solution.py:609
  528.2 22.5 %collective-permute-start.79 = (bf16[128,2048]{1,0:T(8,128)(2,1)}, bf16[128,2048]{1,0:T(8,128)(2,1)S(1)}, u32[]{:S(2)}, u32[]{:S(2)}) collective-permute-start(bf16[128,2048]{1,0:T(8,128)(2,1)} %get-tuple-element.281), channel_id=1, source_target_pairs={{0,4},{2,6},{4,0},{6,2},{1,5},{3,7},{5,1},{7,3},{8,12},{10,14},{12... | collective-permute-start | bytes 1572872 | tf_op jit(solution)/shard_map/ppermute | solution.py:609
  540.8 19.9 %collective-permute-start.78 = (bf16[128,2048]{1,0:T(8,128)(2,1)S(1)}, bf16[128,2048]{1,0:T(8,128)(2,1)S(1)}, u32[]{:S(2)}, u32[]{:S(2)}) collective-permute-start(bf16[128,2048]{1,0:T(8,128)(2,1)S(1)} %add_convert_fusion), channel_id=1, source_target_pairs={{0,4},{2,6},{4,0},{6,2},{1,5},{3,7},{5,1},{7,3},{8,12},{10,14},{12... | collective-permute-start | bytes 1572872 | tf_op jit(solution)/shard_map/ppermute | solution.py:609
  541.6 19.1 %collective-permute-start.77 = (bf16[128,2048]{1,0:T(8,128)(2,1)S(1)}, bf16[128,2048]{1,0:T(8,128)(2,1)S(1)}, u32[]{:S(2)}, u32[]{:S(2)}) collective-permute-start(bf16[128,2048]{1,0:T(8,128)(2,1)S(1)} %add_convert_fusion.1), channel_id=1, source_target_pairs={{0,2},{2,0},{4,6},{6,4},{1,3},{3,1},{5,7},{7,5},{8,10},{10,8},{12,... | collective-permute-start | bytes 1572872 | tf_op jit(solution)/shard_map/ppermute | solution.py:609
  542.7 25.1 %collective-permute-start.86 = (f32[8,128]{1,0:T(8,128)S(1)}, f32[8,128]{1,0:T(8,128)S(1)}, u32[]{:S(2)}, u32[]{:S(2)}) collective-permute-start(f32[8,128]{1,0:T(8,128)S(1)} %copy-done.69), channel_id=1, source_target_pairs={{0,1},{1,0},{2,3},{3,2},{4,5},{5,4},{6,7},{7,6},{8,9},{9,8},{10,11... | collective-permute-start | bytes 12296 | tf_op jit(solution)/shard_map/ppermute | solution.py:613
  567.7 25.1 %collective-permute-start.81 = (f32[256,2048]{1,0:T(8,128)}, f32[256,2048]{1,0:T(8,128)}, u32[]{:S(2)}, u32[]{:S(2)}) collective-permute-start(f32[256,2048]{1,0:T(8,128)} %get-tuple-element.283), channel_id=1, source_target_pairs={{0,1},{1,0},{2,3},{3,2},{4,5},{5,4},{6,7},{7,6},{8,9},{9,8},{10,11... | collective-permute-start | bytes 6291464 | tf_op jit(solution)/shard_map/ppermute | solution.py:613
  (143 other events, 1199.3 us)
Sparse Core Ops, SparseCore 0:
  29.2 63.8 all-gather.3
  95.2 113.9 all-gather.7
  210.8 61.7 all-gather.5
  280.7 60.2 reduce-scatter.3
  363.7 110.7 reduce-scatter.5
  492.9 60.1 reduce-scatter.7

commit v4 on v3

--- a/solution.py
+++ b/solution.py
@@ -563,7 +563,7 @@
         finish(x_bottom, y_bottom)
 
 
-def settle(mode, sums, others, types, core=None, steps=4):
+def settle(mode, sums, others, types, core=None, steps=2):
     rows, width = sums[0].shape
     block = (rows // steps, width)
     half = steps // 2
@@ -638,7 +638,7 @@
     return [own, own_other, by_x, x_other, by_y, y_other] + far
 
 
-def scatter_rows(lefts, weight, column):
+def scatter_rows(lefts, weight, column, beside=()):
     size = lefts[0].shape[0] // (2 * CTX)
     half = size // 2
     wide_step = weight.shape[0] // 2
@@ -653,7 +653,7 @@
         [(3 * size, jnp.bfloat16)],
         [(0, i * size, size) for i in range(3)],
     )[0]
-    far_there = after(other_core(far_there), rest_there)
+    far_there = after(other_core(far_there), rest_there, beside)
     rest_there = other_core(rest_there)
     far_top, far_bottom = rows_product(
         lefts,
@@ -758,6 +758,12 @@
         ]
         return [across(v, j) if j else v for j, v in enumerate(got)]
 
+    def whole_rows(both, half):
+        return lax.dynamic_update_slice_in_dim(both, other_core(half), (1 - core) * half_rows, 0)
+
+    def cut(pieces, start, size):
+        return wide(in_order([p[:, start : start + size] for p in pieces], spot, 1))
+
     attn_scale = wide(attn_gain)[:, None]
     feed_scale = wide(ffn_gain)[:, None]
     scaled = [low(wide(w) * attn_scale) for w in (w_query, w_key, w_value)]
@@ -815,23 +821,27 @@
     )
     out_column = proj_cols // query_cols
     mixed_low, seed_x, seed_y = lax.optimization_barrier((mixed_low, seed_x, seed_y))
-    seed_far = gather_far(seed_x, seed_y)
+    seed_cross = [other_core(seed_x), other_core(seed_y)]
     parts = list(scatter_rows([mixed_low], attn_weight, out_column))
-    parts[0], seed_far = lax.optimization_barrier((parts[0], seed_far))
+    parts[0], seed_cross = lax.optimization_barrier((parts[0], seed_cross))
     parts = scatter_send(parts)
     sums, _ = scatter_end(parts)
-    seeds = [seed, seed_other, seed_x, seed_far[0], seed_y, *seed_far[1:]]
-    seeds += [other_core(v) for v in seed_far[2:]]
     hidden, hat_two = settle("norm", sums, (own,), (jnp.float32, jnp.bfloat16))
 
     total = local_rows * CTX
     other, by_x, by_y = gather_near(hat_two)
     x_other, y_other, far_top, far_bottom = gather_far(by_x, by_y)
+    half = half_rows // 2
+    seed_far = after((seed_x, seed_y), by_x, by_y)
+    seed_far = [across(seed_far[0][:half], 2), across(seed_far[1][half:], 1)]
     filled = feed_expand([[hat_two, other]], 0, feed_weight, total)
     filled = feed_expand([[by_x, x_other], [by_y, y_other]], 1, feed_weight, total, filled)
     far = list(after((far_top, far_bottom), filled[0]))
     far += [other_core(v) for v in far]
     normed_two = [hat_two, other, by_x, x_other, by_y, y_other] + far
+    seed_far = after(seed_far, filled[0])
+    seeds = [seed, seed_other, seed_x, seed_cross[0], seed_y, seed_cross[1]]
+    seeds += seed_far + [other_core(v) for v in seed_far]
     slope, silu, inner = feed_expand([far], 3, feed_weight, total, filled)
     grad_down = weight_terms([(seeds, [inner])])
     down_weight, grad_down = lax.optimization_barrier((down_weight, grad_down))
@@ -843,8 +853,12 @@
     grad_feed = sum_stages(after(grad_feed, grad_down))
     grad_hidden, grad_attn = settle("back", sums, (hidden, seed), (jnp.float32, jnp.bfloat16))
 
-    feed_parts = scatter_rows([after(inner, grad_attn)], down_weight, 0)
-    grad_attn = gather_rows(grad_attn, feed_parts[:2], feed_parts[2])
+    other, by_x, by_y = gather_near(grad_attn)
+    feed_parts = scatter_rows([after(inner, other)], down_weight, 0)
+    by_x, by_y = after((by_x, by_y), feed_parts[:2], feed_parts[2])
+    x_other, y_other, far_top, far_bottom = gather_far(by_x, by_y)
+    far = [far_top, far_bottom, other_core(far_top), other_core(far_bottom)]
+    grad_attn = [grad_attn, other, by_x, x_other, by_y, y_other] + far
     feed_parts = scatter_send(after(feed_parts, grad_attn[6:8]))
     grad_proj, gain_sums = attend_backward(
         info,
@@ -867,32 +881,30 @@
     grad_attn_w = sum_stages(after(grad_attn_w, grad_feed))
     feed_sums, feed_sent = scatter_end(feed_parts, down_pieces)
     feed_pieces = dealt_rows(after(grad_feed, feed_sent))
-    parts = list(scatter_rows([grad_proj], after(weight, feed_sent), 0))
-    parts[0], feed_pieces = lax.optimization_barrier((parts[0], feed_pieces))
-    sums, sent = scatter_end(scatter_send(parts), feed_sums)
-    gain_sums = after(gain_sums, sent)
+    parts = scatter_rows([grad_proj], after(weight, feed_sent), 0)
+    sums, sent = scatter_end(scatter_send(parts), (feed_sums, feed_pieces))
+    grad_gate_w = cut(feed_pieces, 0, units)
+    grad_up_w = cut(feed_pieces, units, units)
+    feed_gain = jnp.sum(wide(w_gate) * grad_gate_w + wide(w_up) * grad_up_w, axis=1)
+    feed_gain = feed_gain + other_core(feed_gain)
+    grad_gate_w = grad_gate_w * feed_scale
+    grad_up_w = grad_up_w * feed_scale
+    grad_down_w = cut(down_pieces, 0, units).T
+    early = (grad_gate_w, grad_up_w, grad_down_w)
+    sums, early, grad_attn_w = lax.optimization_barrier((sums, early, grad_attn_w))
+    grad_gate_w, grad_up_w, grad_down_w = early
+    proj_pieces = dealt_rows(grad_attn_w)
+    tokens_half, grad_tokens = settle("back", sums, (own, grad_hidden), (jnp.float32,), core)
+    feed_sums = after(feed_sums, tokens_half, proj_pieces)
+    gain_sums = after(gain_sums, tokens_half)
     gain_sums = gain_sums + other_core(gain_sums)
     for bit in (1, 2):
         gain_sums = gain_sums + across(gain_sums, bit)
     gain_sums = sum_small(gain_sums)
-    tokens_half, grad_tokens = settle("back", sums, (own, grad_hidden), (jnp.float32,), core)
-    feed_sums = after(feed_sums, tokens_half)
     output_half, output = settle("add", feed_sums, (hidden,), (jnp.bfloat16,), core)
 
-    def whole_rows(both, half):
-        return lax.dynamic_update_slice_in_dim(both, other_core(half), (1 - core) * half_rows, 0)
-
-    def cut(pieces, start, size):
-        return wide(in_order([p[:, start : start + size] for p in pieces], spot, 1))
-
-    grad_down_w = cut(down_pieces, 0, units).T
-    grad_gate_w = cut(feed_pieces, 0, units)
-    grad_up_w = cut(feed_pieces, units, units)
     output = whole_rows(output, output_half)
     grad_tokens = whole_rows(grad_tokens, tokens_half)
-    feed_gain = jnp.sum(wide(w_gate) * grad_gate_w + wide(w_up) * grad_up_w, axis=1)
-    feed_gain = feed_gain + other_core(feed_gain)
-    proj_pieces = dealt_rows(grad_attn_w)
     grad_query_w = cut(proj_pieces, 0, query_cols)
     grad_key_w = cut(proj_pieces, query_cols, head_size)
     grad_value_w = cut(proj_pieces, query_cols + head_size, head_size)
@@ -912,8 +924,8 @@
         gain_sums[0],
         gain_sums[1],
         feed_gain,
-        grad_gate_w * feed_scale,
-        grad_up_w * feed_scale,
+        grad_gate_w,
+        grad_up_w,
         grad_down_w,
     )
 

time: 624 us -> 614 us (0.984)
  waiting for transfers between devices: 203 us -> 194 us
    ppermute x57, waiting for transfers between devices: 182 us -> 164 us  [across(): return lax.ppermute(values, 'ctx', [(i, i ^ bits) for i in range(CTX)])]
    ppermute x33, waiting for transfers between devices: 20.8 us -> 28.1 us  [other_core(): return lax.ppermute(values, 'tp', [(0, 1), (1, 0)])]
    unnamed x192 -> x170, local copies, waits for them, and re-layouts: 22 us -> 22.9 us
  transfers between devices with their start and end apart: 98 -> 98, of which waited for: 42 -> 44; matrix products, arithmetic and copies ran while one was open for 8% -> 8% of each run, Pallas kernels for 41% -> 40%
where the time goes in v4:
time: 614 us; the launch traced here: 605 us
  Pallas kernels  247 us (40%)
  waiting for transfers between devices  194 us (32%)
  starting transfers between devices  73.6 us (12%)
  local copies, waits for them, and re-layouts  40.3 us (7%)
  other arithmetic  33.5 us (5%)
  between operations  16.2 us (3%)
    ppermute x57, waiting for transfers between devices, across(): return lax.ppermute(values, 'ctx', [(i, i ^ bits) for i in range(CTX)])  164 us
    pallas_call x16, Pallas kernels, rows_product(): pl.pallas_call(functools.partial(_rows_kernel, len(lefts), len(picks), th...  83.5 us
    ppermute x57, starting transfers between devices, across(): return lax.ppermute(values, 'ctx', [(i, i ^ bits) for i in range(CTX)])  64.3 us
    pallas_call x3, Pallas kernels, weight_terms(): pl.pallas_call(functools.partial(_terms_kernel, [(len(p), len(o)) for p,...  45.9 us
    pallas_call x1, Pallas kernels, attend_backward(): pl.pallas_call(functools.partial(_backward_kernel, heads, hd ** (-0.5), l...  33.8 us
    pallas_call x3, Pallas kernels, feed_expand(): pl.pallas_call(functools.partial(_expand_kernel, [len(group) for group in...  28.7 us
    ppermute x33, waiting for transfers between devices, other_core(): return lax.ppermute(values, 'tp', [(0, 1), (1, 0)])  28.1 us
    pallas_call x1, Pallas kernels, attend_forward(): pl.pallas_call(functools.partial(_forward_kernel, heads, hd ** (-0.5), le...  23.8 us
  transfers between devices with their start and end apart: 98, of which 44 were waited for; matrix products, arithmetic and copies ran while one was open for 8% of the time, Pallas kernels for 40%

profile of v4, /device:TPU:0, one launch (start us, length us, event | category | flops | bytes accessed | tf_op | source)
XLA Modules:
  0.0 605.4 jit_solution(2067398164286040684)
XLA Ops:
  20.2 3.7 collective-permute-done.2
  29.1 3.7 fusion.6
  37.9 12.0 %collective-permute-done.3.refs_2_ = bf16[256,2048]{1,0:T(8,128)(2,1)} collective-permute-done((bf16[256,2048]{1,0:T(8,128)(2,1)}, bf16[256,2048]{1,0:T(8,128)(2,1)}, u32[]{:S(2)}, u32[]{:S(2)}) %collective-permute-start.3) | collective-permute-done | bytes 1048608 | tf_op jit(solution)/shard_map/ppermute | solution.py:609
  55.1 12.6 %collective-permute-done.33 = bf16[128,2304]{1,0:T(8,128)(2,1)S(1)} collective-permute-done((bf16[128,2304]{1,0:T(8,128)(2,1)S(1)}, bf16[128,2304]{1,0:T(8,128)(2,1)S(1)}, u32[]{:S(2)}, u32[]{:S(2)}) %collective-permute-start.33) | collective-permute-done | bytes 589856 | tf_op jit(solution)/shard_map/ppermute | solution.py:609
  67.6 9.4 %collective-permute-done.32 = bf16[128,2304]{1,0:T(8,128)(2,1)S(1)} collective-permute-done((bf16[128,2304]{1,0:T(8,128)(2,1)S(1)}, bf16[128,2304]{1,0:T(8,128)(2,1)S(1)}, u32[]{:S(2)}, u32[]{:S(2)}) %collective-permute-start.32) | collective-permute-done | bytes 589856 | tf_op jit(solution)/shard_map/ppermute | solution.py:609
  84.6 10.7 %collective-permute-done.5.refs_6_ = bf16[128,2048]{1,0:T(8,128)(2,1)S(1)} collective-permute-done((bf16[128,2048]{1,0:T(8,128)(2,1)S(1)}, bf16[128,2048]{1,0:T(8,128)(2,1)S(1)}, u32[]{:S(2)}, u32[]{:S(2)}) %collective-permute-start.5) | collective-permute-done | bytes 524320 | tf_op jit(solution)/shard_map/ppermute | solution.py:609
  102.4 23.8 %attend_forward.1 = (f32[2048,512]{1,0:T(8,128)}, bf16[2048,512]{1,0:T(8,128)(2,1)}, bf16[2048,256]{1,0:T(8,128)(2,1)}, f32[2048,256]{1,0:T(8,128)}) custom-call(s32[17]{0:T(128)} %pad_add_fusion.info, bf16[256,2048]{1,0:T(8,128)(2,1)} %fusion.1.refs_0_, bf16[256,2048]{1,0:T(8,128)(2,1)} %copy-done.59, bf16[256,2048]{1,0:T(8,128)(2,1)} %collective-permute-done.3.refs_2_, ...), custom_call_target="tpu_custom_call" | custom-call | flops 6442450944 | bytes 26214400 | tf_op jit(solution)/shard_map/attend_forward/pallas_call | solution.py:149
  128.9 4.8 rows_product.17
  134.8 7.3 %collective-permute-done.15.refs_2_ = bf16[256,2048]{1,0:T(8,128)(2,1)S(1)} collective-permute-done((bf16[256,2048]{1,0:T(8,128)(2,1)S(1)}, bf16[256,2048]{1,0:T(8,128)(2,1)S(1)}, u32[]{:S(2)}, u32[]{:S(2)}) %collective-permute-start.15) | collective-permute-done | bytes 1048608 | tf_op jit(solution)/shard_map/ppermute | solution.py:613
  150.0 5.7 rows_product.19
  155.7 4.7 collective-permute-done.21
  166.4 10.6 %collective-permute-done.23.refs_3_ = bf16[128,2048]{1,0:T(8,128)(2,1)S(1)} collective-permute-done((bf16[128,2048]{1,0:T(8,128)(2,1)S(1)}, bf16[128,2048]{1,0:T(8,128)(2,1)S(1)}, u32[]{:S(2)}, u32[]{:S(2)}) %collective-permute-start.23) | collective-permute-done | bytes 524320 | tf_op jit(solution)/shard_map/ppermute | solution.py:609
  178.4 9.3 %collective-permute-done.19.refs_1_ = bf16[128,2048]{1,0:T(8,128)(2,1)S(1)} collective-permute-done((bf16[128,2048]{1,0:T(8,128)(2,1)S(1)}, bf16[128,2048]{1,0:T(8,128)(2,1)S(1)}, u32[]{:S(2)}, u32[]{:S(2)}) %collective-permute-start.19) | collective-permute-done | bytes 524320 | tf_op jit(solution)/shard_map/ppermute | solution.py:609
  189.2 4.1 settle.4
  195.7 21.1 %collective-permute-done.25.refs_0_.refs_2_ = bf16[256,2048]{1,0:T(8,128)(2,1)S(1)} collective-permute-done((bf16[256,2048]{1,0:T(8,128)(2,1)}, bf16[256,2048]{1,0:T(8,128)(2,1)S(1)}, u32[]{:S(2)}, u32[]{:S(2)}) %collective-permute-start.25) | collective-permute-done | bytes 1048608 | tf_op jit(solution)/shard_map/ppermute | solution.py:609
  225.6 7.8 %feed_expand.3 = (bf16[2048,768]{1,0:T(8,128)(2,1)}, bf16[2048,768]{1,0:T(8,128)(2,1)}, bf16[2048,768]{1,0:T(8,128)(2,1)}) custom-call(bf16[256,2048]{1,0:T(8,128)(2,1)} %get-tuple-element.190.refs_0_, bf16[256,2048]{1,0:T(8,128)(2,1)} %collective-permute-done.34.refs_1_, ...), custom_call_target="tpu_custom_call" | custom-call | flops 3221225472 | bytes 12320768 | tf_op jit(solution)/shard_map/feed_expand/pallas_call | solution.py:365
  235.8 13.2 %feed_expand.4 = (bf16[2048,768]{1,0:T(8,128)(2,1)}, bf16[2048,768]{1,0:T(8,128)(2,1)}, bf16[2048,768]{1,0:T(8,128)(2,1)}) custom-call(bf16[256,2048]{1,0:T(8,128)(2,1)} %copy-done.10, bf16[256,2048]{1,0:T(8,128)(2,1)} %collective-permute-done.29.refs_1_.refs_3_, ...), custom_call_target="tpu_custom_call", output_to_operand_aliasing={{0}: (6, {}), {1}: (7, {}), {2}: (8, {})} | custom-call | flops 6442450944 | bytes 18350080 | tf_op jit(solution)/shard_map/feed_expand/pallas_call | solution.py:365
  252.8 7.6 %feed_expand.5 = (bf16[2048,768]{1,0:T(8,128)(2,1)}, bf16[2048,768]{1,0:T(8,128)(2,1)}, bf16[2048,768]{1,0:T(8,128)(2,1)}) custom-call(bf16[128,2048]{1,0:T(8,128)(2,1)} %collective-permute-done.37.refs_0_.refs_6_, bf16[128,2048]{1,0:T(8,128)(2,1)} %collective-permute-done.38.refs_1_.refs_7_, ...), custom_call_target="tpu_custom_call", output_to_operand_aliasing={{0}: (6, {}), {1}: (7, {}), {2}: (8, {})} | custom-call | flops 3221225472 | bytes 12320768 | tf_op jit(solution)/shard_map/feed_expand/pallas_call | solution.py:365
  261.5 12.7 %weight_terms.3 = bf16[2048,768]{1,0:T(8,128)(2,1)} custom-call(bf16[256,2048]{1,0:T(8,128)(2,1)} %copy-done.1, bf16[256,2048]{1,0:T(8,128)(2,1)} %collective-permute-done.7.refs_1_, bf16[256,2048]{1,0:T(8,128)(2,1)} %collective-permute-done.13.refs_2_, bf16[256,2048]{1,0:T(8,128)(2,1)} %copy-done.62, bf16[256,2048]{1,0:T(8,128)(2,1)} %collective-permute-done.14.refs_4_, ...), custom_call_target="tpu_custom_call" | custom-call | flops 6442450944 | bytes 14680064 | tf_op jit(solution)/shard_map/weight_terms/pallas_call | solution.py:449
  274.5 13.7 %feed_back.1 = (bf16[2048,768]{1,0:T(8,128)(2,1)}, bf16[2048,768]{1,0:T(8,128)(2,1)}) custom-call(bf16[256,2048]{1,0:T(8,128)(2,1)} %copy-done.1, bf16[256,2048]{1,0:T(8,128)(2,1)} %collective-permute-done.7.refs_1_, bf16[256,2048]{1,0:T(8,128)(2,1)} %collective-permute-done.13.refs_2_, bf16[256,2048]{1,0:T(8,128)(2,1)} %copy-done.62, ...), custom_call_target="tpu_custom_call" | custom-call | flops 6442450944 | bytes 30408704 | tf_op jit(solution)/shard_map/feed_back/pallas_call | solution.py:407
  288.2 5.0 rows_product.20
  293.1 9.2 %rows_product.21 = bf16[768,2048]{1,0:T(8,128)(2,1)} custom-call(bf16[2048,768]{1,0:T(8,128)(2,1)} %get-tuple-element.224.refs_0_.refs_1_.refs_2_.refs_10_, bf16[2048,768]{1,0:T(8,128)(2,1)} %get-tuple-element.224.refs_0_.refs_1_.refs_2_.refs_10_, bf16[2048,768]{1,0:T(8,128)(2,1)} %get-tuple-element.224.refs_0_.refs_1_.refs_2_.refs_10_, ...), custom_call_target="tpu_custom_call" | custom-call | flops 4831838208 | bytes 18087936 | tf_op jit(solution)/shard_map/rows_product/pallas_call | solution.py:505
  302.8 6.3 %collective-permute-done.41.refs_3_ = bf16[256,2048]{1,0:T(8,128)(2,1)S(1)} collective-permute-done((bf16[256,2048]{1,0:T(8,128)(2,1)S(1)}, bf16[256,2048]{1,0:T(8,128)(2,1)S(1)}, u32[]{:S(2)}, u32[]{:S(2)}) %collective-permute-start.41) | collective-permute-done | bytes 1048608 | tf_op jit(solution)/shard_map/ppermute | solution.py:613
  310.1 5.2 rows_product.22
  319.1 9.4 %rows_product.23 = (f32[256,2048]{1,0:T(8,128)}, bf16[128,2048]{1,0:T(8,128)(2,1)}, f32[128,2048]{1,0:T(8,128)}, f32[128,2048]{1,0:T(8,128)}, bf16[128,2048]{1,0:T(8,128)(2,1)}) custom-call(bf16[2048,768]{1,0:T(8,128)(2,1)} %get-tuple-element.224.refs_0_.refs_1_.refs_2_.refs_10_, bf16[2048,768]{1,0:T(8,128)(2,1)} %get-tuple-element.224.refs_0_.refs_1_.refs_2_.refs_10_, ...), custom_call_target="tpu_custom_call" | custom-call | flops 4831838208 | bytes 18087936 | tf_op jit(solution)/shard_map/rows_product/pallas_call | solution.py:505
  336.9 19.3 %weight_terms.4 = bf16[2048,1536]{1,0:T(8,128)(2,1)} custom-call(bf16[256,2048]{1,0:T(8,128)(2,1)} %get-tuple-element.190.refs_0_, bf16[256,2048]{1,0:T(8,128)(2,1)} %collective-permute-done.34.refs_1_, bf16[256,2048]{1,0:T(8,128)(2,1)} %copy-done.10, bf16[256,2048]{1,0:T(8,128)(2,1)} %collective-permute-done.29.refs_1_.refs_3_, ...), custom_call_target="tpu_custom_call" | custom-call | flops 12884901888 | bytes 20971520 | tf_op jit(solution)/shard_map/weight_terms/pallas_call | solution.py:449
  359.0 4.8 settle.5
  366.8 3.5 rows_product.24
  370.3 6.5 %rows_product.25 = bf16[768,2048]{1,0:T(8,128)(2,1)} custom-call(bf16[2048,768]{1,0:T(8,128)(2,1)} %get-tuple-element.232.refs_10_.refs_0_.refs_1_.refs_2_, bf16[2048,768]{1,0:T(8,128)(2,1)} %get-tuple-element.232.refs_10_.refs_0_.refs_1_.refs_2_, bf16[2048,768]{1,0:T(8,128)(2,1)} %get-tuple-element.232.refs_10_.refs_0_.refs_1_.refs_2_, ...), custom_call_target="tpu_custom_call" | custom-call | flops 2415919104 | bytes 13762560 | tf_op jit(solution)/shard_map/rows_product/pallas_call | solution.py:505
  379.2 4.6 collective-permute-done.52.refs_2_
  384.8 3.7 rows_product.26
  390.1 7.1 %rows_product.27 = (f32[256,2048]{1,0:T(8,128)}, bf16[128,2048]{1,0:T(8,128)(2,1)}, f32[128,2048]{1,0:T(8,128)}, f32[128,2048]{1,0:T(8,128)}, bf16[128,2048]{1,0:T(8,128)(2,1)}) custom-call(bf16[2048,768]{1,0:T(8,128)(2,1)} %get-tuple-element.232.refs_10_.refs_0_.refs_1_.refs_2_, bf16[2048,768]{1,0:T(8,128)(2,1)} %get-tuple-element.232.refs_10_.refs_0_.refs_1_.refs_2_, ...), custom_call_target="tpu_custom_call" | custom-call | flops 2415919104 | bytes 13762560 | tf_op jit(solution)/shard_map/rows_product/pallas_call | solution.py:505
  397.2 5.4 collective-permute-done.50.refs_2_.refs_13_
  407.6 8.4 %collective-permute-done.56.refs_6_.refs_17_ = bf16[128,2048]{1,0:T(8,128)(2,1)S(1)} collective-permute-done((bf16[128,2048]{1,0:T(8,128)(2,1)S(1)}, bf16[128,2048]{1,0:T(8,128)(2,1)S(1)}, u32[]{:S(2)}, u32[]{:S(2)}) %collective-permute-start.56) | collective-permute-done | bytes 524320 | tf_op jit(solution)/shard_map/ppermute | solution.py:609
  423.4 33.8 %attend_backward.1 = (bf16[2048,512]{1,0:T(8,128)(2,1)}, f32[8,128]{1,0:T(8,128)}) custom-call(s32[17]{0:T(128)} %pad_add_fusion.info, bf16[256,2048]{1,0:T(8,128)(2,1)} %get-tuple-element.231.refs_0_.refs_11_, bf16[256,2048]{1,0:T(8,128)(2,1)} %collective-permute-done.49.refs_1_.refs_12_, bf16[256,2048]{1,0:T(8,128)(2,1)} %copy-done.53, ...), custom_call_target="tpu_custom_call" | custom-call | flops 7516192768 | bytes 36700160 | tf_op jit(solution)/shard_map/attend_backward/pallas_call | solution.py:309
  460.9 13.9 %weight_terms.5 = bf16[2048,768]{1,0:T(8,128)(2,1)} custom-call(bf16[256,2048]{1,0:T(8,128)(2,1)} %fusion.1.refs_0_, bf16[256,2048]{1,0:T(8,128)(2,1)} %copy-done.59, bf16[256,2048]{1,0:T(8,128)(2,1)} %collective-permute-done.3.refs_2_, bf16[256,2048]{1,0:T(8,128)(2,1)} %copy-done.61, bf16[256,2048]{1,0:T(8,128)(2,1)} %collective-permute-done.4.refs_4_, ...), custom_call_target="tpu_custom_call" | custom-call | flops 6442450944 | bytes 23068672 | tf_op jit(solution)/shard_map/weight_terms/pallas_call | solution.py:449
  479.2 3.0 rows_product.28
  482.2 5.5 rows_product.29
  491.8 3.1 collective-permute-done.69.refs_2_
  494.9 3.2 rows_product.30
  509.0 6.4 %rows_product.31 = (f32[256,2048]{1,0:T(8,128)}, bf16[128,2048]{1,0:T(8,128)(2,1)}, f32[128,2048]{1,0:T(8,128)}, f32[128,2048]{1,0:T(8,128)}, bf16[128,2048]{1,0:T(8,128)(2,1)}) custom-call(bf16[2048,512]{1,0:T(8,128)(2,1)} %get-tuple-element.262.refs_10_.refs_0_.refs_1_.refs_2_, bf16[2048,512]{1,0:T(8,128)(2,1)} %get-tuple-element.262.refs_10_.refs_0_.refs_1_.refs_2_, ...), custom_call_target="tpu_custom_call" | custom-call | flops 1610612736 | bytes 12320768 | tf_op jit(solution)/shard_map/rows_product/pallas_call | solution.py:505
  517.3 7.0 %collective-permute-done.74 = bf16[128,1536]{1,0:T(8,128)(2,1)S(1)} collective-permute-done((bf16[128,1536]{1,0:T(8,128)(2,1)}, bf16[128,1536]{1,0:T(8,128)(2,1)S(1)}, u32[]{:S(2)}, u32[]{:S(2)}) %collective-permute-start.74) | collective-permute-done | bytes 393248 | tf_op jit(solution)/shard_map/ppermute | solution.py:609
  524.3 8.4 %collective-permute-done.76 = bf16[128,1536]{1,0:T(8,128)(2,1)S(1)} collective-permute-done((bf16[128,1536]{1,0:T(8,128)(2,1)S(1)}, bf16[128,1536]{1,0:T(8,128)(2,1)S(1)}, u32[]{:S(2)}, u32[]{:S(2)}) %collective-permute-start.76) | collective-permute-done | bytes 393248 | tf_op jit(solution)/shard_map/ppermute | solution.py:609
  544.0 8.9 %collective-permute-done.78.refs_3_ = bf16[128,2048]{1,0:T(8,128)(2,1)S(1)} collective-permute-done((bf16[128,2048]{1,0:T(8,128)(2,1)S(1)}, bf16[128,2048]{1,0:T(8,128)(2,1)S(1)}, u32[]{:S(2)}, u32[]{:S(2)}) %collective-permute-start.78) | collective-permute-done | bytes 524320 | tf_op jit(solution)/shard_map/ppermute | solution.py:609
  554.3 5.1 settle.6
  581.7 4.0 collective-permute-done.81
  585.7 4.0 settle.7
  595.2 3.1 constant_dynamic-update-slice_fusion
  (443 shorter events, 182.9 us)
Async XLA Ops:
  7.2 95.2 %all-gather.4.cloned.1.call-start = ((), (), s32[]{:S(2)}) async-start(), calls=%async_computation.3 | async-start | bytes 3932160 | tf_op jit(solution)/shard_map/all_gather | solution.py:708
  25.8 24.1 %collective-permute-start.3 = (bf16[256,2048]{1,0:T(8,128)(2,1)}, bf16[256,2048]{1,0:T(8,128)(2,1)}, u32[]{:S(2)}, u32[]{:S(2)}) collective-permute-start(bf16[256,2048]{1,0:T(8,128)(2,1)} %fusion.1.refs_0_), channel_id=1, source_target_pairs={{0,2},{2,0},{4,6},{6,4},{1,3},{3,1},{5,7},{7,5},{8,10},{10,8},{12,... | collective-permute-start | bytes 3145736 | tf_op jit(solution)/shard_map/ppermute | solution.py:609
  27.3 23.7 %collective-permute-start.4 = (bf16[256,2048]{1,0:T(8,128)(2,1)}, bf16[256,2048]{1,0:T(8,128)(2,1)}, u32[]{:S(2)}, u32[]{:S(2)}) collective-permute-start(bf16[256,2048]{1,0:T(8,128)(2,1)} %fusion.1.refs_0_), channel_id=1, source_target_pairs={{0,4},{2,6},{4,0},{6,2},{1,5},{3,7},{5,1},{7,3},{8,12},{10,14},{12... | collective-permute-start | bytes 3145736 | tf_op jit(solution)/shard_map/ppermute | solution.py:609
  29.1 196.6 %all-gather.6.cloned.1.call-start = ((), (), s32[]{:S(2)}) async-start(), calls=%async_computation.4 | async-start | bytes 7864320 | tf_op jit(solution)/shard_map/all_gather | solution.py:708
  51.3 16.3 %collective-permute-start.33 = (bf16[128,2304]{1,0:T(8,128)(2,1)S(1)}, bf16[128,2304]{1,0:T(8,128)(2,1)S(1)}, u32[]{:S(2)}, u32[]{:S(2)}) collective-permute-start(bf16[128,2304]{1,0:T(8,128)(2,1)S(1)} %pad_maximum_fusion.9), channel_id=1, source_target_pairs={{0,2},{2,0},{4,6},{6,4},{1,3},{3,1},{5,7},{7,5},{8,10},{10,8},{12,... | collective-permute-start | bytes 1769480 | tf_op jit(solution)/shard_map/ppermute | solution.py:609
  52.0 25.1 %collective-permute-start.32 = (bf16[128,2304]{1,0:T(8,128)(2,1)S(1)}, bf16[128,2304]{1,0:T(8,128)(2,1)S(1)}, u32[]{:S(2)}, u32[]{:S(2)}) collective-permute-start(bf16[128,2304]{1,0:T(8,128)(2,1)S(1)} %pad_maximum_fusion.8), channel_id=1, source_target_pairs={{0,4},{2,6},{4,0},{6,2},{1,5},{3,7},{5,1},{7,3},{8,12},{10,14},{12... | collective-permute-start | bytes 1769480 | tf_op jit(solution)/shard_map/ppermute | solution.py:609
  52.4 24.6 %collective-permute-start.31 = (bf16[128,2304]{1,0:T(8,128)(2,1)S(1)}, bf16[128,2304]{1,0:T(8,128)(2,1)S(1)}, u32[]{:S(2)}, u32[]{:S(2)}) collective-permute-start(bf16[128,2304]{1,0:T(8,128)(2,1)S(1)} %pad_maximum_fusion.7), channel_id=1, source_target_pairs={{0,6},{2,4},{4,2},{6,0},{1,7},{3,5},{5,3},{7,1},{8,14},{10,12},{12... | collective-permute-start | bytes 1769480 | tf_op jit(solution)/shard_map/ppermute | solution.py:609
  79.1 195.0 %all-gather.8.cloned.1.call-start = ((), (), s32[]{:S(2)}) async-start(), calls=%async_computation.5 | async-start | bytes 3932160 | tf_op jit(solution)/shard_map/all_gather | solution.py:708
  79.7 17.9 %collective-permute-start.8 = (bf16[256,2048]{1,0:T(8,128)(2,1)}, bf16[256,2048]{1,0:T(8,128)(2,1)S(1)}, u32[]{:S(2)}, u32[]{:S(2)}) collective-permute-start(bf16[256,2048]{1,0:T(8,128)(2,1)} %fusion.1.refs_0_), channel_id=1, source_target_pairs={{0,1},{1,0},{2,3},{3,2},{4,5},{5,4},{6,7},{7,6},{8,9},{9,8},{10,11... | collective-permute-start | bytes 3145736 | tf_op jit(solution)/shard_map/ppermute | solution.py:613
  79.7 18.8 %collective-permute-start.10 = (bf16[256,2048]{1,0:T(8,128)(2,1)}, bf16[256,2048]{1,0:T(8,128)(2,1)S(1)}, u32[]{:S(2)}, u32[]{:S(2)}) collective-permute-start(bf16[256,2048]{1,0:T(8,128)(2,1)} %collective-permute-done.4.refs_4_), channel_id=1, source_target_pairs={{0,1},{1,0},{2,3},{3,2},{4,5},{5,4},{6,7},{7,6},{8,9},{9,8},{10,11... | collective-permute-start | bytes 3145736 | tf_op jit(solution)/shard_map/ppermute | solution.py:613
  97.5 28.7 %collective-permute-start.13 = (bf16[256,2048]{1,0:T(8,128)(2,1)S(1)}, bf16[256,2048]{1,0:T(8,128)(2,1)}, u32[]{:S(2)}, u32[]{:S(2)}) collective-permute-start(bf16[256,2048]{1,0:T(8,128)(2,1)S(1)} %dynamic-slice_select_fusion.refs_0_.refs_6_), channel_id=1, source_target_pairs={{0,2},{2,0},{4,6},{6,4},{1,3},{3,1},{5,7},{7,5},{8,10},{10,8},{12,... | collective-permute-start | bytes 3145736 | tf_op jit(solution)/shard_map/ppermute | solution.py:609
  98.5 27.8 %collective-permute-start.14 = (bf16[256,2048]{1,0:T(8,128)(2,1)S(1)}, bf16[256,2048]{1,0:T(8,128)(2,1)}, u32[]{:S(2)}, u32[]{:S(2)}) collective-permute-start(bf16[256,2048]{1,0:T(8,128)(2,1)S(1)} %dynamic-slice_select_fusion.refs_0_.refs_6_), channel_id=1, source_target_pairs={{0,4},{2,6},{4,0},{6,2},{1,5},{3,7},{5,1},{7,3},{8,12},{10,14},{12... | collective-permute-start | bytes 3145736 | tf_op jit(solution)/shard_map/ppermute | solution.py:609
  133.8 16.2 %collective-permute-start.18 = (bf16[768,2048]{1,0:T(8,128)(2,1)}, bf16[768,2048]{1,0:T(8,128)(2,1)}, u32[]{:S(2)}, u32[]{:S(2)}) collective-permute-start(bf16[768,2048]{1,0:T(8,128)(2,1)} %rows_product.17), channel_id=1, source_target_pairs={{0,1},{1,0},{2,3},{3,2},{4,5},{5,4},{6,7},{7,6},{8,9},{9,8},{10,11... | collective-permute-start | bytes 9437192 | tf_op jit(solution)/shard_map/ppermute | solution.py:613
  149.8 207.9 %reduce-scatter.4.cloned.1.call-start = ((), (), s32[]{:S(2)}) async-start(), calls=%async_computation.6 | async-start | bytes 3932160 | tf_op jit(solution)/shard_map/reduce_scatter | solution.py:712
  164.1 23.5 %collective-permute-start.19 = (bf16[128,2048]{1,0:T(8,128)(2,1)S(1)}, bf16[128,2048]{1,0:T(8,128)(2,1)S(1)}, u32[]{:S(2)}, u32[]{:S(2)}) collective-permute-start(bf16[128,2048]{1,0:T(8,128)(2,1)S(1)} %copy-done.79), channel_id=1, source_target_pairs={{0,2},{2,0},{4,6},{6,4},{1,3},{3,1},{5,7},{7,5},{8,10},{10,8},{12,... | collective-permute-start | bytes 1572872 | tf_op jit(solution)/shard_map/ppermute | solution.py:609
  165.5 22.1 %collective-permute-start.24 = (bf16[128,2048]{1,0:T(8,128)(2,1)S(1)}, bf16[128,2048]{1,0:T(8,128)(2,1)S(1)}, u32[]{:S(2)}, u32[]{:S(2)}) collective-permute-start(bf16[128,2048]{1,0:T(8,128)(2,1)S(1)} %copy-done.78), channel_id=1, source_target_pairs={{0,4},{2,6},{4,0},{6,2},{1,5},{3,7},{5,1},{7,3},{8,12},{10,14},{12... | collective-permute-start | bytes 1572872 | tf_op jit(solution)/shard_map/ppermute | solution.py:609
  193.3 23.5 %collective-permute-start.25 = (bf16[256,2048]{1,0:T(8,128)(2,1)}, bf16[256,2048]{1,0:T(8,128)(2,1)S(1)}, u32[]{:S(2)}, u32[]{:S(2)}) collective-permute-start(bf16[256,2048]{1,0:T(8,128)(2,1)} %get-tuple-element.190.refs_0_), channel_id=1, source_target_pairs={{0,2},{2,0},{4,6},{6,4},{1,3},{3,1},{5,7},{7,5},{8,10},{10,8},{12,... | collective-permute-start | bytes 3145736 | tf_op jit(solution)/shard_map/ppermute | solution.py:609
  194.3 23.6 %collective-permute-start.26 = (bf16[256,2048]{1,0:T(8,128)(2,1)}, bf16[256,2048]{1,0:T(8,128)(2,1)S(1)}, u32[]{:S(2)}, u32[]{:S(2)}) collective-permute-start(bf16[256,2048]{1,0:T(8,128)(2,1)} %get-tuple-element.190.refs_0_), channel_id=1, source_target_pairs={{0,4},{2,6},{4,0},{6,2},{1,5},{3,7},{5,1},{7,3},{8,12},{10,14},{12... | collective-permute-start | bytes 3145736 | tf_op jit(solution)/shard_map/ppermute | solution.py:609
  195.7 29.3 %collective-permute-start.34 = (bf16[256,2048]{1,0:T(8,128)(2,1)}, bf16[256,2048]{1,0:T(8,128)(2,1)}, u32[]{:S(2)}, u32[]{:S(2)}) collective-permute-start(bf16[256,2048]{1,0:T(8,128)(2,1)} %get-tuple-element.190.refs_0_), channel_id=1, source_target_pairs={{0,1},{1,0},{2,3},{3,2},{4,5},{5,4},{6,7},{7,6},{8,9},{9,8},{10,11... | collective-permute-start | bytes 3145736 | tf_op jit(solution)/shard_map/ppermute | solution.py:613
  216.8 16.6 %collective-permute-start.29 = (bf16[256,2048]{1,0:T(8,128)(2,1)S(1)}, bf16[256,2048]{1,0:T(8,128)(2,1)}, u32[]{:S(2)}, u32[]{:S(2)}) collective-permute-start(bf16[256,2048]{1,0:T(8,128)(2,1)S(1)} %collective-permute-done.25.refs_0_.refs_2_), channel_id=1, source_target_pairs={{0,1},{1,0},{2,3},{3,2},{4,5},{5,4},{6,7},{7,6},{8,9},{9,8},{10,11... | collective-permute-start | bytes 3145736 | tf_op jit(solution)/shard_map/ppermute | solution.py:613
  217.8 16.7 %collective-permute-start.30 = (bf16[256,2048]{1,0:T(8,128)(2,1)S(1)}, bf16[256,2048]{1,0:T(8,128)(2,1)}, u32[]{:S(2)}, u32[]{:S(2)}) collective-permute-start(bf16[256,2048]{1,0:T(8,128)(2,1)S(1)} %collective-permute-done.26.refs_2_.refs_4_), channel_id=1, source_target_pairs={{0,1},{1,0},{2,3},{3,2},{4,5},{5,4},{6,7},{7,6},{8,9},{9,8},{10,11... | collective-permute-start | bytes 3145736 | tf_op jit(solution)/shard_map/ppermute | solution.py:613
  217.8 42.6 %collective-permute-start.7 = (bf16[256,2048]{1,0:T(8,128)(2,1)S(1)}, bf16[256,2048]{1,0:T(8,128)(2,1)}, u32[]{:S(2)}, u32[]{:S(2)}) collective-permute-start(bf16[256,2048]{1,0:T(8,128)(2,1)S(1)} %dynamic-slice_select_fusion.refs_0_.refs_6_), channel_id=1, source_target_pairs={{0,1},{1,0},{2,3},{3,2},{4,5},{5,4},{6,7},{7,6},{8,9},{9,8},{10,11... | collective-permute-start | bytes 3145736 | tf_op jit(solution)/shard_map/ppermute | solution.py:613
  219.2 29.9 %collective-permute-start.37 = (bf16[128,2048]{1,0:T(8,128)(2,1)}, bf16[128,2048]{1,0:T(8,128)(2,1)}, u32[]{:S(2)}, u32[]{:S(2)}) collective-permute-start(bf16[128,2048]{1,0:T(8,128)(2,1)} %slice.176), channel_id=1, source_target_pairs={{0,4},{2,6},{4,0},{6,2},{1,5},{3,7},{5,1},{7,3},{8,12},{10,14},{12... | collective-permute-start | bytes 1572872 | tf_op jit(solution)/shard_map/ppermute | solution.py:609
  225.0 24.1 %collective-permute-start.38 = (bf16[128,2048]{1,0:T(8,128)(2,1)}, bf16[128,2048]{1,0:T(8,128)(2,1)}, u32[]{:S(2)}, u32[]{:S(2)}) collective-permute-start(bf16[128,2048]{1,0:T(8,128)(2,1)} %slice.177), channel_id=1, source_target_pairs={{0,2},{2,0},{4,6},{6,4},{1,3},{3,1},{5,7},{7,5},{8,10},{10,8},{12,... | collective-permute-start | bytes 1572872 | tf_op jit(solution)/shard_map/ppermute | solution.py:609
  274.2 201.5 %reduce-scatter.6.cloned.1.call-start = ((), (), s32[]{:S(2)}) async-start(), calls=%async_computation.7 | async-start | bytes 7864320 | tf_op jit(solution)/shard_map/reduce_scatter | solution.py:712
  332.6 23.6 %collective-permute-start.47 = (bf16[128,2048]{1,0:T(8,128)(2,1)S(1)}, bf16[128,2048]{1,0:T(8,128)(2,1)S(1)}, u32[]{:S(2)}, u32[]{:S(2)}) collective-permute-start(bf16[128,2048]{1,0:T(8,128)(2,1)S(1)} %add_convert_fusion.4), channel_id=1, source_target_pairs={{0,4},{2,6},{4,0},{6,2},{1,5},{3,7},{5,1},{7,3},{8,12},{10,14},{12... | collective-permute-start | bytes 1572872 | tf_op jit(solution)/shard_map/ppermute | solution.py:609
  333.2 23.1 %collective-permute-start.46 = (bf16[128,2048]{1,0:T(8,128)(2,1)S(1)}, bf16[128,2048]{1,0:T(8,128)(2,1)S(1)}, u32[]{:S(2)}, u32[]{:S(2)}) collective-permute-start(bf16[128,2048]{1,0:T(8,128)(2,1)S(1)} %add_convert_fusion.5), channel_id=1, source_target_pairs={{0,2},{2,0},{4,6},{6,4},{1,3},{3,1},{5,7},{7,5},{8,10},{10,8},{12,... | collective-permute-start | bytes 1572872 | tf_op jit(solution)/shard_map/ppermute | solution.py:609
  333.9 23.7 %collective-permute-start.43 = (bf16[128,2048]{1,0:T(8,128)(2,1)}, bf16[128,2048]{1,0:T(8,128)(2,1)S(1)}, u32[]{:S(2)}, u32[]{:S(2)}) collective-permute-start(bf16[128,2048]{1,0:T(8,128)(2,1)} %get-tuple-element.217), channel_id=1, source_target_pairs={{0,2},{2,0},{4,6},{6,4},{1,3},{3,1},{5,7},{7,5},{8,10},{10,8},{12,... | collective-permute-start | bytes 1572872 | tf_op jit(solution)/shard_map/ppermute | solution.py:609
  335.2 22.4 %collective-permute-start.48 = (bf16[128,2048]{1,0:T(8,128)(2,1)}, bf16[128,2048]{1,0:T(8,128)(2,1)S(1)}, u32[]{:S(2)}, u32[]{:S(2)}) collective-permute-start(bf16[128,2048]{1,0:T(8,128)(2,1)} %get-tuple-element.223), channel_id=1, source_target_pairs={{0,4},{2,6},{4,0},{6,2},{1,5},{3,7},{5,1},{7,3},{8,12},{10,14},{12... | collective-permute-start | bytes 1572872 | tf_op jit(solution)/shard_map/ppermute | solution.py:609
  358.6 195.7 %reduce-scatter.8.cloned.1.call-start = ((), (), s32[]{:S(2)}) async-start(), calls=%async_computation.8 | async-start | bytes 3932160 | tf_op jit(solution)/shard_map/reduce_scatter | solution.py:712
  377.4 25.2 %collective-permute-start.50 = (bf16[256,2048]{1,0:T(8,128)(2,1)S(1)}, bf16[256,2048]{1,0:T(8,128)(2,1)S(1)}, u32[]{:S(2)}, u32[]{:S(2)}) collective-permute-start(bf16[256,2048]{1,0:T(8,128)(2,1)S(1)} %copy-done.64), channel_id=1, source_target_pairs={{0,2},{2,0},{4,6},{6,4},{1,3},{3,1},{5,7},{7,5},{8,10},{10,8},{12,... | collective-permute-start | bytes 3145736 | tf_op jit(solution)/shard_map/ppermute | solution.py:609
  377.8 25.0 %collective-permute-start.51 = (bf16[256,2048]{1,0:T(8,128)(2,1)S(1)}, bf16[256,2048]{1,0:T(8,128)(2,1)}, u32[]{:S(2)}, u32[]{:S(2)}) collective-permute-start(bf16[256,2048]{1,0:T(8,128)(2,1)S(1)} %copy-done.64), channel_id=1, source_target_pairs={{0,4},{2,6},{4,0},{6,2},{1,5},{3,7},{5,1},{7,3},{8,12},{10,14},{12... | collective-permute-start | bytes 3145736 | tf_op jit(solution)/shard_map/ppermute | solution.py:609
  418.2 39.0 %collective-permute-start.60 = (bf16[128,2048]{1,0:T(8,128)(2,1)}, bf16[128,2048]{1,0:T(8,128)(2,1)S(1)}, u32[]{:S(2)}, u32[]{:S(2)}) collective-permute-start(bf16[128,2048]{1,0:T(8,128)(2,1)} %get-tuple-element.250), channel_id=1, source_target_pairs={{0,2},{2,0},{4,6},{6,4},{1,3},{3,1},{5,7},{7,5},{8,10},{10,8},{12,... | collective-permute-start | bytes 1572872 | tf_op jit(solution)/shard_map/ppermute | solution.py:609
  419.6 37.6 %collective-permute-start.61 = (bf16[128,2048]{1,0:T(8,128)(2,1)}, bf16[128,2048]{1,0:T(8,128)(2,1)S(1)}, u32[]{:S(2)}, u32[]{:S(2)}) collective-permute-start(bf16[128,2048]{1,0:T(8,128)(2,1)} %get-tuple-element.251), channel_id=1, source_target_pairs={{0,4},{2,6},{4,0},{6,2},{1,5},{3,7},{5,1},{7,3},{8,12},{10,14},{12... | collective-permute-start | bytes 1572872 | tf_op jit(solution)/shard_map/ppermute | solution.py:609
  420.3 37.0 %collective-permute-start.62 = (bf16[128,2048]{1,0:T(8,128)(2,1)}, bf16[128,2048]{1,0:T(8,128)(2,1)S(1)}, u32[]{:S(2)}, u32[]{:S(2)}) collective-permute-start(bf16[128,2048]{1,0:T(8,128)(2,1)} %get-tuple-element.252), channel_id=1, source_target_pairs={{0,4},{2,6},{4,0},{6,2},{1,5},{3,7},{5,1},{7,3},{8,12},{10,14},{12... | collective-permute-start | bytes 1572872 | tf_op jit(solution)/shard_map/ppermute | solution.py:609
  421.7 35.6 %collective-permute-start.63 = (bf16[128,2048]{1,0:T(8,128)(2,1)S(1)}, bf16[128,2048]{1,0:T(8,128)(2,1)S(1)}, u32[]{:S(2)}, u32[]{:S(2)}) collective-permute-start(bf16[128,2048]{1,0:T(8,128)(2,1)S(1)} %copy-done.72), channel_id=1, source_target_pairs={{0,2},{2,0},{4,6},{6,4},{1,3},{3,1},{5,7},{7,5},{8,10},{10,8},{12,... | collective-permute-start | bytes 1572872 | tf_op jit(solution)/shard_map/ppermute | solution.py:609
  457.3 17.5 %collective-permute-start.64 = (bf16[128,768]{1,0:T(8,128)(2,1)S(1)}, bf16[128,768]{1,0:T(8,128)(2,1)S(1)}, u32[]{:S(2)}, u32[]{:S(2)}) collective-permute-start(bf16[128,768]{1,0:T(8,128)(2,1)S(1)} %get-tuple-element.393), channel_id=1, source_target_pairs={{0,2},{2,0},{4,6},{6,4},{1,3},{3,1},{5,7},{7,5},{8,10},{10,8},{12,... | collective-permute-start | bytes 589832 | tf_op jit(solution)/shard_map/ppermute | solution.py:609
  487.8 19.4 %collective-permute-start.70 = (bf16[768,2048]{1,0:T(8,128)(2,1)}, bf16[768,2048]{1,0:T(8,128)(2,1)S(1)}, u32[]{:S(2)}, u32[]{:S(2)}) collective-permute-start(bf16[768,2048]{1,0:T(8,128)(2,1)} %rows_product.29), channel_id=1, source_target_pairs={{0,1},{1,0},{2,3},{3,2},{4,5},{5,4},{6,7},{7,6},{8,9},{9,8},{10,11... | collective-permute-start | bytes 9437192 | tf_op jit(solution)/shard_map/ppermute | solution.py:613
  498.1 17.3 %collective-permute-start.72 = (bf16[128,2048]{1,0:T(8,128)(2,1)}, bf16[128,2048]{1,0:T(8,128)(2,1)S(1)}, u32[]{:S(2)}, u32[]{:S(2)}) collective-permute-start(bf16[128,2048]{1,0:T(8,128)(2,1)} %get-tuple-element.277), channel_id=1, source_target_pairs={{0,4},{2,6},{4,0},{6,2},{1,5},{3,7},{5,1},{7,3},{8,12},{10,14},{12... | collective-permute-start | bytes 1572872 | tf_op jit(solution)/shard_map/ppermute | solution.py:609
  499.6 17.1 %collective-permute-start.73 = (bf16[128,2048]{1,0:T(8,128)(2,1)}, bf16[128,2048]{1,0:T(8,128)(2,1)}, u32[]{:S(2)}, u32[]{:S(2)}) collective-permute-start(bf16[128,2048]{1,0:T(8,128)(2,1)} %get-tuple-element.272), channel_id=1, source_target_pairs={{0,2},{2,0},{4,6},{6,4},{1,3},{3,1},{5,7},{7,5},{8,10},{10,8},{12,... | collective-permute-start | bytes 1572872 | tf_op jit(solution)/shard_map/ppermute | solution.py:609
  504.1 20.2 %collective-permute-start.74 = (bf16[128,1536]{1,0:T(8,128)(2,1)}, bf16[128,1536]{1,0:T(8,128)(2,1)S(1)}, u32[]{:S(2)}, u32[]{:S(2)}) collective-permute-start(bf16[128,1536]{1,0:T(8,128)(2,1)} %get-tuple-element.367), channel_id=1, source_target_pairs={{0,2},{2,0},{4,6},{6,4},{1,3},{3,1},{5,7},{7,5},{8,10},{10,8},{12,... | collective-permute-start | bytes 1179656 | tf_op jit(solution)/shard_map/ppermute | solution.py:609
  506.5 17.8 %collective-permute-start.75 = (bf16[128,1536]{1,0:T(8,128)(2,1)}, bf16[128,1536]{1,0:T(8,128)(2,1)S(1)}, u32[]{:S(2)}, u32[]{:S(2)}) collective-permute-start(bf16[128,1536]{1,0:T(8,128)(2,1)} %get-tuple-element.366), channel_id=1, source_target_pairs={{0,4},{2,6},{4,0},{6,2},{1,5},{3,7},{5,1},{7,3},{8,12},{10,14},{12... | collective-permute-start | bytes 1179656 | tf_op jit(solution)/shard_map/ppermute | solution.py:609
  507.2 25.5 %collective-permute-start.76 = (bf16[128,1536]{1,0:T(8,128)(2,1)S(1)}, bf16[128,1536]{1,0:T(8,128)(2,1)S(1)}, u32[]{:S(2)}, u32[]{:S(2)}) collective-permute-start(bf16[128,1536]{1,0:T(8,128)(2,1)S(1)} %get-tuple-element.365), channel_id=1, source_target_pairs={{0,6},{2,4},{4,2},{6,0},{1,7},{3,5},{5,3},{7,1},{8,14},{10,12},{12... | collective-permute-start | bytes 1179656 | tf_op jit(solution)/shard_map/ppermute | solution.py:609
  515.4 28.6 %collective-permute-start.71 = (bf16[128,2048]{1,0:T(8,128)(2,1)}, bf16[128,2048]{1,0:T(8,128)(2,1)S(1)}, u32[]{:S(2)}, u32[]{:S(2)}) collective-permute-start(bf16[128,2048]{1,0:T(8,128)(2,1)} %get-tuple-element.275), channel_id=1, source_target_pairs={{0,2},{2,0},{4,6},{6,4},{1,3},{3,1},{5,7},{7,5},{8,10},{10,8},{12,... | collective-permute-start | bytes 1572872 | tf_op jit(solution)/shard_map/ppermute | solution.py:609
  516.7 27.3 %collective-permute-start.79 = (bf16[128,2048]{1,0:T(8,128)(2,1)}, bf16[128,2048]{1,0:T(8,128)(2,1)S(1)}, u32[]{:S(2)}, u32[]{:S(2)}) collective-permute-start(bf16[128,2048]{1,0:T(8,128)(2,1)} %get-tuple-element.284), channel_id=1, source_target_pairs={{0,4},{2,6},{4,0},{6,2},{1,5},{3,7},{5,1},{7,3},{8,12},{10,14},{12... | collective-permute-start | bytes 1572872 | tf_op jit(solution)/shard_map/ppermute | solution.py:609
  534.1 18.8 %collective-permute-start.78 = (bf16[128,2048]{1,0:T(8,128)(2,1)S(1)}, bf16[128,2048]{1,0:T(8,128)(2,1)S(1)}, u32[]{:S(2)}, u32[]{:S(2)}) collective-permute-start(bf16[128,2048]{1,0:T(8,128)(2,1)S(1)} %add_convert_fusion), channel_id=1, source_target_pairs={{0,4},{2,6},{4,0},{6,2},{1,5},{3,7},{5,1},{7,3},{8,12},{10,14},{12... | collective-permute-start | bytes 1572872 | tf_op jit(solution)/shard_map/ppermute | solution.py:609
  535.8 18.5 %collective-permute-start.77 = (bf16[128,2048]{1,0:T(8,128)(2,1)S(1)}, bf16[128,2048]{1,0:T(8,128)(2,1)}, u32[]{:S(2)}, u32[]{:S(2)}) collective-permute-start(bf16[128,2048]{1,0:T(8,128)(2,1)S(1)} %add_convert_fusion.1), channel_id=1, source_target_pairs={{0,2},{2,0},{4,6},{6,4},{1,3},{3,1},{5,7},{7,5},{8,10},{10,8},{12,... | collective-permute-start | bytes 1572872 | tf_op jit(solution)/shard_map/ppermute | solution.py:609
  569.5 25.7 %collective-permute-start.84 = (f32[256,2048]{1,0:T(8,128)}, f32[256,2048]{1,0:T(8,128)}, u32[]{:S(2)}, u32[]{:S(2)}) collective-permute-start(f32[256,2048]{1,0:T(8,128)} %get-tuple-element.292), channel_id=1, source_target_pairs={{0,1},{1,0},{2,3},{3,2},{4,5},{5,4},{6,7},{7,6},{8,9},{9,8},{10,11... | collective-permute-start | bytes 6291464 | tf_op jit(solution)/shard_map/ppermute | solution.py:613
  (132 other events, 1042.7 us)
Sparse Core Ops, SparseCore 0:
  29.2 63.8 all-gather.3
  95.2 113.9 all-gather.5
  210.8 61.7 all-gather.7
  274.7 60.5 reduce-scatter.3
  357.8 111.0 reduce-scatter.5
  475.9 60.7 reduce-scatter.7
